TPU v7x, 32 devices: a whole 2x2x4 slice. The times are simulated.
32 devices in a mesh: section: 8 (over y, x, core), dp: 4 (over z).
Axes of the slice: x: 2, y: 2, z: 4, core: 2. Of those that a mesh axis runs over, the one named last changes fastest.
Arguments:
- tokens: bfloat16 [6144, 4096], P(('section', 'dp')), may hold values from -6 to 6
- cotangent: bfloat16 [6144, 4096], P(('section', 'dp')), may hold values from -0.09375 to 0.09375
- gate_weight: bfloat16 [256, 4096], P('section'), may hold values from -0.09375 to 0.09375
- up_weight: bfloat16 [256, 4096], P('section'), may hold values from -0.09375 to 0.09375
- down_weight: bfloat16 [256, 4096], P('section'), may hold values from -0.375 to 0.375
Outputs:
- grad_gate: bfloat16 [256, 4096], P('section')
- grad_up: bfloat16 [256, 4096], P('section')
- grad_down: bfloat16 [256, 4096], P('section')
All inputs are finite; a program needn't handle non-finite values.
Results may differ from a plain program's by a relative error of at most 0.0051.
Values may be sent and summed in bfloat16 or wider, within the bound.
No kernel may reach another device: no remote copies, remote signals or barrier semaphores. Data moves between devices by JAX's collectives and lax.ppermute only.
A program may use at most 64 MiB of HBM per device.

v0:
```python
import jax
import jax.numpy as jnp
from jax import lax
from jax.sharding import PartitionSpec as P

STEPS = 6


def from_behind(block, axis, distance):
    devices = range(lax.axis_size(axis))
    route = [((i - distance) % len(devices), i) for i in devices]
    return lax.ppermute(block, axis, route)


def contract(left, right):
    return lax.dot_general(
        left, right, (((1,), (1,)), ((), ())), preferred_element_type=jnp.float32
    )


def block_grads(tokens, cotangent, weights):
    gate_sum = contract(weights[0], tokens)
    up_sum = contract(weights[1], tokens)
    squash = jax.nn.sigmoid(gate_sum)
    activated = gate_sum * squash
    hidden = (activated * up_sum).astype(jnp.bfloat16)
    backward = contract(weights[2], cotangent)
    gate_back = (backward * up_sum * squash * (1.0 + gate_sum * (1.0 - squash))).astype(
        jnp.bfloat16
    )
    up_back = (backward * activated).astype(jnp.bfloat16)
    return jnp.stack(
        [
            jnp.dot(gate_back, tokens, preferred_element_type=jnp.float32),
            jnp.dot(up_back, tokens, preferred_element_type=jnp.float32),
            jnp.dot(hidden, cotangent, preferred_element_type=jnp.float32),
        ]
    )


def per_device(tokens, cotangent, gate_weight, up_weight, down_weight):
    held = jnp.stack([gate_weight, up_weight, down_weight])
    summed = None
    for position in range(STEPS):
        if position > 0:
            held = from_behind(held, "section", 1)
        piece = block_grads(tokens, cotangent, held)
        if position > 0:
            summed = from_behind(summed, "section", 1) + piece
        else:
            summed = piece
    finished = lax.psum(summed, "dp").astype(jnp.bfloat16)
    return (finished[0], finished[1], finished[2])


def solution(mesh):
    return jax.shard_map(
        per_device,
        mesh=mesh,
        in_specs=(
            P(("section", "dp"), None),
            P(("section", "dp"), None),
            P("section", None),
            P("section", None),
            P("section", None),
        ),
        out_specs=(P("section", None), P("section", None), P("section", None)),
        check_vma=False,
    )
```

profile of v0, /device:TPU:0, one launch (start us, length us, event | category | flops | bytes accessed | tf_op | source)
XLA Modules:
  0.0 193.8 jit_solution(3229031589994300953)
XLA Ops:
  0.6 0.0 copy-start
  0.7 1.3 pad_maximum_fusion.1
  2.0 0.5 collective-permute-start.1
  2.5 0.6 fusion.59
  3.1 0.0 copy-done.3
  3.1 0.6 fusion.58
  3.7 0.0 copy-done.1
  3.8 0.6 fusion.57
  4.3 0.4 convolution_bitcast_fusion.15
  4.7 0.4 convolution_bitcast_fusion.17
  5.1 0.4 convolution_bitcast_fusion.16
  5.5 0.1 pad_maximum_fusion
  5.6 2.7 %collective-permute-start = (f32[3,32,4096]{2,1,0:T(8,128)S(1)}, f32[3,32,4096]{2,1,0:T(8,128)S(1)}, u32[]{:S(2)}, u32[]{:S(2)}) collective-permute-start(f32[3,32,4096]{2,1,0:T(8,128)S(1)} %pad_maximum_fusion), channel_id=1, source_target_pairs={{28,0},{0,4},{4,8},{8,12},{12,16},{16,20},{20,24},{24,28},{29,1},{... | collective-permute-start | bytes 4718600 | tf_op jit(solution)/shard_map/ppermute | solution.py:12
  8.3 6.8 %collective-permute-done.1 = bf16[3,32,4096]{2,1,0:T(8,128)(2,1)S(1)} collective-permute-done((bf16[3,32,4096]{2,1,0:T(8,128)(2,1)S(1)}, bf16[3,32,4096]{2,1,0:T(8,128)(2,1)S(1)}, u32[]{:S(2)}, u32[]{:S(2)}) %collective-permute-start.1) | collective-permute-done | bytes 786464 | tf_op jit(solution)/shard_map/ppermute | solution.py:12
  15.1 0.6 fusion.12
  15.7 0.6 fusion.13
  16.3 0.4 convolution_bitcast_fusion.12
  16.7 0.6 fusion.14
  17.3 0.4 convolution_bitcast_fusion.13
  17.6 0.4 convolution_bitcast_fusion.14
  18.0 13.9 %collective-permute-done = f32[3,32,4096]{2,1,0:T(8,128)S(1)} collective-permute-done((f32[3,32,4096]{2,1,0:T(8,128)S(1)}, f32[3,32,4096]{2,1,0:T(8,128)S(1)}, u32[]{:S(2)}, u32[]{:S(2)}) %collective-permute-start) | collective-permute-done | bytes 1572896 | tf_op jit(solution)/shard_map/ppermute | solution.py:12
  31.9 0.2 maximum_add_fusion
  32.1 0.1 collective-permute-start.2
  32.2 8.2 %collective-permute-done.3 = bf16[3,32,4096]{2,1,0:T(8,128)(2,1)S(1)} collective-permute-done((bf16[3,32,4096]{2,1,0:T(8,128)(2,1)S(1)}, bf16[3,32,4096]{2,1,0:T(8,128)(2,1)S(1)}, u32[]{:S(2)}, u32[]{:S(2)}) %collective-permute-start.3) | collective-permute-done | bytes 786464 | tf_op jit(solution)/shard_map/ppermute | solution.py:12
  40.4 0.6 fusion.9
  41.0 0.6 fusion.11
  41.6 0.4 convolution_bitcast_fusion.10
  41.9 0.6 fusion.10
  42.5 0.4 convolution_bitcast_fusion.9
  42.9 0.4 convolution_bitcast_fusion.11
  43.3 13.9 %collective-permute-done.2 = f32[3,32,4096]{2,1,0:T(8,128)S(1)} collective-permute-done((f32[3,32,4096]{2,1,0:T(8,128)S(1)}, f32[3,32,4096]{2,1,0:T(8,128)S(1)}, u32[]{:S(2)}, u32[]{:S(2)}) %collective-permute-start.2) | collective-permute-done | bytes 1572896 | tf_op jit(solution)/shard_map/ppermute | solution.py:12
  57.2 0.2 maximum_add_fusion.1
  57.4 0.1 collective-permute-start.4
  57.5 8.2 %collective-permute-done.5 = bf16[3,32,4096]{2,1,0:T(8,128)(2,1)S(1)} collective-permute-done((bf16[3,32,4096]{2,1,0:T(8,128)(2,1)S(1)}, bf16[3,32,4096]{2,1,0:T(8,128)(2,1)S(1)}, u32[]{:S(2)}, u32[]{:S(2)}) %collective-permute-start.5) | collective-permute-done | bytes 786464 | tf_op jit(solution)/shard_map/ppermute | solution.py:12
  65.7 0.6 fusion.6
  66.2 0.6 fusion.7
  66.8 0.4 convolution_bitcast_fusion.6
  67.2 0.6 fusion.8
  67.8 0.4 convolution_bitcast_fusion.7
  68.2 0.4 convolution_bitcast_fusion.8
  68.6 13.9 %collective-permute-done.4 = f32[3,32,4096]{2,1,0:T(8,128)S(1)} collective-permute-done((f32[3,32,4096]{2,1,0:T(8,128)S(1)}, f32[3,32,4096]{2,1,0:T(8,128)S(1)}, u32[]{:S(2)}, u32[]{:S(2)}) %collective-permute-start.4) | collective-permute-done | bytes 1572896 | tf_op jit(solution)/shard_map/ppermute | solution.py:12
  82.5 0.2 maximum_add_fusion.2
  82.7 0.1 collective-permute-start.6
  82.7 8.2 %collective-permute-done.7 = bf16[3,32,4096]{2,1,0:T(8,128)(2,1)S(1)} collective-permute-done((bf16[3,32,4096]{2,1,0:T(8,128)(2,1)S(1)}, bf16[3,32,4096]{2,1,0:T(8,128)(2,1)S(1)}, u32[]{:S(2)}, u32[]{:S(2)}) %collective-permute-start.7) | collective-permute-done | bytes 786464 | tf_op jit(solution)/shard_map/ppermute | solution.py:12
  90.9 0.6 fusion.3
  91.5 0.6 fusion.4
  92.1 0.4 convolution_bitcast_fusion.3
  92.5 0.6 fusion.5
  93.1 0.4 convolution_bitcast_fusion.4
  93.5 0.4 convolution_bitcast_fusion.5
  93.9 13.9 %collective-permute-done.6 = f32[3,32,4096]{2,1,0:T(8,128)S(1)} collective-permute-done((f32[3,32,4096]{2,1,0:T(8,128)S(1)}, f32[3,32,4096]{2,1,0:T(8,128)S(1)}, u32[]{:S(2)}, u32[]{:S(2)}) %collective-permute-start.6) | collective-permute-done | bytes 1572896 | tf_op jit(solution)/shard_map/ppermute | solution.py:12
  107.8 0.2 maximum_add_fusion.3
  108.0 0.2 collective-permute-start.8
  108.2 8.0 %collective-permute-done.9 = bf16[3,32,4096]{2,1,0:T(8,128)(2,1)S(1)} collective-permute-done((bf16[3,32,4096]{2,1,0:T(8,128)(2,1)S(1)}, bf16[3,32,4096]{2,1,0:T(8,128)(2,1)S(1)}, u32[]{:S(2)}, u32[]{:S(2)}) %collective-permute-start.9) | collective-permute-done | bytes 786464 | tf_op jit(solution)/shard_map/ppermute | solution.py:12
  116.2 0.6 fusion
  116.8 0.6 fusion.1
  117.4 0.4 convolution_bitcast_fusion
  117.8 0.6 fusion.2
  118.4 0.4 convolution_bitcast_fusion.1
  118.8 0.4 convolution_bitcast_fusion.2
  119.2 13.9 %collective-permute-done.8 = f32[3,32,4096]{2,1,0:T(8,128)S(1)} collective-permute-done((f32[3,32,4096]{2,1,0:T(8,128)S(1)}, f32[3,32,4096]{2,1,0:T(8,128)S(1)}, u32[]{:S(2)}, u32[]{:S(2)}) %collective-permute-start.8) | collective-permute-done | bytes 1572896 | tf_op jit(solution)/shard_map/ppermute | solution.py:12
  133.1 0.2 maximum_add_fusion.4
  133.2 58.6 %all-reduce.1 = bf16[3,32,4096]{2,1,0:T(8,128)(2,1)} all-reduce(f32[3,32,4096]{2,1,0:T(8,128)S(1)} %maximum_add_fusion.4), channel_id=1, replica_groups=mesh['section'=8,'dp'=4] {'dp'}, use_global_device_ids=true, to_apply=%region_0.0 | all-reduce | flops 393216 | bytes 2359296 | tf_op jit(solution)/shard_map/psum | solution.py:52
  191.8 2.0 %slice_bitcast_fusion = (bf16[32,4096]{1,0:T(8,128)(2,1)}, bf16[32,4096]{1,0:T(8,128)(2,1)}, bf16[32,4096]{1,0:T(8,128)(2,1)}) fusion(bf16[3,32,4096]{2,1,0:T(8,128)(2,1)} %all-reduce.1), kind=kLoop, calls=%fused_computation.25 | loop fusion | bytes 1572864 | tf_op jit(solution)/shard_map/squeeze | solution.py:53
  (11 shorter events, 0.0 us)
Async XLA Ops:
  0.6 1.9 copy-start
  0.6 1.9 copy-start.2
  0.7 2.5 %copy-start.3 = (bf16[32,4096]{1,0:T(8,128)(2,1)S(1)}, bf16[32,4096]{1,0:T(8,128)(2,1)}, u32[]{:S(2)}) copy-start(bf16[32,4096]{1,0:T(8,128)(2,1)} %param.8) | copy-start | bytes 786436
  2.0 1.7 copy-start.1
  2.0 1.7 copy-start.4
  2.0 13.1 %collective-permute-start.1 = (bf16[3,32,4096]{2,1,0:T(8,128)(2,1)S(1)}, bf16[3,32,4096]{2,1,0:T(8,128)(2,1)S(1)}, u32[]{:S(2)}, u32[]{:S(2)}) collective-permute-start(bf16[3,32,4096]{2,1,0:T(8,128)(2,1)S(1)} %pad_maximum_fusion.1), channel_id=1, source_target_pairs={{28,0},{0,4},{4,8},{8,12},{12,16},{16,20},{20,24},{24,28},{29,1},{... | collective-permute-start | bytes 2359304 | tf_op jit(solution)/shard_map/ppermute | solution.py:12
  5.6 26.3 %collective-permute-start = (f32[3,32,4096]{2,1,0:T(8,128)S(1)}, f32[3,32,4096]{2,1,0:T(8,128)S(1)}, u32[]{:S(2)}, u32[]{:S(2)}) collective-permute-start(f32[3,32,4096]{2,1,0:T(8,128)S(1)} %pad_maximum_fusion), channel_id=1, source_target_pairs={{28,0},{0,4},{4,8},{8,12},{12,16},{16,20},{20,24},{24,28},{29,1},{... | collective-permute-start | bytes 4718600 | tf_op jit(solution)/shard_map/ppermute | solution.py:12
  15.1 25.3 %collective-permute-start.3 = (bf16[3,32,4096]{2,1,0:T(8,128)(2,1)S(1)}, bf16[3,32,4096]{2,1,0:T(8,128)(2,1)S(1)}, u32[]{:S(2)}, u32[]{:S(2)}) collective-permute-start(bf16[3,32,4096]{2,1,0:T(8,128)(2,1)S(1)} %collective-permute-done.1), channel_id=1, source_target_pairs={{28,0},{0,4},{4,8},{8,12},{12,16},{16,20},{20,24},{24,28},{29,1},{... | collective-permute-start | bytes 2359304 | tf_op jit(solution)/shard_map/ppermute | solution.py:12
  32.1 25.1 %collective-permute-start.2 = (f32[3,32,4096]{2,1,0:T(8,128)S(1)}, f32[3,32,4096]{2,1,0:T(8,128)S(1)}, u32[]{:S(2)}, u32[]{:S(2)}) collective-permute-start(f32[3,32,4096]{2,1,0:T(8,128)S(1)} %maximum_add_fusion), channel_id=1, source_target_pairs={{28,0},{0,4},{4,8},{8,12},{12,16},{16,20},{20,24},{24,28},{29,1},{... | collective-permute-start | bytes 4718600 | tf_op jit(solution)/shard_map/ppermute | solution.py:12
  40.4 25.3 %collective-permute-start.5 = (bf16[3,32,4096]{2,1,0:T(8,128)(2,1)S(1)}, bf16[3,32,4096]{2,1,0:T(8,128)(2,1)S(1)}, u32[]{:S(2)}, u32[]{:S(2)}) collective-permute-start(bf16[3,32,4096]{2,1,0:T(8,128)(2,1)S(1)} %collective-permute-done.3), channel_id=1, source_target_pairs={{28,0},{0,4},{4,8},{8,12},{12,16},{16,20},{20,24},{24,28},{29,1},{... | collective-permute-start | bytes 2359304 | tf_op jit(solution)/shard_map/ppermute | solution.py:12
  57.4 25.1 %collective-permute-start.4 = (f32[3,32,4096]{2,1,0:T(8,128)S(1)}, f32[3,32,4096]{2,1,0:T(8,128)S(1)}, u32[]{:S(2)}, u32[]{:S(2)}) collective-permute-start(f32[3,32,4096]{2,1,0:T(8,128)S(1)} %maximum_add_fusion.1), channel_id=1, source_target_pairs={{28,0},{0,4},{4,8},{8,12},{12,16},{16,20},{20,24},{24,28},{29,1},{... | collective-permute-start | bytes 4718600 | tf_op jit(solution)/shard_map/ppermute | solution.py:12
  65.7 25.3 %collective-permute-start.7 = (bf16[3,32,4096]{2,1,0:T(8,128)(2,1)S(1)}, bf16[3,32,4096]{2,1,0:T(8,128)(2,1)S(1)}, u32[]{:S(2)}, u32[]{:S(2)}) collective-permute-start(bf16[3,32,4096]{2,1,0:T(8,128)(2,1)S(1)} %collective-permute-done.5), channel_id=1, source_target_pairs={{28,0},{0,4},{4,8},{8,12},{12,16},{16,20},{20,24},{24,28},{29,1},{... | collective-permute-start | bytes 2359304 | tf_op jit(solution)/shard_map/ppermute | solution.py:12
  82.7 25.1 %collective-permute-start.6 = (f32[3,32,4096]{2,1,0:T(8,128)S(1)}, f32[3,32,4096]{2,1,0:T(8,128)S(1)}, u32[]{:S(2)}, u32[]{:S(2)}) collective-permute-start(f32[3,32,4096]{2,1,0:T(8,128)S(1)} %maximum_add_fusion.2), channel_id=1, source_target_pairs={{28,0},{0,4},{4,8},{8,12},{12,16},{16,20},{20,24},{24,28},{29,1},{... | collective-permute-start | bytes 4718600 | tf_op jit(solution)/shard_map/ppermute | solution.py:12
  90.9 25.3 %collective-permute-start.9 = (bf16[3,32,4096]{2,1,0:T(8,128)(2,1)S(1)}, bf16[3,32,4096]{2,1,0:T(8,128)(2,1)S(1)}, u32[]{:S(2)}, u32[]{:S(2)}) collective-permute-start(bf16[3,32,4096]{2,1,0:T(8,128)(2,1)S(1)} %collective-permute-done.7), channel_id=1, source_target_pairs={{28,0},{0,4},{4,8},{8,12},{12,16},{16,20},{20,24},{24,28},{29,1},{... | collective-permute-start | bytes 2359304 | tf_op jit(solution)/shard_map/ppermute | solution.py:12
  108.0 25.1 %collective-permute-start.8 = (f32[3,32,4096]{2,1,0:T(8,128)S(1)}, f32[3,32,4096]{2,1,0:T(8,128)S(1)}, u32[]{:S(2)}, u32[]{:S(2)}) collective-permute-start(f32[3,32,4096]{2,1,0:T(8,128)S(1)} %maximum_add_fusion.3), channel_id=1, source_target_pairs={{28,0},{0,4},{4,8},{8,12},{12,16},{16,20},{20,24},{24,28},{29,1},{... | collective-permute-start | bytes 4718600 | tf_op jit(solution)/shard_map/ppermute | solution.py:12
where the time goes:
time: 194 us
  waiting for transfers between devices  109 us (56%)
  blocking collectives  58.6 us (30%)
  matrix products  17.5 us (9%)
  starting transfers between devices  3.58 us (2%)
  other arithmetic  2.27 us (1%)
  local copies, waits for them, and re-layouts  2.06 us (1%)
    ppermute x10, waiting for transfers between devices, from_behind(): return lax.ppermute(block, axis, route)  109 us
    psum x1, blocking collectives, per_device(): finished = lax.psum(summed, 'dp').astype(jnp.bfloat16)  58.6 us
    dot_general x18, matrix products, contract(): lax.dot_general(left, right, (((1,), (1,)), ((), ())), preferred_element_...  10.6 us
  transfers between devices with their start and end apart: 10, of which 10 were waited for; matrix products, arithmetic and copies ran while one was open for 9% of the time, Pallas kernels for 0%

commit v1 on v0

v1 whole, which is shorter than its diff:
```python
import jax
import jax.numpy as jnp
from jax import lax
from jax.sharding import PartitionSpec as P

STEPS = 6
F32 = jnp.float32
BF16 = jnp.bfloat16


def from_behind(block, axis, distance):
    devices = range(lax.axis_size(axis))
    route = [((i - distance) % len(devices), i) for i in devices]
    return lax.ppermute(block, axis, route)


def contract(left, right):
    return lax.dot_general(
        left, right, (((1,), (1,)), ((), ())), preferred_element_type=F32
    )


def rows_dot(left, right):
    return jnp.dot(left, right, preferred_element_type=F32)


def activations(tokens, cotangent, gate, upper, down):
    gate_sum = contract(gate, tokens)
    up_sum = contract(upper, tokens)
    squash = jax.nn.sigmoid(gate_sum)
    activated = gate_sum * squash
    hidden = (activated * up_sum).astype(BF16)
    backward = contract(down, cotangent)
    gate_back = (backward * up_sum * squash * (1.0 + gate_sum * (1.0 - squash))).astype(
        BF16
    )
    up_back = (backward * activated).astype(BF16)
    return gate_back, up_back, hidden


def ring(tokens, cotangent, gate_weight, up_weight, down_weight):
    held = jnp.stack([gate_weight, up_weight, down_weight])
    summed = None
    for position in range(STEPS):
        if position > 0:
            held = from_behind(held, "section", 1)
        parts = activations(tokens, cotangent, held[0], held[1], held[2])
        piece = jnp.stack(
            [
                rows_dot(parts[0], tokens),
                rows_dot(parts[1], tokens),
                rows_dot(parts[2], cotangent),
            ]
        )
        if position > 0:
            summed = from_behind(summed, "section", 1) + piece
        else:
            summed = piece
    finished = lax.psum(summed, "dp").astype(BF16)
    return (finished[0], finished[1], finished[2])


def flip(block, mask):
    return lax.ppermute(block, "section", [(i, i ^ mask) for i in range(8)])


def along(block, route):
    return lax.ppermute(block, "dp", route)


CORE, X, Y = 1, 2, 4
COLUMN_PARTS = 2


def square(tokens, cotangent, gate_weight, up_weight, down_weight):
    section = lax.axis_index("section")
    core = section % 2
    chip = section // 2
    line = lax.axis_index("dp")
    block = gate_weight.shape[0]
    half = block // 2
    tok = tokens.shape[0]
    width = tokens.shape[1]

    tokens2 = jnp.concatenate([tokens, flip(tokens, CORE)])
    cotangent2 = jnp.concatenate([cotangent, flip(cotangent, CORE)])

    own = [gate_weight, up_weight, down_weight]
    from_x = [flip(w, X) for w in own]
    from_y = [flip(w, Y) for w in own]
    diagonal = [
        jnp.concatenate([flip(fy[:half], X), flip(fx[half:], Y)])
        for fx, fy in zip(from_x, from_y)
    ]

    sections2 = jnp.repeat(jnp.stack([section, section ^ 1]), tok)

    def masked(parts, chips):
        blocks = jnp.repeat(jnp.stack([2 * c + core for c in chips]), block)
        meets = (sections2[None, :] - blocks[:, None]) % 8 < STEPS
        return [jnp.where(meets, part, 0).astype(BF16) for part in parts]

    near = [jnp.concatenate([o, x, y]) for o, x, y in zip(own, from_x, from_y)]
    near = masked(
        activations(tokens2, cotangent2, *near), [chip, chip ^ 1, chip ^ 2]
    )
    far = masked(activations(tokens2, cotangent2, *diagonal), [chip ^ 3])
    even_core = core == 0
    even_chip = chip % 2 == 0

    def pick(a, b, c):
        return jnp.where(even_core, a, jnp.where(even_chip, b, c))

    sources = [tokens2, tokens2, cotangent2]
    to_diagonal = []
    rest = []
    for part, last in zip(near, far):
        o, x, y = part[:block], part[block : 2 * block], part[2 * block :]
        to_diagonal.append(pick(x, o, y))
        rest.append(
            jnp.concatenate([pick(last, y, o), pick(o, last, x), pick(y, x, last)])
        )

    relayed = []
    for left, right in zip(to_diagonal, sources):
        sums = rows_dot(left, right).astype(BF16)
        relayed.append((flip(sums[:half], X), flip(sums[half:], Y)))

    step = width // COLUMN_PARTS
    results = []
    for at in range(3):
        row = []
        for part in range(COLUMN_PARTS):
            columns = slice(part * step, (part + 1) * step)
            sums = rows_dot(rest[at], sources[at][:, columns])
            via_x, via_y = relayed[at]
            to_x = jnp.concatenate(
                [sums[:half], sums[half:block] + via_y[:, columns].astype(F32)]
            ).astype(BF16)
            to_y = jnp.concatenate(
                [
                    sums[block : block + half] + via_x[:, columns].astype(F32),
                    sums[block + half : 2 * block],
                ]
            ).astype(BF16)
            stay = flip(sums[2 * block :].astype(BF16), CORE)
            total = (
                flip(to_x, X | CORE).astype(F32)
                + flip(to_y, Y | CORE).astype(F32)
                + stay.astype(F32)
            )
            inward = along(total.astype(BF16), [(0, 1), (3, 2)])
            pair = lax.reduce_precision(total + inward.astype(F32), 8, 7)
            across = along(pair.astype(BF16), [(1, 2), (2, 1)])
            done = (pair + across.astype(F32)).astype(BF16)
            outward = along(done, [(1, 0), (2, 3)])
            row.append(jnp.where((line == 1) | (line == 2), done, outward))
        results.append(jnp.concatenate(row, axis=1))
    return tuple(results)


def solution(mesh):
    fits = mesh.shape["section"] == 8 and mesh.shape["dp"] == 4
    return jax.shard_map(
        square if fits else ring,
        mesh=mesh,
        in_specs=(
            P(("section", "dp"), None),
            P(("section", "dp"), None),
            P("section", None),
            P("section", None),
            P("section", None),
        ),
        out_specs=(P("section", None), P("section", None), P("section", None)),
        check_vma=False,
    )
```

time: 194 us -> 139 us (0.72)
  waiting for transfers between devices: 109 us -> 50.3 us
  blocking collectives: 58.6 us -> 0 us
  starting transfers between devices: 3.58 us -> 57.2 us
  local copies, waits for them, and re-layouts: 2.06 us -> 10.9 us
  matrix products: 17.5 us -> 14.1 us
    ppermute x10 -> x56, waiting for transfers between devices: 109 us -> 50.3 us  [the longest x38 28.4 us: flip(): return lax.ppermute(block, 'section', [(i, i ^ mask) for i in range(8)])]
    psum x1 -> x0, blocking collectives: 58.6 us -> none  [per_device(): finished = lax.psum(summed, 'dp').astype(jnp.bfloat16)]
    ppermute x10 -> x56, starting transfers between devices: 3.58 us -> 57.2 us  [the longest x38 34.7 us: flip(): return lax.ppermute(block, 'section', [(i, i ^ mask) for i in range(8)])]
    slice x0 -> x21, local copies, waits for them, and re-layouts: none -> 4.81 us  [the longest x3 2.78 us: square(): fx[half:]]
    concatenate x0 -> x2, local copies, waits for them, and re-layouts: none -> 3.02 us  [the longest x1 1.51 us: square(): cotangent2 = jnp.concatenate([cotangent, flip(cotangent, CORE)])]
    unnamed x10 -> x12, local copies, waits for them, and re-layouts: 0.06 us -> 2.79 us
    dot_general x18 -> x9, matrix products: 6.95 us -> 4.62 us  [rows_dot(): return jnp.dot(left, right, preferred_element_type=F32)]
    concatenate x0 -> x15, other arithmetic: none -> 2.3 us  [the longest x3 2.16 us: square(): results.append(jnp.concatenate(row, axis=1))]
  transfers between devices with their start and end apart: 10 -> 56, of which waited for: 10 -> 27; matrix products, arithmetic and copies ran while one was open for 9% -> 16% of each run, Pallas kernels for 0% -> 0%
where the time goes in v1:
time: 139 us; the launch traced here: 138 us
  starting transfers between devices  57.2 us (41%)
  waiting for transfers between devices  50.3 us (36%)
  matrix products  14.1 us (10%)
  local copies, waits for them, and re-layouts  10.9 us (8%)
  other arithmetic  4.09 us (3%)
  between operations  1.53 us (1%)
    ppermute x38, starting transfers between devices, flip(): return lax.ppermute(block, 'section', [(i, i ^ mask) for i in range(8)])  34.7 us
    ppermute x38, waiting for transfers between devices, flip(): return lax.ppermute(block, 'section', [(i, i ^ mask) for i in range(8)])  28.4 us
    ppermute x18, starting transfers between devices, along(): return lax.ppermute(block, 'dp', route)  22.5 us
    ppermute x18, waiting for transfers between devices, along(): return lax.ppermute(block, 'dp', route)  21.9 us
    dot_general x6, matrix products, contract(): lax.dot_general(left, right, (((1,), (1,)), ((), ())), preferred_element_...  9.46 us
    dot_general x9, matrix products, rows_dot(): return jnp.dot(left, right, preferred_element_type=F32)  4.62 us
    unnamed x12, local copies, waits for them, and re-layouts  2.79 us
    slice x3, local copies, waits for them, and re-layouts, square(): fx[half:]  2.78 us
  transfers between devices with their start and end apart: 56, of which 27 were waited for; matrix products, arithmetic and copies ran while one was open for 16% of the time, Pallas kernels for 0%

profile of v1, /device:TPU:0, one launch (start us, length us, event | category | flops | bytes accessed | tf_op | source)
XLA Modules:
  0.0 138.1 jit_solution(12916296349956916909)
XLA Ops:
  0.6 3.0 %collective-permute-start.10 = (bf16[32,4096]{1,0:T(8,128)(2,1)}, bf16[32,4096]{1,0:T(8,128)(2,1)S(1)}, u32[]{:S(2)}, u32[]{:S(2)}) collective-permute-start(bf16[32,4096]{1,0:T(8,128)(2,1)} %param.7), channel_id=1, source_target_pairs={{0,16},{4,20},{8,24},{12,28},{16,0},{20,4},{24,8},{28,12},{1,17},{... | collective-permute-start | bytes 786440 | tf_op jit(solution)/shard_map/ppermute | solution.py:64
  3.7 1.5 %collective-permute-start.12 = (bf16[32,4096]{1,0:T(8,128)(2,1)}, bf16[32,4096]{1,0:T(8,128)(2,1)}, u32[]{:S(2)}, u32[]{:S(2)}) collective-permute-start(bf16[32,4096]{1,0:T(8,128)(2,1)} %param.7), channel_id=1, source_target_pairs={{0,8},{4,12},{8,0},{12,4},{16,24},{20,28},{24,16},{28,20},{1,9},{5... | collective-permute-start | bytes 786440 | tf_op jit(solution)/shard_map/ppermute | solution.py:64
  6.2 1.5 %constant_dynamic-update-slice_fusion.3 = bf16[384,4096]{1,0:T(8,128)(2,1)S(1)} fusion(bf16[192,4096]{1,0:T(8,128)(2,1)} %param.5), kind=kLoop, calls=%fused_computation.180 | loop fusion | bytes 3145728
  7.7 1.3 constant_dynamic-update-slice_fusion.1
  9.2 1.8 %collective-permute-done.10 = bf16[32,4096]{1,0:T(8,128)(2,1)S(1)} collective-permute-done((bf16[32,4096]{1,0:T(8,128)(2,1)}, bf16[32,4096]{1,0:T(8,128)(2,1)S(1)}, u32[]{:S(2)}, u32[]{:S(2)}) %collective-permute-start.10) | collective-permute-done | bytes 262176 | tf_op jit(solution)/shard_map/ppermute | solution.py:64
  11.0 2.0 %collective-permute-start.2 = (bf16[32,4096]{1,0:T(8,128)(2,1)}, bf16[32,4096]{1,0:T(8,128)(2,1)}, u32[]{:S(2)}, u32[]{:S(2)}) collective-permute-start(bf16[32,4096]{1,0:T(8,128)(2,1)} %param.9), channel_id=1, source_target_pairs={{0,8},{4,12},{8,0},{12,4},{16,24},{20,28},{24,16},{28,20},{1,9},{5... | collective-permute-start | bytes 786440 | tf_op jit(solution)/shard_map/ppermute | solution.py:64
  13.1 1.5 %collective-permute-start.5 = (bf16[32,4096]{1,0:T(8,128)(2,1)}, bf16[32,4096]{1,0:T(8,128)(2,1)}, u32[]{:S(2)}, u32[]{:S(2)}) collective-permute-start(bf16[32,4096]{1,0:T(8,128)(2,1)} %param.8), channel_id=1, source_target_pairs={{0,16},{4,20},{8,24},{12,28},{16,0},{20,4},{24,8},{28,12},{1,17},{... | collective-permute-start | bytes 786440 | tf_op jit(solution)/shard_map/ppermute | solution.py:64
  14.6 2.2 %collective-permute-done = bf16[32,4096]{1,0:T(8,128)(2,1)} collective-permute-done((bf16[32,4096]{1,0:T(8,128)(2,1)}, bf16[32,4096]{1,0:T(8,128)(2,1)}, u32[]{:S(2)}, u32[]{:S(2)}) %collective-permute-start) | collective-permute-done | bytes 262176 | tf_op jit(solution)/shard_map/ppermute | solution.py:64
  16.7 2.0 %collective-permute-start.7 = (bf16[32,4096]{1,0:T(8,128)(2,1)}, bf16[32,4096]{1,0:T(8,128)(2,1)}, u32[]{:S(2)}, u32[]{:S(2)}) collective-permute-start(bf16[32,4096]{1,0:T(8,128)(2,1)} %param.8), channel_id=1, source_target_pairs={{0,8},{4,12},{8,0},{12,4},{16,24},{20,28},{24,16},{28,20},{1,9},{5... | collective-permute-start | bytes 786440 | tf_op jit(solution)/shard_map/ppermute | solution.py:64
  19.0 1.0 slice.293
  20.0 0.9 slice.288
  21.0 0.9 slice.289
  21.9 2.1 %collective-permute-start.13 = (bf16[16,4096]{1,0:T(8,128)(2,1)S(1)}, bf16[16,4096]{1,0:T(8,128)(2,1)S(1)}, u32[]{:S(2)}, u32[]{:S(2)}) collective-permute-start(bf16[16,4096]{1,0:T(8,128)(2,1)S(1)} %slice.293), channel_id=1, source_target_pairs={{0,16},{4,20},{8,24},{12,28},{16,0},{20,4},{24,8},{28,12},{1,17},{... | collective-permute-start | bytes 393224 | tf_op jit(solution)/shard_map/ppermute | solution.py:64
  24.0 0.9 slice.290
  25.1 1.6 %collective-permute-start.1 = (bf16[16,4096]{1,0:T(8,128)(2,1)S(1)}, bf16[16,4096]{1,0:T(8,128)(2,1)S(1)}, u32[]{:S(2)}, u32[]{:S(2)}) collective-permute-start(bf16[16,4096]{1,0:T(8,128)(2,1)S(1)} %slice.288), channel_id=1, source_target_pairs={{0,8},{4,12},{8,0},{12,4},{16,24},{20,28},{24,16},{28,20},{1,9},{5... | collective-permute-start | bytes 393224 | tf_op jit(solution)/shard_map/ppermute | solution.py:64
  27.7 2.1 %collective-permute-start.3 = (bf16[16,4096]{1,0:T(8,128)(2,1)S(1)}, bf16[16,4096]{1,0:T(8,128)(2,1)S(1)}, u32[]{:S(2)}, u32[]{:S(2)}) collective-permute-start(bf16[16,4096]{1,0:T(8,128)(2,1)S(1)} %slice.289), channel_id=1, source_target_pairs={{0,16},{4,20},{8,24},{12,28},{16,0},{20,4},{24,8},{28,12},{1,17},{... | collective-permute-start | bytes 393224 | tf_op jit(solution)/shard_map/ppermute | solution.py:64
  29.8 1.5 %constant_dynamic-update-slice_fusion.2 = bf16[384,4096]{1,0:T(8,128)(2,1)S(1)} fusion(bf16[384,4096]{1,0:T(8,128)(2,1)S(1)} %constant_dynamic-update-slice_fusion.3, bf16[192,4096]{1,0:T(8,128)(2,1)} %collective-permute-done.9), kind=kLoop, calls=%fused_computation.179 | loop fusion | bytes 3145728 | tf_op jit(solution)/shard_map/concatenate | solution.py:85
  31.4 2.1 %fusion.24 = f32[96,384]{1,0:T(8,128)S(1)} fusion(bf16[384,4096]{1,0:T(8,128)(2,1)S(1)} %constant_dynamic-update-slice_fusion.2, bf16[32,4096]{1,0:T(8,128)(2,1)S(1)} %collective-permute-done.10, bf16[32,4096]{1,0:T(8,128)(2,1)} %collective-permute-done.12, bf16[32,4096]{1,0:T(8,128)(2,1)S(1)} %copy-done.2), kind=kOutput, calls=%fused_computation.27 | convolution fusion | flops 304349184 | bytes 4079616 | tf_op jit(solution)/shard_map/dot_general | solution.py:18
  33.5 1.0 collective-permute-start.6
  34.4 1.5 %constant_dynamic-update-slice_fusion = bf16[384,4096]{1,0:T(8,128)(2,1)S(1)} fusion(bf16[384,4096]{1,0:T(8,128)(2,1)S(1)} %copy-done, bf16[192,4096]{1,0:T(8,128)(2,1)} %collective-permute-done.4), kind=kLoop, calls=%fused_computation.177 | loop fusion | bytes 3145728 | tf_op jit(solution)/shard_map/concatenate | solution.py:86
  36.0 2.1 %fusion.12 = f32[96,384]{1,0:T(8,128)S(1)} fusion(bf16[384,4096]{1,0:T(8,128)(2,1)S(1)} %constant_dynamic-update-slice_fusion, bf16[32,4096]{1,0:T(8,128)(2,1)} %collective-permute-done, bf16[32,4096]{1,0:T(8,128)(2,1)} %collective-permute-done.2, bf16[32,4096]{1,0:T(8,128)(2,1)S(1)} %copy-done.3), kind=kOutput, calls=%fused_computation.15 | convolution fusion | flops 304349184 | bytes 4079616 | tf_op jit(solution)/shard_map/dot_general | solution.py:18
  38.1 2.2 %fusion.64 = (bf16[96,384]{1,0:T(8,128)(2,1)S(1)}, bf16[96,384]{1,0:T(8,128)(2,1)S(1)}, bf16[96,384]{1,0:T(8,128)(2,1)S(1)}) fusion(s32[96]{0:T(128)S(1)} %sub.54, s32[384]{0:T(512)S(1)} %sub.45, f32[96,384]{1,0:T(8,128)S(1)} %fusion.24, f32[96,384]{1,0:T(8,128)S(1)} %fusion.12, bf16[384,4096]{1,0:T(8,128)(2,1)S(1)} %constant_dynamic-update-slice_fusion.2, ...), kind=kOutput, calls=%fused_computation.127 | convolution fusion | flops 305491968 | bytes 4450176 | tf_op jit(solution)/shard_map/dot_general | solution.py:18
  40.5 1.0 fusion.38
  41.6 1.0 fusion.30
  42.6 2.7 %collective-permute-done.8 = bf16[16,4096]{1,0:T(8,128)(2,1)S(1)} collective-permute-done((bf16[16,4096]{1,0:T(8,128)(2,1)S(1)}, bf16[16,4096]{1,0:T(8,128)(2,1)S(1)}, u32[]{:S(2)}, u32[]{:S(2)}) %collective-permute-start.8) | collective-permute-done | bytes 131104 | tf_op jit(solution)/shard_map/ppermute | solution.py:64
  45.3 1.1 select_select_fusion.2
  51.5 1.1 collective-permute-start.44
  53.2 1.9 %collective-permute-start.28 = (bf16[16,4096]{1,0:T(8,128)(2,1)S(1)}, bf16[16,4096]{1,0:T(8,128)(2,1)S(1)}, u32[]{:S(2)}, u32[]{:S(2)}) collective-permute-start(bf16[16,4096]{1,0:T(8,128)(2,1)S(1)} %get-tuple-element.46), channel_id=1, source_target_pairs={{0,16},{4,20},{8,24},{12,28},{16,0},{20,4},{24,8},{28,12},{1,17},{... | collective-permute-start | bytes 393224 | tf_op jit(solution)/shard_map/ppermute | solution.py:64
  55.2 1.5 %collective-permute-done.42 = bf16[16,4096]{1,0:T(8,128)(2,1)S(1)} collective-permute-done((bf16[16,4096]{1,0:T(8,128)(2,1)S(1)}, bf16[16,4096]{1,0:T(8,128)(2,1)S(1)}, u32[]{:S(2)}, u32[]{:S(2)}) %collective-permute-start.42) | collective-permute-done | bytes 131104 | tf_op jit(solution)/shard_map/ppermute | solution.py:64
  56.7 1.4 %collective-permute-start.30 = (bf16[16,4096]{1,0:T(8,128)(2,1)S(1)}, bf16[16,4096]{1,0:T(8,128)(2,1)S(1)}, u32[]{:S(2)}, u32[]{:S(2)}) collective-permute-start(bf16[16,4096]{1,0:T(8,128)(2,1)S(1)} %get-tuple-element.47), channel_id=1, source_target_pairs={{0,8},{4,12},{8,0},{12,4},{16,24},{20,28},{24,16},{28,20},{1,9},{5... | collective-permute-start | bytes 393224 | tf_op jit(solution)/shard_map/ppermute | solution.py:64
  58.2 0.9 collective-permute-done.28
  59.2 1.4 %collective-permute-start.14 = (bf16[16,4096]{1,0:T(8,128)(2,1)S(1)}, bf16[16,4096]{1,0:T(8,128)(2,1)S(1)}, u32[]{:S(2)}, u32[]{:S(2)}) collective-permute-start(bf16[16,4096]{1,0:T(8,128)(2,1)S(1)} %get-tuple-element.48), channel_id=1, source_target_pairs={{0,16},{4,20},{8,24},{12,28},{16,0},{20,4},{24,8},{28,12},{1,17},{... | collective-permute-start | bytes 393224 | tf_op jit(solution)/shard_map/ppermute | solution.py:64
  60.6 1.1 collective-permute-done.30
  61.6 1.4 %collective-permute-start.16 = (bf16[16,4096]{1,0:T(8,128)(2,1)S(1)}, bf16[16,4096]{1,0:T(8,128)(2,1)S(1)}, u32[]{:S(2)}, u32[]{:S(2)}) collective-permute-start(bf16[16,4096]{1,0:T(8,128)(2,1)S(1)} %get-tuple-element.49), channel_id=1, source_target_pairs={{0,8},{4,12},{8,0},{12,4},{16,24},{20,28},{24,16},{28,20},{1,9},{5... | collective-permute-start | bytes 393224 | tf_op jit(solution)/shard_map/ppermute | solution.py:64
  63.2 1.0 collective-permute-done.14
  64.2 2.4 %collective-permute-done.16 = bf16[16,4096]{1,0:T(8,128)(2,1)S(1)} collective-permute-done((bf16[16,4096]{1,0:T(8,128)(2,1)S(1)}, bf16[16,4096]{1,0:T(8,128)(2,1)S(1)}, u32[]{:S(2)}, u32[]{:S(2)}) %collective-permute-start.16) | collective-permute-done | bytes 131104 | tf_op jit(solution)/shard_map/ppermute | solution.py:64
  66.8 2.8 %collective-permute-done.43 = bf16[32,2048]{1,0:T(8,128)(2,1)S(1)} collective-permute-done((bf16[32,2048]{1,0:T(8,128)(2,1)S(1)}, bf16[32,2048]{1,0:T(8,128)(2,1)S(1)}, u32[]{:S(2)}, u32[]{:S(2)}) %collective-permute-start.43) | collective-permute-done | bytes 131104 | tf_op jit(solution)/shard_map/ppermute | solution.py:64
  70.2 1.1 collective-permute-done.45
  71.8 3.6 %collective-permute-done.50 = bf16[32,2048]{1,0:T(8,128)(2,1)S(1)} collective-permute-done((bf16[32,2048]{1,0:T(8,128)(2,1)S(1)}, bf16[32,2048]{1,0:T(8,128)(2,1)S(1)}, u32[]{:S(2)}, u32[]{:S(2)}) %collective-permute-start.50) | collective-permute-done | bytes 131104 | tf_op jit(solution)/shard_map/ppermute | solution.py:64
  75.4 0.9 collective-permute-start.29
  77.6 3.3 %collective-permute-done.29 = bf16[32,2048]{1,0:T(8,128)(2,1)S(1)} collective-permute-done((bf16[32,2048]{1,0:T(8,128)(2,1)S(1)}, bf16[32,2048]{1,0:T(8,128)(2,1)S(1)}, u32[]{:S(2)}, u32[]{:S(2)}) %collective-permute-start.29) | collective-permute-done | bytes 131104 | tf_op jit(solution)/shard_map/ppermute | solution.py:64
  80.9 1.2 collective-permute-start.36
  83.8 2.4 %collective-permute-done.36 = bf16[32,2048]{1,0:T(8,128)(2,1)S(1)} collective-permute-done((bf16[32,2048]{1,0:T(8,128)(2,1)S(1)}, bf16[32,2048]{1,0:T(8,128)(2,1)S(1)}, u32[]{:S(2)}, u32[]{:S(2)}) %collective-permute-start.36) | collective-permute-done | bytes 131104 | tf_op jit(solution)/shard_map/ppermute | solution.py:64
  86.3 1.7 %collective-permute-start.17 = (bf16[32,2048]{1,0:T(8,128)(2,1)S(1)}, bf16[32,2048]{1,0:T(8,128)(2,1)S(1)}, u32[]{:S(2)}, u32[]{:S(2)}) collective-permute-start(bf16[32,2048]{1,0:T(8,128)(2,1)S(1)} %pad_maximum_fusion.4), channel_id=1, source_target_pairs={{0,20},{4,16},{8,28},{12,24},{16,4},{20,0},{24,12},{28,8},{1,21},{... | collective-permute-start | bytes 393224 | tf_op jit(solution)/shard_map/ppermute | solution.py:64
  89.1 0.9 collective-permute-start.23
  90.0 3.5 %collective-permute-start.47 = (bf16[32,2048]{1,0:T(8,128)(2,1)S(1)}, bf16[32,2048]{1,0:T(8,128)(2,1)S(1)}, u32[]{:S(2)}, u32[]{:S(2)}) collective-permute-start(bf16[32,2048]{1,0:T(8,128)(2,1)S(1)} %fusion.46), channel_id=1, source_target_pairs={{0,1},{3,2},{4,5},{7,6},{8,9},{11,10},{12,13},{15,14},{16,17},{19,... | collective-permute-start | bytes 393224 | tf_op jit(solution)/shard_map/ppermute | solution.py:68
  93.6 1.8 %collective-permute-start.53 = (bf16[32,2048]{1,0:T(8,128)(2,1)S(1)}, bf16[32,2048]{1,0:T(8,128)(2,1)S(1)}, u32[]{:S(2)}, u32[]{:S(2)}) collective-permute-start(bf16[32,2048]{1,0:T(8,128)(2,1)S(1)} %fusion.47), channel_id=1, source_target_pairs={{0,1},{3,2},{4,5},{7,6},{8,9},{11,10},{12,13},{15,14},{16,17},{19,... | collective-permute-start | bytes 393224 | tf_op jit(solution)/shard_map/ppermute | solution.py:68
  95.4 1.3 collective-permute-start.33
  96.8 1.3 collective-permute-start.39
  98.1 1.3 collective-permute-start.19
  99.4 1.6 %collective-permute-start.25 = (bf16[32,2048]{1,0:T(8,128)(2,1)S(1)}, bf16[32,2048]{1,0:T(8,128)(2,1)S(1)}, u32[]{:S(2)}, u32[]{:S(2)}) collective-permute-start(bf16[32,2048]{1,0:T(8,128)(2,1)S(1)} %fusion.43), channel_id=1, source_target_pairs={{0,1},{3,2},{4,5},{7,6},{8,9},{11,10},{12,13},{15,14},{16,17},{19,... | collective-permute-start | bytes 393224 | tf_op jit(solution)/shard_map/ppermute | solution.py:68
  103.0 2.1 %collective-permute-done.39 = bf16[32,2048]{1,0:T(8,128)(2,1)S(1)} collective-permute-done((bf16[32,2048]{1,0:T(8,128)(2,1)S(1)}, bf16[32,2048]{1,0:T(8,128)(2,1)S(1)}, u32[]{:S(2)}, u32[]{:S(2)}) %collective-permute-start.39) | collective-permute-done | bytes 131104 | tf_op jit(solution)/shard_map/ppermute | solution.py:68
  105.8 2.1 %collective-permute-done.19 = bf16[32,2048]{1,0:T(8,128)(2,1)S(1)} collective-permute-done((bf16[32,2048]{1,0:T(8,128)(2,1)S(1)}, bf16[32,2048]{1,0:T(8,128)(2,1)S(1)}, u32[]{:S(2)}, u32[]{:S(2)}) %collective-permute-start.19) | collective-permute-done | bytes 131104 | tf_op jit(solution)/shard_map/ppermute | solution.py:68
  108.6 1.7 %collective-permute-done.25 = bf16[32,2048]{1,0:T(8,128)(2,1)S(1)} collective-permute-done((bf16[32,2048]{1,0:T(8,128)(2,1)S(1)}, bf16[32,2048]{1,0:T(8,128)(2,1)S(1)}, u32[]{:S(2)}, u32[]{:S(2)}) %collective-permute-start.25) | collective-permute-done | bytes 131104 | tf_op jit(solution)/shard_map/ppermute | solution.py:68
  111.8 1.3 collective-permute-start.49
  113.2 1.3 collective-permute-start.55
  114.6 1.3 collective-permute-start.35
  116.0 1.3 collective-permute-start.41
  117.5 1.3 collective-permute-start.21
  118.9 7.2 %collective-permute-done.49 = bf16[32,2048]{1,0:T(8,128)(2,1)S(1)} collective-permute-done((bf16[32,2048]{1,0:T(8,128)(2,1)S(1)}, bf16[32,2048]{1,0:T(8,128)(2,1)S(1)}, u32[]{:S(2)}, u32[]{:S(2)}) %collective-permute-start.49) | collective-permute-done | bytes 131104 | tf_op jit(solution)/shard_map/ppermute | solution.py:68
  126.0 1.3 collective-permute-start.27
  127.4 1.5 %collective-permute-done.55 = bf16[32,2048]{1,0:T(8,128)(2,1)S(1)} collective-permute-done((bf16[32,2048]{1,0:T(8,128)(2,1)S(1)}, bf16[32,2048]{1,0:T(8,128)(2,1)S(1)}, u32[]{:S(2)}, u32[]{:S(2)}) %collective-permute-start.55) | collective-permute-done | bytes 131104 | tf_op jit(solution)/shard_map/ppermute | solution.py:68
  128.9 2.8 %collective-permute-done.35 = bf16[32,2048]{1,0:T(8,128)(2,1)S(1)} collective-permute-done((bf16[32,2048]{1,0:T(8,128)(2,1)S(1)}, bf16[32,2048]{1,0:T(8,128)(2,1)S(1)}, u32[]{:S(2)}, u32[]{:S(2)}) %collective-permute-start.35) | collective-permute-done | bytes 131104 | tf_op jit(solution)/shard_map/ppermute | solution.py:68
  131.7 2.8 %collective-permute-done.41 = bf16[32,2048]{1,0:T(8,128)(2,1)S(1)} collective-permute-done((bf16[32,2048]{1,0:T(8,128)(2,1)S(1)}, bf16[32,2048]{1,0:T(8,128)(2,1)S(1)}, u32[]{:S(2)}, u32[]{:S(2)}) %collective-permute-start.41) | collective-permute-done | bytes 131104 | tf_op jit(solution)/shard_map/ppermute | solution.py:68
  (150 shorter events, 23.4 us)
Async XLA Ops:
  0.6 7.1 %copy-start.1 = (bf16[192,4096]{1,0:T(8,128)(2,1)S(1)}, bf16[192,4096]{1,0:T(8,128)(2,1)}, u32[]{:S(2)}) copy-start(bf16[192,4096]{1,0:T(8,128)(2,1)} %param.6) | copy-start | bytes 4718596
  0.6 10.4 %collective-permute-start.10 = (bf16[32,4096]{1,0:T(8,128)(2,1)}, bf16[32,4096]{1,0:T(8,128)(2,1)S(1)}, u32[]{:S(2)}, u32[]{:S(2)}) collective-permute-start(bf16[32,4096]{1,0:T(8,128)(2,1)} %param.7), channel_id=1, source_target_pairs={{0,16},{4,20},{8,24},{12,28},{16,0},{20,4},{24,8},{28,12},{1,17},{... | collective-permute-start | bytes 786440 | tf_op jit(solution)/shard_map/ppermute | solution.py:64
  3.7 9.4 %collective-permute-start.12 = (bf16[32,4096]{1,0:T(8,128)(2,1)}, bf16[32,4096]{1,0:T(8,128)(2,1)}, u32[]{:S(2)}, u32[]{:S(2)}) collective-permute-start(bf16[32,4096]{1,0:T(8,128)(2,1)} %param.7), channel_id=1, source_target_pairs={{0,8},{4,12},{8,0},{12,4},{16,24},{20,28},{24,16},{28,20},{1,9},{5... | collective-permute-start | bytes 786440 | tf_op jit(solution)/shard_map/ppermute | solution.py:64
  5.2 22.5 %collective-permute-start.9 = (bf16[192,4096]{1,0:T(8,128)(2,1)}, bf16[192,4096]{1,0:T(8,128)(2,1)}, u32[]{:S(2)}, u32[]{:S(2)}) collective-permute-start(bf16[192,4096]{1,0:T(8,128)(2,1)} %param.5), channel_id=1, source_target_pairs={{0,4},{4,0},{8,12},{12,8},{16,20},{20,16},{24,28},{28,24},{1,5},{5... | collective-permute-start | bytes 4718600 | tf_op jit(solution)/shard_map/ppermute | solution.py:64
  5.2 28.3 %collective-permute-start.4 = (bf16[192,4096]{1,0:T(8,128)(2,1)}, bf16[192,4096]{1,0:T(8,128)(2,1)}, u32[]{:S(2)}, u32[]{:S(2)}) collective-permute-start(bf16[192,4096]{1,0:T(8,128)(2,1)} %param.6), channel_id=1, source_target_pairs={{0,4},{4,0},{8,12},{12,8},{16,20},{20,16},{24,28},{28,24},{1,5},{5... | collective-permute-start | bytes 4718600 | tf_op jit(solution)/shard_map/ppermute | solution.py:64
  5.7 11.1 %collective-permute-start = (bf16[32,4096]{1,0:T(8,128)(2,1)}, bf16[32,4096]{1,0:T(8,128)(2,1)}, u32[]{:S(2)}, u32[]{:S(2)}) collective-permute-start(bf16[32,4096]{1,0:T(8,128)(2,1)} %param.9), channel_id=1, source_target_pairs={{0,16},{4,20},{8,24},{12,28},{16,0},{20,4},{24,8},{28,12},{1,17},{... | collective-permute-start | bytes 786440 | tf_op jit(solution)/shard_map/ppermute | solution.py:64
  11.0 9.9 %collective-permute-start.2 = (bf16[32,4096]{1,0:T(8,128)(2,1)}, bf16[32,4096]{1,0:T(8,128)(2,1)}, u32[]{:S(2)}, u32[]{:S(2)}) collective-permute-start(bf16[32,4096]{1,0:T(8,128)(2,1)} %param.9), channel_id=1, source_target_pairs={{0,8},{4,12},{8,0},{12,4},{16,24},{20,28},{24,16},{28,20},{1,9},{5... | collective-permute-start | bytes 786440 | tf_op jit(solution)/shard_map/ppermute | solution.py:64
  13.1 8.9 %collective-permute-start.5 = (bf16[32,4096]{1,0:T(8,128)(2,1)}, bf16[32,4096]{1,0:T(8,128)(2,1)}, u32[]{:S(2)}, u32[]{:S(2)}) collective-permute-start(bf16[32,4096]{1,0:T(8,128)(2,1)} %param.8), channel_id=1, source_target_pairs={{0,16},{4,20},{8,24},{12,28},{16,0},{20,4},{24,8},{28,12},{1,17},{... | collective-permute-start | bytes 786440 | tf_op jit(solution)/shard_map/ppermute | solution.py:64
  16.7 8.4 %collective-permute-start.7 = (bf16[32,4096]{1,0:T(8,128)(2,1)}, bf16[32,4096]{1,0:T(8,128)(2,1)}, u32[]{:S(2)}, u32[]{:S(2)}) collective-permute-start(bf16[32,4096]{1,0:T(8,128)(2,1)} %param.8), channel_id=1, source_target_pairs={{0,8},{4,12},{8,0},{12,4},{16,24},{20,28},{24,16},{28,20},{1,9},{5... | collective-permute-start | bytes 786440 | tf_op jit(solution)/shard_map/ppermute | solution.py:64
  19.0 12.3 %copy-start.2 = (bf16[32,4096]{1,0:T(8,128)(2,1)S(1)}, bf16[32,4096]{1,0:T(8,128)(2,1)}, u32[]{:S(2)}) copy-start(bf16[32,4096]{1,0:T(8,128)(2,1)} %param.7) | copy-start | bytes 786436
  20.9 19.3 %collective-permute-start.11 = (bf16[16,4096]{1,0:T(8,128)(2,1)S(1)}, bf16[16,4096]{1,0:T(8,128)(2,1)S(1)}, u32[]{:S(2)}, u32[]{:S(2)}) collective-permute-start(bf16[16,4096]{1,0:T(8,128)(2,1)S(1)} %slice.292), channel_id=1, source_target_pairs={{0,8},{4,12},{8,0},{12,4},{16,24},{20,28},{24,16},{28,20},{1,9},{5... | collective-permute-start | bytes 393224 | tf_op jit(solution)/shard_map/ppermute | solution.py:64
  21.9 18.6 %collective-permute-start.13 = (bf16[16,4096]{1,0:T(8,128)(2,1)S(1)}, bf16[16,4096]{1,0:T(8,128)(2,1)S(1)}, u32[]{:S(2)}, u32[]{:S(2)}) collective-permute-start(bf16[16,4096]{1,0:T(8,128)(2,1)S(1)} %slice.293), channel_id=1, source_target_pairs={{0,16},{4,20},{8,24},{12,28},{16,0},{20,4},{24,8},{28,12},{1,17},{... | collective-permute-start | bytes 393224 | tf_op jit(solution)/shard_map/ppermute | solution.py:64
  25.1 16.4 %collective-permute-start.1 = (bf16[16,4096]{1,0:T(8,128)(2,1)S(1)}, bf16[16,4096]{1,0:T(8,128)(2,1)S(1)}, u32[]{:S(2)}, u32[]{:S(2)}) collective-permute-start(bf16[16,4096]{1,0:T(8,128)(2,1)S(1)} %slice.288), channel_id=1, source_target_pairs={{0,8},{4,12},{8,0},{12,4},{16,24},{20,28},{24,16},{28,20},{1,9},{5... | collective-permute-start | bytes 393224 | tf_op jit(solution)/shard_map/ppermute | solution.py:64
  27.7 6.8 %copy-start = (bf16[384,4096]{1,0:T(8,128)(2,1)S(1)}, bf16[384,4096]{1,0:T(8,128)(2,1)}, u32[]{:S(2)}) copy-start(bf16[384,4096]{1,0:T(8,128)(2,1)} %constant_dynamic-update-slice_fusion.1) | copy-start | bytes 9437188
  27.7 13.9 %collective-permute-start.3 = (bf16[16,4096]{1,0:T(8,128)(2,1)S(1)}, bf16[16,4096]{1,0:T(8,128)(2,1)S(1)}, u32[]{:S(2)}, u32[]{:S(2)}) collective-permute-start(bf16[16,4096]{1,0:T(8,128)(2,1)S(1)} %slice.289), channel_id=1, source_target_pairs={{0,16},{4,20},{8,24},{12,28},{16,0},{20,4},{24,8},{28,12},{1,17},{... | collective-permute-start | bytes 393224 | tf_op jit(solution)/shard_map/ppermute | solution.py:64
  31.4 4.6 %copy-start.3 = (bf16[32,4096]{1,0:T(8,128)(2,1)S(1)}, bf16[32,4096]{1,0:T(8,128)(2,1)}, u32[]{:S(2)}) copy-start(bf16[32,4096]{1,0:T(8,128)(2,1)} %param.9) | copy-start | bytes 786436
  33.4 4.6 %copy-start.4 = (bf16[32,4096]{1,0:T(8,128)(2,1)S(1)}, bf16[32,4096]{1,0:T(8,128)(2,1)}, u32[]{:S(2)}) copy-start(bf16[32,4096]{1,0:T(8,128)(2,1)} %param.8) | copy-start | bytes 786436
  33.5 9.1 %collective-permute-start.6 = (bf16[16,4096]{1,0:T(8,128)(2,1)S(1)}, bf16[16,4096]{1,0:T(8,128)(2,1)S(1)}, u32[]{:S(2)}, u32[]{:S(2)}) collective-permute-start(bf16[16,4096]{1,0:T(8,128)(2,1)S(1)} %slice.290), channel_id=1, source_target_pairs={{0,8},{4,12},{8,0},{12,4},{16,24},{20,28},{24,16},{28,20},{1,9},{5... | collective-permute-start | bytes 393224 | tf_op jit(solution)/shard_map/ppermute | solution.py:64
  40.3 5.0 %collective-permute-start.8 = (bf16[16,4096]{1,0:T(8,128)(2,1)S(1)}, bf16[16,4096]{1,0:T(8,128)(2,1)S(1)}, u32[]{:S(2)}, u32[]{:S(2)}) collective-permute-start(bf16[16,4096]{1,0:T(8,128)(2,1)S(1)} %slice.291), channel_id=1, source_target_pairs={{0,16},{4,20},{8,24},{12,28},{16,0},{20,4},{24,8},{28,12},{1,17},{... | collective-permute-start | bytes 393224 | tf_op jit(solution)/shard_map/ppermute | solution.py:64
  51.3 5.3 %collective-permute-start.42 = (bf16[16,4096]{1,0:T(8,128)(2,1)S(1)}, bf16[16,4096]{1,0:T(8,128)(2,1)S(1)}, u32[]{:S(2)}, u32[]{:S(2)}) collective-permute-start(bf16[16,4096]{1,0:T(8,128)(2,1)S(1)} %get-tuple-element.44), channel_id=1, source_target_pairs={{0,16},{4,20},{8,24},{12,28},{16,0},{20,4},{24,8},{28,12},{1,17},{... | collective-permute-start | bytes 393224 | tf_op jit(solution)/shard_map/ppermute | solution.py:64
  51.5 6.5 %collective-permute-start.44 = (bf16[16,4096]{1,0:T(8,128)(2,1)S(1)}, bf16[16,4096]{1,0:T(8,128)(2,1)S(1)}, u32[]{:S(2)}, u32[]{:S(2)}) collective-permute-start(bf16[16,4096]{1,0:T(8,128)(2,1)S(1)} %get-tuple-element.45), channel_id=1, source_target_pairs={{0,8},{4,12},{8,0},{12,4},{16,24},{20,28},{24,16},{28,20},{1,9},{5... | collective-permute-start | bytes 393224 | tf_op jit(solution)/shard_map/ppermute | solution.py:64
  52.7 14.1 %collective-permute-start.46 = (bf16[32,2048]{1,0:T(8,128)(2,1)S(1)}, bf16[32,2048]{1,0:T(8,128)(2,1)S(1)}, u32[]{:S(2)}, u32[]{:S(2)}) collective-permute-start(bf16[32,2048]{1,0:T(8,128)(2,1)S(1)} %slice.346), channel_id=1, source_target_pairs={{0,4},{4,0},{8,12},{12,8},{16,20},{20,16},{24,28},{28,24},{1,5},{5... | collective-permute-start | bytes 393224 | tf_op jit(solution)/shard_map/ppermute | solution.py:64
  52.7 19.1 %collective-permute-start.52 = (bf16[32,2048]{1,0:T(8,128)(2,1)S(1)}, bf16[32,2048]{1,0:T(8,128)(2,1)S(1)}, u32[]{:S(2)}, u32[]{:S(2)}) collective-permute-start(bf16[32,2048]{1,0:T(8,128)(2,1)S(1)} %slice.354), channel_id=1, source_target_pairs={{0,4},{4,0},{8,12},{12,8},{16,20},{20,16},{24,28},{28,24},{1,5},{5... | collective-permute-start | bytes 393224 | tf_op jit(solution)/shard_map/ppermute | solution.py:64
  53.2 5.9 %collective-permute-start.28 = (bf16[16,4096]{1,0:T(8,128)(2,1)S(1)}, bf16[16,4096]{1,0:T(8,128)(2,1)S(1)}, u32[]{:S(2)}, u32[]{:S(2)}) collective-permute-start(bf16[16,4096]{1,0:T(8,128)(2,1)S(1)} %get-tuple-element.46), channel_id=1, source_target_pairs={{0,16},{4,20},{8,24},{12,28},{16,0},{20,4},{24,8},{28,12},{1,17},{... | collective-permute-start | bytes 393224 | tf_op jit(solution)/shard_map/ppermute | solution.py:64
  56.7 5.0 %collective-permute-start.30 = (bf16[16,4096]{1,0:T(8,128)(2,1)S(1)}, bf16[16,4096]{1,0:T(8,128)(2,1)S(1)}, u32[]{:S(2)}, u32[]{:S(2)}) collective-permute-start(bf16[16,4096]{1,0:T(8,128)(2,1)S(1)} %get-tuple-element.47), channel_id=1, source_target_pairs={{0,8},{4,12},{8,0},{12,4},{16,24},{20,28},{24,16},{28,20},{1,9},{5... | collective-permute-start | bytes 393224 | tf_op jit(solution)/shard_map/ppermute | solution.py:64
  58.1 19.4 %collective-permute-start.32 = (bf16[32,2048]{1,0:T(8,128)(2,1)S(1)}, bf16[32,2048]{1,0:T(8,128)(2,1)S(1)}, u32[]{:S(2)}, u32[]{:S(2)}) collective-permute-start(bf16[32,2048]{1,0:T(8,128)(2,1)S(1)} %slice.326), channel_id=1, source_target_pairs={{0,4},{4,0},{8,12},{12,8},{16,20},{20,16},{24,28},{28,24},{1,5},{5... | collective-permute-start | bytes 393224 | tf_op jit(solution)/shard_map/ppermute | solution.py:64
  59.2 5.1 %collective-permute-start.14 = (bf16[16,4096]{1,0:T(8,128)(2,1)S(1)}, bf16[16,4096]{1,0:T(8,128)(2,1)S(1)}, u32[]{:S(2)}, u32[]{:S(2)}) collective-permute-start(bf16[16,4096]{1,0:T(8,128)(2,1)S(1)} %get-tuple-element.48), channel_id=1, source_target_pairs={{0,16},{4,20},{8,24},{12,28},{16,0},{20,4},{24,8},{28,12},{1,17},{... | collective-permute-start | bytes 393224 | tf_op jit(solution)/shard_map/ppermute | solution.py:64
  61.6 5.0 %collective-permute-start.16 = (bf16[16,4096]{1,0:T(8,128)(2,1)S(1)}, bf16[16,4096]{1,0:T(8,128)(2,1)S(1)}, u32[]{:S(2)}, u32[]{:S(2)}) collective-permute-start(bf16[16,4096]{1,0:T(8,128)(2,1)S(1)} %get-tuple-element.49), channel_id=1, source_target_pairs={{0,8},{4,12},{8,0},{12,4},{16,24},{20,28},{24,16},{28,20},{1,9},{5... | collective-permute-start | bytes 393224 | tf_op jit(solution)/shard_map/ppermute | solution.py:64
  64.2 5.4 %collective-permute-start.43 = (bf16[32,2048]{1,0:T(8,128)(2,1)S(1)}, bf16[32,2048]{1,0:T(8,128)(2,1)S(1)}, u32[]{:S(2)}, u32[]{:S(2)}) collective-permute-start(bf16[32,2048]{1,0:T(8,128)(2,1)S(1)} %pad_maximum_fusion.11), channel_id=1, source_target_pairs={{0,12},{4,8},{8,4},{12,0},{16,28},{20,24},{24,20},{28,16},{1,13},{... | collective-permute-start | bytes 393224 | tf_op jit(solution)/shard_map/ppermute | solution.py:64
  66.6 4.8 %collective-permute-start.45 = (bf16[32,2048]{1,0:T(8,128)(2,1)S(1)}, bf16[32,2048]{1,0:T(8,128)(2,1)S(1)}, u32[]{:S(2)}, u32[]{:S(2)}) collective-permute-start(bf16[32,2048]{1,0:T(8,128)(2,1)S(1)} %pad_maximum_fusion.12), channel_id=1, source_target_pairs={{0,20},{4,16},{8,28},{12,24},{16,4},{20,0},{24,12},{28,8},{1,21},{... | collective-permute-start | bytes 393224 | tf_op jit(solution)/shard_map/ppermute | solution.py:64
  66.7 16.3 %collective-permute-start.38 = (bf16[32,2048]{1,0:T(8,128)(2,1)S(1)}, bf16[32,2048]{1,0:T(8,128)(2,1)S(1)}, u32[]{:S(2)}, u32[]{:S(2)}) collective-permute-start(bf16[32,2048]{1,0:T(8,128)(2,1)S(1)} %slice.333), channel_id=1, source_target_pairs={{0,4},{4,0},{8,12},{12,8},{16,20},{20,16},{24,28},{28,24},{1,5},{5... | collective-permute-start | bytes 393224 | tf_op jit(solution)/shard_map/ppermute | solution.py:64
  69.6 5.8 %collective-permute-start.50 = (bf16[32,2048]{1,0:T(8,128)(2,1)S(1)}, bf16[32,2048]{1,0:T(8,128)(2,1)S(1)}, u32[]{:S(2)}, u32[]{:S(2)}) collective-permute-start(bf16[32,2048]{1,0:T(8,128)(2,1)S(1)} %pad_maximum_fusion.13), channel_id=1, source_target_pairs={{0,12},{4,8},{8,4},{12,0},{16,28},{20,24},{24,20},{28,16},{1,13},{... | collective-permute-start | bytes 393224 | tf_op jit(solution)/shard_map/ppermute | solution.py:64
  71.4 5.6 %collective-permute-start.51 = (bf16[32,2048]{1,0:T(8,128)(2,1)S(1)}, bf16[32,2048]{1,0:T(8,128)(2,1)S(1)}, u32[]{:S(2)}, u32[]{:S(2)}) collective-permute-start(bf16[32,2048]{1,0:T(8,128)(2,1)S(1)} %pad_maximum_fusion.14), channel_id=1, source_target_pairs={{0,20},{4,16},{8,28},{12,24},{16,4},{20,0},{24,12},{28,8},{1,21},{... | collective-permute-start | bytes 393224 | tf_op jit(solution)/shard_map/ppermute | solution.py:64
  71.7 17.3 %collective-permute-start.18 = (bf16[32,2048]{1,0:T(8,128)(2,1)S(1)}, bf16[32,2048]{1,0:T(8,128)(2,1)S(1)}, u32[]{:S(2)}, u32[]{:S(2)}) collective-permute-start(bf16[32,2048]{1,0:T(8,128)(2,1)S(1)} %slice.306), channel_id=1, source_target_pairs={{0,4},{4,0},{8,12},{12,8},{16,20},{20,16},{24,28},{28,24},{1,5},{5... | collective-permute-start | bytes 393224 | tf_op jit(solution)/shard_map/ppermute | solution.py:64
  75.4 5.5 %collective-permute-start.29 = (bf16[32,2048]{1,0:T(8,128)(2,1)S(1)}, bf16[32,2048]{1,0:T(8,128)(2,1)S(1)}, u32[]{:S(2)}, u32[]{:S(2)}) collective-permute-start(bf16[32,2048]{1,0:T(8,128)(2,1)S(1)} %pad_maximum_fusion.7), channel_id=1, source_target_pairs={{0,12},{4,8},{8,4},{12,0},{16,28},{20,24},{24,20},{28,16},{1,13},{... | collective-permute-start | bytes 393224 | tf_op jit(solution)/shard_map/ppermute | solution.py:64
  76.9 5.7 %collective-permute-start.31 = (bf16[32,2048]{1,0:T(8,128)(2,1)S(1)}, bf16[32,2048]{1,0:T(8,128)(2,1)S(1)}, u32[]{:S(2)}, u32[]{:S(2)}) collective-permute-start(bf16[32,2048]{1,0:T(8,128)(2,1)S(1)} %pad_maximum_fusion.8), channel_id=1, source_target_pairs={{0,20},{4,16},{8,28},{12,24},{16,4},{20,0},{24,12},{28,8},{1,21},{... | collective-permute-start | bytes 393224 | tf_op jit(solution)/shard_map/ppermute | solution.py:64
  77.5 18.0 %collective-permute-start.24 = (bf16[32,2048]{1,0:T(8,128)(2,1)S(1)}, bf16[32,2048]{1,0:T(8,128)(2,1)S(1)}, u32[]{:S(2)}, u32[]{:S(2)}) collective-permute-start(bf16[32,2048]{1,0:T(8,128)(2,1)S(1)} %slice.314), channel_id=1, source_target_pairs={{0,4},{4,0},{8,12},{12,8},{16,20},{20,16},{24,28},{28,24},{1,5},{5... | collective-permute-start | bytes 393224 | tf_op jit(solution)/shard_map/ppermute | solution.py:64
  80.9 5.3 %collective-permute-start.36 = (bf16[32,2048]{1,0:T(8,128)(2,1)S(1)}, bf16[32,2048]{1,0:T(8,128)(2,1)S(1)}, u32[]{:S(2)}, u32[]{:S(2)}) collective-permute-start(bf16[32,2048]{1,0:T(8,128)(2,1)S(1)} %pad_maximum_fusion.9), channel_id=1, source_target_pairs={{0,12},{4,8},{8,4},{12,0},{16,28},{20,24},{24,20},{28,16},{1,13},{... | collective-permute-start | bytes 393224 | tf_op jit(solution)/shard_map/ppermute | solution.py:64
  82.7 5.5 %collective-permute-start.37 = (bf16[32,2048]{1,0:T(8,128)(2,1)S(1)}, bf16[32,2048]{1,0:T(8,128)(2,1)S(1)}, u32[]{:S(2)}, u32[]{:S(2)}) collective-permute-start(bf16[32,2048]{1,0:T(8,128)(2,1)S(1)} %pad_maximum_fusion.10), channel_id=1, source_target_pairs={{0,20},{4,16},{8,28},{12,24},{16,4},{20,0},{24,12},{28,8},{1,21},{... | collective-permute-start | bytes 393224 | tf_op jit(solution)/shard_map/ppermute | solution.py:64
  83.0 7.0 %collective-permute-start.15 = (bf16[32,2048]{1,0:T(8,128)(2,1)S(1)}, bf16[32,2048]{1,0:T(8,128)(2,1)S(1)}, u32[]{:S(2)}, u32[]{:S(2)}) collective-permute-start(bf16[32,2048]{1,0:T(8,128)(2,1)S(1)} %pad_maximum_fusion.3), channel_id=1, source_target_pairs={{0,12},{4,8},{8,4},{12,0},{16,28},{20,24},{24,20},{28,16},{1,13},{... | collective-permute-start | bytes 393224 | tf_op jit(solution)/shard_map/ppermute | solution.py:64
  86.3 7.3 %collective-permute-start.17 = (bf16[32,2048]{1,0:T(8,128)(2,1)S(1)}, bf16[32,2048]{1,0:T(8,128)(2,1)S(1)}, u32[]{:S(2)}, u32[]{:S(2)}) collective-permute-start(bf16[32,2048]{1,0:T(8,128)(2,1)S(1)} %pad_maximum_fusion.4), channel_id=1, source_target_pairs={{0,20},{4,16},{8,28},{12,24},{16,4},{20,0},{24,12},{28,8},{1,21},{... | collective-permute-start | bytes 393224 | tf_op jit(solution)/shard_map/ppermute | solution.py:64
  88.2 8.6 %collective-permute-start.22 = (bf16[32,2048]{1,0:T(8,128)(2,1)S(1)}, bf16[32,2048]{1,0:T(8,128)(2,1)S(1)}, u32[]{:S(2)}, u32[]{:S(2)}) collective-permute-start(bf16[32,2048]{1,0:T(8,128)(2,1)S(1)} %pad_maximum_fusion.5), channel_id=1, source_target_pairs={{0,12},{4,8},{8,4},{12,0},{16,28},{20,24},{24,20},{28,16},{1,13},{... | collective-permute-start | bytes 393224 | tf_op jit(solution)/shard_map/ppermute | solution.py:64
  89.1 9.0 %collective-permute-start.23 = (bf16[32,2048]{1,0:T(8,128)(2,1)S(1)}, bf16[32,2048]{1,0:T(8,128)(2,1)S(1)}, u32[]{:S(2)}, u32[]{:S(2)}) collective-permute-start(bf16[32,2048]{1,0:T(8,128)(2,1)S(1)} %pad_maximum_fusion.6), channel_id=1, source_target_pairs={{0,20},{4,16},{8,28},{12,24},{16,4},{20,0},{24,12},{28,8},{1,21},{... | collective-permute-start | bytes 393224 | tf_op jit(solution)/shard_map/ppermute | solution.py:64
  90.0 9.4 %collective-permute-start.47 = (bf16[32,2048]{1,0:T(8,128)(2,1)S(1)}, bf16[32,2048]{1,0:T(8,128)(2,1)S(1)}, u32[]{:S(2)}, u32[]{:S(2)}) collective-permute-start(bf16[32,2048]{1,0:T(8,128)(2,1)S(1)} %fusion.46), channel_id=1, source_target_pairs={{0,1},{3,2},{4,5},{7,6},{8,9},{11,10},{12,13},{15,14},{16,17},{19,... | collective-permute-start | bytes 393224 | tf_op jit(solution)/shard_map/ppermute | solution.py:68
  93.6 7.5 %collective-permute-start.53 = (bf16[32,2048]{1,0:T(8,128)(2,1)S(1)}, bf16[32,2048]{1,0:T(8,128)(2,1)S(1)}, u32[]{:S(2)}, u32[]{:S(2)}) collective-permute-start(bf16[32,2048]{1,0:T(8,128)(2,1)S(1)} %fusion.47), channel_id=1, source_target_pairs={{0,1},{3,2},{4,5},{7,6},{8,9},{11,10},{12,13},{15,14},{16,17},{19,... | collective-permute-start | bytes 393224 | tf_op jit(solution)/shard_map/ppermute | solution.py:68
  95.4 6.8 %collective-permute-start.33 = (bf16[32,2048]{1,0:T(8,128)(2,1)S(1)}, bf16[32,2048]{1,0:T(8,128)(2,1)S(1)}, u32[]{:S(2)}, u32[]{:S(2)}) collective-permute-start(bf16[32,2048]{1,0:T(8,128)(2,1)S(1)} %fusion.44), channel_id=1, source_target_pairs={{0,1},{3,2},{4,5},{7,6},{8,9},{11,10},{12,13},{15,14},{16,17},{19,... | collective-permute-start | bytes 393224 | tf_op jit(solution)/shard_map/ppermute | solution.py:68
  96.8 8.3 %collective-permute-start.39 = (bf16[32,2048]{1,0:T(8,128)(2,1)S(1)}, bf16[32,2048]{1,0:T(8,128)(2,1)S(1)}, u32[]{:S(2)}, u32[]{:S(2)}) collective-permute-start(bf16[32,2048]{1,0:T(8,128)(2,1)S(1)} %fusion.45), channel_id=1, source_target_pairs={{0,1},{3,2},{4,5},{7,6},{8,9},{11,10},{12,13},{15,14},{16,17},{19,... | collective-permute-start | bytes 393224 | tf_op jit(solution)/shard_map/ppermute | solution.py:68
  98.1 9.8 %collective-permute-start.19 = (bf16[32,2048]{1,0:T(8,128)(2,1)S(1)}, bf16[32,2048]{1,0:T(8,128)(2,1)S(1)}, u32[]{:S(2)}, u32[]{:S(2)}) collective-permute-start(bf16[32,2048]{1,0:T(8,128)(2,1)S(1)} %fusion.42), channel_id=1, source_target_pairs={{0,1},{3,2},{4,5},{7,6},{8,9},{11,10},{12,13},{15,14},{16,17},{19,... | collective-permute-start | bytes 393224 | tf_op jit(solution)/shard_map/ppermute | solution.py:68
  99.4 10.8 %collective-permute-start.25 = (bf16[32,2048]{1,0:T(8,128)(2,1)S(1)}, bf16[32,2048]{1,0:T(8,128)(2,1)S(1)}, u32[]{:S(2)}, u32[]{:S(2)}) collective-permute-start(bf16[32,2048]{1,0:T(8,128)(2,1)S(1)} %fusion.43), channel_id=1, source_target_pairs={{0,1},{3,2},{4,5},{7,6},{8,9},{11,10},{12,13},{15,14},{16,17},{19,... | collective-permute-start | bytes 393224 | tf_op jit(solution)/shard_map/ppermute | solution.py:68
  101.1 9.9 %collective-permute-start.48 = (bf16[32,2048]{1,0:T(8,128)(2,1)S(1)}, bf16[32,2048]{1,0:T(8,128)(2,1)S(1)}, u32[]{:S(2)}, u32[]{:S(2)}) collective-permute-start(bf16[32,2048]{1,0:T(8,128)(2,1)S(1)} %fusion.70), channel_id=1, source_target_pairs={{1,2},{2,1},{5,6},{6,5},{9,10},{10,9},{13,14},{14,13},{17,18},{18,... | collective-permute-start | bytes 393224 | tf_op jit(solution)/shard_map/ppermute | solution.py:68
  102.2 9.6 %collective-permute-start.54 = (bf16[32,2048]{1,0:T(8,128)(2,1)S(1)}, bf16[32,2048]{1,0:T(8,128)(2,1)S(1)}, u32[]{:S(2)}, u32[]{:S(2)}) collective-permute-start(bf16[32,2048]{1,0:T(8,128)(2,1)S(1)} %fusion.71), channel_id=1, source_target_pairs={{1,2},{2,1},{5,6},{6,5},{9,10},{10,9},{13,14},{14,13},{17,18},{18,... | collective-permute-start | bytes 393224 | tf_op jit(solution)/shard_map/ppermute | solution.py:68
  105.0 8.2 %collective-permute-start.34 = (bf16[32,2048]{1,0:T(8,128)(2,1)S(1)}, bf16[32,2048]{1,0:T(8,128)(2,1)S(1)}, u32[]{:S(2)}, u32[]{:S(2)}) collective-permute-start(bf16[32,2048]{1,0:T(8,128)(2,1)S(1)} %fusion.68), channel_id=1, source_target_pairs={{1,2},{2,1},{5,6},{6,5},{9,10},{10,9},{13,14},{14,13},{17,18},{18,... | collective-permute-start | bytes 393224 | tf_op jit(solution)/shard_map/ppermute | solution.py:68
  107.8 6.8 %collective-permute-start.40 = (bf16[32,2048]{1,0:T(8,128)(2,1)S(1)}, bf16[32,2048]{1,0:T(8,128)(2,1)S(1)}, u32[]{:S(2)}, u32[]{:S(2)}) collective-permute-start(bf16[32,2048]{1,0:T(8,128)(2,1)S(1)} %fusion.69), channel_id=1, source_target_pairs={{1,2},{2,1},{5,6},{6,5},{9,10},{10,9},{13,14},{14,13},{17,18},{18,... | collective-permute-start | bytes 393224 | tf_op jit(solution)/shard_map/ppermute | solution.py:68
  110.2 5.8 %collective-permute-start.20 = (bf16[32,2048]{1,0:T(8,128)(2,1)S(1)}, bf16[32,2048]{1,0:T(8,128)(2,1)S(1)}, u32[]{:S(2)}, u32[]{:S(2)}) collective-permute-start(bf16[32,2048]{1,0:T(8,128)(2,1)S(1)} %fusion.66), channel_id=1, source_target_pairs={{1,2},{2,1},{5,6},{6,5},{9,10},{10,9},{13,14},{14,13},{17,18},{18,... | collective-permute-start | bytes 393224 | tf_op jit(solution)/shard_map/ppermute | solution.py:68
  111.0 6.4 %collective-permute-start.26 = (bf16[32,2048]{1,0:T(8,128)(2,1)S(1)}, bf16[32,2048]{1,0:T(8,128)(2,1)S(1)}, u32[]{:S(2)}, u32[]{:S(2)}) collective-permute-start(bf16[32,2048]{1,0:T(8,128)(2,1)S(1)} %fusion.67), channel_id=1, source_target_pairs={{1,2},{2,1},{5,6},{6,5},{9,10},{10,9},{13,14},{14,13},{17,18},{18,... | collective-permute-start | bytes 393224 | tf_op jit(solution)/shard_map/ppermute | solution.py:68
  111.8 14.2 %collective-permute-start.49 = (bf16[32,2048]{1,0:T(8,128)(2,1)S(1)}, bf16[32,2048]{1,0:T(8,128)(2,1)S(1)}, u32[]{:S(2)}, u32[]{:S(2)}) collective-permute-start(bf16[32,2048]{1,0:T(8,128)(2,1)S(1)} %add_convert_fusion.1), channel_id=1, source_target_pairs={{1,0},{2,3},{5,4},{6,7},{9,8},{10,11},{13,12},{14,15},{17,16},{18,... | collective-permute-start | bytes 393224 | tf_op jit(solution)/shard_map/ppermute | solution.py:68
  113.2 15.6 %collective-permute-start.55 = (bf16[32,2048]{1,0:T(8,128)(2,1)S(1)}, bf16[32,2048]{1,0:T(8,128)(2,1)S(1)}, u32[]{:S(2)}, u32[]{:S(2)}) collective-permute-start(bf16[32,2048]{1,0:T(8,128)(2,1)S(1)} %add_convert_fusion), channel_id=1, source_target_pairs={{1,0},{2,3},{5,4},{6,7},{9,8},{10,11},{13,12},{14,15},{17,16},{18,... | collective-permute-start | bytes 393224 | tf_op jit(solution)/shard_map/ppermute | solution.py:68
  114.6 17.0 %collective-permute-start.35 = (bf16[32,2048]{1,0:T(8,128)(2,1)S(1)}, bf16[32,2048]{1,0:T(8,128)(2,1)S(1)}, u32[]{:S(2)}, u32[]{:S(2)}) collective-permute-start(bf16[32,2048]{1,0:T(8,128)(2,1)S(1)} %add_convert_fusion.3), channel_id=1, source_target_pairs={{1,0},{2,3},{5,4},{6,7},{9,8},{10,11},{13,12},{14,15},{17,16},{18,... | collective-permute-start | bytes 393224 | tf_op jit(solution)/shard_map/ppermute | solution.py:68
  116.0 18.4 %collective-permute-start.41 = (bf16[32,2048]{1,0:T(8,128)(2,1)S(1)}, bf16[32,2048]{1,0:T(8,128)(2,1)S(1)}, u32[]{:S(2)}, u32[]{:S(2)}) collective-permute-start(bf16[32,2048]{1,0:T(8,128)(2,1)S(1)} %add_convert_fusion.2), channel_id=1, source_target_pairs={{1,0},{2,3},{5,4},{6,7},{9,8},{10,11},{13,12},{14,15},{17,16},{18,... | collective-permute-start | bytes 393224 | tf_op jit(solution)/shard_map/ppermute | solution.py:68
  117.5 18.5 %collective-permute-start.21 = (bf16[32,2048]{1,0:T(8,128)(2,1)S(1)}, bf16[32,2048]{1,0:T(8,128)(2,1)S(1)}, u32[]{:S(2)}, u32[]{:S(2)}) collective-permute-start(bf16[32,2048]{1,0:T(8,128)(2,1)S(1)} %add_convert_fusion.5), channel_id=1, source_target_pairs={{1,0},{2,3},{5,4},{6,7},{9,8},{10,11},{13,12},{14,15},{17,16},{18,... | collective-permute-start | bytes 393224 | tf_op jit(solution)/shard_map/ppermute | solution.py:68
  126.0 11.4 %collective-permute-start.27 = (bf16[32,2048]{1,0:T(8,128)(2,1)S(1)}, bf16[32,2048]{1,0:T(8,128)(2,1)S(1)}, u32[]{:S(2)}, u32[]{:S(2)}) collective-permute-start(bf16[32,2048]{1,0:T(8,128)(2,1)S(1)} %add_convert_fusion.4), channel_id=1, source_target_pairs={{1,0},{2,3},{5,4},{6,7},{9,8},{10,11},{13,12},{14,15},{17,16},{18,... | collective-permute-start | bytes 393224 | tf_op jit(solution)/shard_map/ppermute | solution.py:68

commit v2 on v0

v2 whole, which is shorter than its diff:
```python
import jax
import jax.numpy as jnp
from jax import lax
from jax.sharding import PartitionSpec as P

STEPS = 6
F32 = jnp.float32
BF16 = jnp.bfloat16


def from_behind(block, axis, distance):
    devices = range(lax.axis_size(axis))
    route = [((i - distance) % len(devices), i) for i in devices]
    return lax.ppermute(block, axis, route)


def contract(left, right):
    return lax.dot_general(
        left, right, (((1,), (1,)), ((), ())), preferred_element_type=F32
    )


def rows_dot(left, right):
    return jnp.dot(left, right, preferred_element_type=F32)


def activations(tokens, cotangent, gate, upper, down):
    gate_sum = contract(gate, tokens)
    up_sum = contract(upper, tokens)
    squash = jax.nn.sigmoid(gate_sum)
    activated = gate_sum * squash
    hidden = (activated * up_sum).astype(BF16)
    backward = contract(down, cotangent)
    gate_back = (backward * up_sum * squash * (1.0 + gate_sum * (1.0 - squash))).astype(
        BF16
    )
    up_back = (backward * activated).astype(BF16)
    return gate_back, up_back, hidden


def ring(tokens, cotangent, gate_weight, up_weight, down_weight):
    held = jnp.stack([gate_weight, up_weight, down_weight])
    summed = None
    for position in range(STEPS):
        if position > 0:
            held = from_behind(held, "section", 1)
        parts = activations(tokens, cotangent, held[0], held[1], held[2])
        piece = jnp.stack(
            [
                rows_dot(parts[0], tokens),
                rows_dot(parts[1], tokens),
                rows_dot(parts[2], cotangent),
            ]
        )
        if position > 0:
            summed = from_behind(summed, "section", 1) + piece
        else:
            summed = piece
    finished = lax.psum(summed, "dp").astype(BF16)
    return (finished[0], finished[1], finished[2])


def hop(block, step, only=None):
    route = [(i, i ^ step(i)) for i in range(8) if only is None or i % 2 == only]
    return lax.ppermute(block, "section", route)


def along(block, route):
    return lax.ppermute(block, "dp", route)


CORE, X, Y = 1, 2, 4
PAIRS = [(0, 1), (1, 0), (2, 3), (3, 2)]
ACROSS = [(0, 3), (3, 0), (1, 2), (2, 1)]


def after(value, *others):
    return lax.optimization_barrier((value, others))[0]


def square(tokens, cotangent, gate_weight, up_weight, down_weight):
    section = lax.axis_index("section")
    core = section % 2
    chip = section // 2
    line = lax.axis_index("dp")
    block = gate_weight.shape[0]
    half = block // 2
    tok = tokens.shape[0]
    first = core == 0
    even = chip % 2 == 0
    keep_low = jnp.logical_or(line == 0, line == 3)

    def spread(own):
        v = [(i, i ^ (Y | CORE if i % 4 == 2 else CORE)) for i in range(8)]
        u = [
            (i, i ^ (X | CORE if i % 2 else (Y | CORE if i % 4 == 0 else CORE)))
            for i in range(8)
        ]
        return lax.ppermute(own, "section", v), lax.ppermute(own, "section", u)

    def other(i):
        return Y if i % 2 == 0 else X

    gu = jnp.stack([gate_weight, up_weight]).reshape(2 * block, -1)
    gu_v, gu_u = spread(gu)
    tokens_in = hop(after(tokens, gu), lambda i: CORE)
    dn_v, dn_u = spread(after(down_weight, gu))
    cotangent_in = hop(after(cotangent, gu), lambda i: CORE)
    gu_s = hop(gu_v, other)
    dn_s = hop(dn_v, other)

    tokens2 = jnp.concatenate([tokens, tokens_in])
    cotangent2 = jnp.concatenate([cotangent, cotangent_in])

    swapped = jnp.logical_and(core == 1, chip % 2 == 1)
    next_chip = jnp.where(first, chip ^ 1, chip ^ 2)
    sections = jnp.concatenate(
        [jnp.full((1, tok), section), jnp.full((1, tok), section ^ 1)], axis=1
    )

    def forward_half(weights, holder):
        sums = contract(weights, tokens2)
        gate_sum, up_sum = sums[:block], sums[block:]
        squash = jax.nn.sigmoid(gate_sum)
        activated = gate_sum * squash
        meets = (sections - (2 * holder + 1 - core)) % 8 < STEPS
        hidden = jnp.where(meets, activated * up_sum, 0).astype(BF16)
        slope = up_sum * squash * (1.0 + gate_sum * (1.0 - squash))
        return hidden, jnp.where(meets, slope, 0), jnp.where(meets, activated, 0)

    def backward_half(weights, found):
        backward = contract(weights, cotangent2)
        return jnp.concatenate(
            [(backward * found[1]).astype(BF16), (backward * found[2]).astype(BF16)]
        )

    def spots(v, u, e):
        z = jnp.where(first, e, v)
        return jnp.concatenate([jnp.where(even, z, u), jnp.where(even, u, z)])

    fv = forward_half(gu_v, jnp.where(swapped, next_chip, chip))
    fu = forward_half(gu_u, jnp.where(swapped, chip, next_chip))
    gu_e = hop(after(gu_u, fv), lambda i: Y, 0)
    down_p = hop(rows_dot(fv[0], cotangent2).astype(BF16), lambda i: X, 0)
    bv = backward_half(dn_v, fv)
    bu = backward_half(dn_u, fu)
    dn_e = hop(after(dn_u, bv), lambda i: Y, 0)
    both_p = hop(rows_dot(bv, tokens2).astype(BF16), lambda i: X, 0)

    fs = forward_half(gu_s, jnp.where(first, chip ^ 2, (chip + 3) % 4))
    down_q = hop(rows_dot(fs[0], cotangent2).astype(BF16), lambda i: X)
    bs = backward_half(dn_s, fs)
    sums_q = rows_dot(bs, tokens2).astype(BF16)
    gate_q = hop(sums_q[:block], lambda i: X)
    up_q = hop(sums_q[block:], lambda i: X)

    fe = forward_half(gu_e, chip ^ 3)
    down_r = rows_dot(spots(fv[0], fu[0], fe[0]), cotangent2)
    be = backward_half(dn_e, fe)
    both_r = rows_dot(spots(bv, bu, be), tokens2)

    def reduced(p, q, leaving, staying):
        p, q = p.astype(F32), q.astype(F32)
        leaving = leaving + jnp.where(even, q, p)
        r = hop(leaving.astype(BF16), lambda i: Y)
        total = staying + jnp.where(even, p, q) + r.astype(F32)
        low, high = total[:half], total[half:]
        other = along(jnp.where(keep_low, high, low).astype(BF16), PAIRS)
        kept = jnp.where(keep_low, low, high) + other.astype(F32)
        kept = lax.reduce_precision(kept, 8, 7)
        done = (kept + along(kept.astype(BF16), ACROSS).astype(F32)).astype(BF16)
        back = along(done, PAIRS)
        return jnp.concatenate(
            [jnp.where(keep_low, done, back), jnp.where(keep_low, back, done)]
        )

    grad_down = reduced(down_p, down_q, down_r[:block], down_r[block:])
    part = [both_r[at * block : (at + 1) * block] for at in range(4)]
    grad_gate = reduced(both_p[:block], gate_q, part[0], part[2])
    grad_up = reduced(both_p[block:], up_q, part[1], part[3])
    return grad_gate, grad_up, grad_down


def solution(mesh):
    fits = mesh.shape["section"] == 8 and mesh.shape["dp"] == 4
    return jax.shard_map(
        square if fits else ring,
        mesh=mesh,
        in_specs=(
            P(("section", "dp"), None),
            P(("section", "dp"), None),
            P("section", None),
            P("section", None),
            P("section", None),
        ),
        out_specs=(P("section", None), P("section", None), P("section", None)),
        check_vma=False,
    )
```

time: 194 us -> 94.1 us (0.49)
  waiting for transfers between devices: 109 us -> 20.6 us
  blocking collectives: 58.6 us -> 0 us
  starting transfers between devices: 3.58 us -> 44.2 us
  local copies, waits for them, and re-layouts: 2.06 us -> 7.95 us
  other arithmetic: 2.27 us -> 5.4 us
  matrix products: 17.5 us -> 14.5 us
    ppermute x10 -> x27, waiting for transfers between devices: 109 us -> 20.6 us  [the longest x9 12.7 us: along(): return lax.ppermute(block, 'dp', route)]
    psum x1 -> x0, blocking collectives: 58.6 us -> none  [per_device(): finished = lax.psum(summed, 'dp').astype(jnp.bfloat16)]
    ppermute x10 -> x27, starting transfers between devices: 3.58 us -> 44.2 us  [the longest x14 26.1 us: hop(): return lax.ppermute(block, 'section', route)]
    concatenate x0 -> x2, local copies, waits for them, and re-layouts: none -> 4.4 us  [the longest x1 2.7 us: square(): tokens2 = jnp.concatenate([tokens, tokens_in])]
    unnamed x10 -> x6, local copies, waits for them, and re-layouts: 0.06 us -> 3.51 us
    dot_general x18 -> x6, matrix products: 6.95 us -> 4.06 us  [rows_dot(): return jnp.dot(left, right, preferred_element_type=F32)]
    concatenate x0 -> x3, other arithmetic: none -> 2.16 us  [reduced(): jnp.concatenate([jnp.where(keep_low, done, back), jnp.where(keep_low, bac...]
    squeeze x1 -> x0, local copies, waits for them, and re-layouts: 2 us -> none  [per_device(): return (finished[0], finished[1], finished[2])]
  transfers between devices with their start and end apart: 10 -> 27, of which waited for: 10 -> 10; matrix products, arithmetic and copies ran while one was open for 9% -> 26% of each run, Pallas kernels for 0% -> 0%
where the time goes in v2:
time: 94.1 us; the launch traced here: 93.7 us
  starting transfers between devices  44.2 us (47%)
  waiting for transfers between devices  20.6 us (22%)
  matrix products  14.5 us (15%)
  local copies, waits for them, and re-layouts  7.95 us (8%)
  other arithmetic  5.4 us (6%)
  between operations  1.06 us (1%)
    ppermute x14, starting transfers between devices, hop(): return lax.ppermute(block, 'section', route)  26.1 us
    ppermute x9, starting transfers between devices, along(): return lax.ppermute(block, 'dp', route)  14.3 us
    ppermute x9, waiting for transfers between devices, along(): return lax.ppermute(block, 'dp', route)  12.7 us
    dot_general x8, matrix products, contract(): lax.dot_general(left, right, (((1,), (1,)), ((), ())), preferred_element_...  10.5 us
    ppermute x14, waiting for transfers between devices, hop(): return lax.ppermute(block, 'section', route)  6.66 us
    dot_general x6, matrix products, rows_dot(): return jnp.dot(left, right, preferred_element_type=F32)  4.06 us
    ppermute x4, starting transfers between devices, spread(): return (lax.ppermute(own, 'section', v), lax.ppermute(own, 'section', u))  3.79 us
    unnamed x6, local copies, waits for them, and re-layouts  3.51 us
  transfers between devices with their start and end apart: 27, of which 10 were waited for; matrix products, arithmetic and copies ran while one was open for 26% of the time, Pallas kernels for 0%

profile of v2, /device:TPU:0, one launch (start us, length us, event | category | flops | bytes accessed | tf_op | source)
XLA Modules:
  0.0 93.7 jit_solution(17622969214047181899)
XLA Ops:
  0.6 2.0 %pad_maximum_fusion = bf16[2,32,4096]{2,1,0:T(8,128)(2,1)} fusion(bf16[1,32,4096]{2,1,0:T(8,128)(2,1)} %bitcast.26, bf16[1,32,4096]{2,1,0:T(8,128)(2,1)} %bitcast.27), kind=kLoop, calls=%fused_computation.22 | loop fusion | flops 262144 | bytes 1048576 | tf_op jit(solution)/shard_map/stack | solution.py:104
  2.6 0.5 collective-permute-start.4
  3.2 0.5 collective-permute-start.1
  3.6 2.6 %collective-permute-start = (bf16[32,4096]{1,0:T(8,128)(2,1)}, bf16[32,4096]{1,0:T(8,128)(2,1)S(1)}, u32[]{:S(2)}, u32[]{:S(2)}) collective-permute-start(bf16[32,4096]{1,0:T(8,128)(2,1)} %param.9), channel_id=1, source_target_pairs={{0,20},{4,8},{8,12},{12,0},{16,4},{20,24},{24,28},{28,16},{1,21},{... | collective-permute-start | bytes 786440 | tf_op jit(solution)/shard_map/ppermute | solution.py:99
  6.2 1.1 %collective-permute-start.2 = (bf16[192,4096]{1,0:T(8,128)(2,1)}, bf16[192,4096]{1,0:T(8,128)(2,1)}, u32[]{:S(2)}, u32[]{:S(2)}) collective-permute-start(bf16[192,4096]{1,0:T(8,128)(2,1)} %param.6), channel_id=1, source_target_pairs={{0,4},{4,0},{8,12},{12,8},{16,20},{20,16},{24,28},{28,24},{1,5},{5... | collective-permute-start | bytes 4718600 | tf_op jit(solution)/shard_map/ppermute | solution.py:65
  7.4 2.7 %constant_dynamic-update-slice_fusion.3 = bf16[384,4096]{1,0:T(8,128)(2,1)} fusion(bf16[192,4096]{1,0:T(8,128)(2,1)} %param.5), kind=kLoop, calls=%fused_computation.87 | loop fusion | bytes 3145728
  10.1 0.1 constant_dynamic-update-slice_fusion.1
  10.3 1.2 %collective-permute-done = bf16[32,4096]{1,0:T(8,128)(2,1)S(1)} collective-permute-done((bf16[32,4096]{1,0:T(8,128)(2,1)}, bf16[32,4096]{1,0:T(8,128)(2,1)S(1)}, u32[]{:S(2)}, u32[]{:S(2)}) %collective-permute-start) | collective-permute-done | bytes 262176 | tf_op jit(solution)/shard_map/ppermute | solution.py:99
  11.6 0.6 collective-permute-start.6
  12.2 2.3 %collective-permute-start.5 = (bf16[32,4096]{1,0:T(8,128)(2,1)S(1)}, bf16[32,4096]{1,0:T(8,128)(2,1)S(1)}, u32[]{:S(2)}, u32[]{:S(2)}) collective-permute-start(bf16[32,4096]{1,0:T(8,128)(2,1)S(1)} %collective-permute-done), channel_id=1, source_target_pairs={{0,16},{8,24},{16,0},{24,8},{1,17},{9,25},{17,1},{25,9},{2,18},{10... | collective-permute-start | bytes 786440 | tf_op jit(solution)/shard_map/ppermute | solution.py:65
  14.5 1.7 %collective-permute-start.9 = (bf16[32,4096]{1,0:T(8,128)(2,1)}, bf16[32,4096]{1,0:T(8,128)(2,1)S(1)}, u32[]{:S(2)}, u32[]{:S(2)}) collective-permute-start(bf16[32,4096]{1,0:T(8,128)(2,1)} %collective-permute-done.1), channel_id=1, source_target_pairs={{0,16},{4,12},{8,24},{12,4},{16,0},{20,28},{24,8},{28,20},{1,17},{... | collective-permute-start | bytes 786440 | tf_op jit(solution)/shard_map/ppermute | solution.py:65
  16.3 0.4 collective-permute-start.10
  16.6 2.7 %constant_dynamic-update-slice_fusion.2 = bf16[384,4096]{1,0:T(8,128)(2,1)} fusion(bf16[384,4096]{1,0:T(8,128)(2,1)} %constant_dynamic-update-slice_fusion.3, bf16[192,4096]{1,0:T(8,128)(2,1)} %collective-permute-done.4), kind=kLoop, calls=%fused_computation.86 | loop fusion | bytes 3145728 | tf_op jit(solution)/shard_map/concatenate | solution.py:112
  19.4 1.7 %constant_dynamic-update-slice_fusion = bf16[384,4096]{1,0:T(8,128)(2,1)S(1)} fusion(bf16[384,4096]{1,0:T(8,128)(2,1)S(1)} %constant_dynamic-update-slice_fusion.1, bf16[192,4096]{1,0:T(8,128)(2,1)} %collective-permute-done.2), kind=kLoop, calls=%fused_computation.84 | loop fusion | bytes 3145728 | tf_op jit(solution)/shard_map/concatenate | solution.py:113
  21.1 0.6 copy-done
  21.7 2.1 %fusion.53 = f32[64,384]{1,0:T(8,128)S(1)} fusion(bf16[64,4096]{1,0:T(8,128)(2,1)} %collective-permute-done.3, bf16[384,4096]{1,0:T(8,128)(2,1)S(1)} %copy-done), kind=kOutput, calls=%fused_computation.125 | convolution fusion | flops 201326592 | bytes 3768320 | tf_op jit(solution)/shard_map/dot_general | solution.py:18
  23.8 2.0 %multiply_convert_fusion.6 = (bf16[32,384]{1,0:T(8,128)(2,1)S(1)}, bf16[32,384]{1,0:T(8,128)(2,1)S(1)}, bf16[32,384]{1,0:T(8,128)(2,1)S(1)}) fusion(f32[64,384]{1,0:T(8,128)S(1)} %fusion.53, pred[384]{0:T(512)(128)(4,1)S(1)} %get-tuple-element.41, bf16[32,4096]{1,0:T(8,128)(2,1)} %collective-permute-done.1, ...), kind=kOutput, calls=%fused_computation.71 | convolution fusion | flops 100884480 | bytes 3580288 | tf_op jit(solution)/shard_map/dot_general | solution.py:18
  25.8 3.5 %collective-permute-start.7 = (bf16[64,4096]{1,0:T(8,128)(2,1)S(1)}, bf16[64,4096]{1,0:T(8,128)(2,1)S(1)}, u32[]{:S(2)}, u32[]{:S(2)}) collective-permute-start(bf16[64,4096]{1,0:T(8,128)(2,1)S(1)} %collective-permute-done.6), channel_id=1, source_target_pairs={{0,16},{8,24},{16,0},{24,8},{1,17},{9,25},{17,1},{25,9},{2,18},{10... | collective-permute-start | bytes 1572872 | tf_op jit(solution)/shard_map/ppermute | solution.py:65
  29.4 0.7 convolution_convert_fusion.3
  30.1 6.7 %collective-permute-start.21 = (bf16[32,4096]{1,0:T(8,128)(2,1)S(1)}, bf16[32,4096]{1,0:T(8,128)(2,1)S(1)}, u32[]{:S(2)}, u32[]{:S(2)}) collective-permute-start(bf16[32,4096]{1,0:T(8,128)(2,1)S(1)} %convolution_convert_fusion.3), channel_id=1, source_target_pairs={{0,8},{8,0},{16,24},{24,16},{1,9},{9,1},{17,25},{25,17},{2,10},{10... | collective-permute-start | bytes 786440 | tf_op jit(solution)/shard_map/ppermute | solution.py:65
  36.8 1.1 %fusion.56 = f32[64,384]{1,0:T(8,128)S(1)} fusion(bf16[64,4096]{1,0:T(8,128)(2,1)S(1)} %collective-permute-done.10, bf16[384,4096]{1,0:T(8,128)(2,1)S(1)} %copy-done), kind=kOutput, calls=%fused_computation.128 | convolution fusion | flops 201326592 | bytes 3768320 | tf_op jit(solution)/shard_map/dot_general | solution.py:18
  37.9 0.6 convolution_convert_fusion.2
  38.6 0.7 convolution_convert_fusion.1
  39.3 4.1 %collective-permute-start.8 = (bf16[64,4096]{1,0:T(8,128)(2,1)S(1)}, bf16[64,4096]{1,0:T(8,128)(2,1)S(1)}, u32[]{:S(2)}, u32[]{:S(2)}) collective-permute-start(bf16[64,4096]{1,0:T(8,128)(2,1)S(1)} %convolution_convert_fusion.1), channel_id=1, source_target_pairs={{0,8},{8,0},{16,24},{24,16},{1,9},{9,1},{17,25},{25,17},{2,10},{10... | collective-permute-start | bytes 1572872 | tf_op jit(solution)/shard_map/ppermute | solution.py:65
  43.4 1.0 %multiply_convert_fusion.1 = (bf16[32,384]{1,0:T(8,128)(2,1)S(1)}, bf16[32,384]{1,0:T(8,128)(2,1)S(1)}) fusion(f32[64,384]{1,0:T(8,128)S(1)} %fusion.56, pred[384]{0:T(512)(128)(4,1)S(1)} %get-tuple-element.44, bf16[32,4096]{1,0:T(8,128)(2,1)S(1)} %collective-permute-done.9, bf16[384,4096]{1,0:T(8,128)(2,1)S(1)} %constant_dynamic-update-slice_fusion), kind=kOutput, calls=%fused_computation.59 | convolution fusion | flops 100847616 | bytes 3555712 | tf_op jit(solution)/shard_map/dot_general | solution.py:18
  44.4 0.7 convolution_convert_fusion
  45.1 1.1 %fusion.55 = f32[64,384]{1,0:T(8,128)S(1)} fusion(bf16[64,4096]{1,0:T(8,128)(2,1)S(1)} %collective-permute-done.6, bf16[384,4096]{1,0:T(8,128)(2,1)S(1)} %copy-done), kind=kOutput, calls=%fused_computation.127 | convolution fusion | flops 201326592 | bytes 3768320 | tf_op jit(solution)/shard_map/dot_general | solution.py:18
  46.2 1.0 %multiply_convert_fusion.3 = (bf16[32,384]{1,0:T(8,128)(2,1)S(1)}, bf16[32,384]{1,0:T(8,128)(2,1)S(1)}) fusion(f32[64,384]{1,0:T(8,128)S(1)} %fusion.55, pred[384]{0:T(512)(128)(4,1)S(1)} %get-tuple-element.42, bf16[32,4096]{1,0:T(8,128)(2,1)S(1)} %collective-permute-done, bf16[384,4096]{1,0:T(8,128)(2,1)S(1)} %constant_dynamic-update-slice_fusion), kind=kOutput, calls=%fused_computation.63 | convolution fusion | flops 100847616 | bytes 3555712 | tf_op jit(solution)/shard_map/dot_general | solution.py:18
  47.3 0.1 collective-permute-start.16
  47.4 1.1 %fusion.54 = f32[64,384]{1,0:T(8,128)S(1)} fusion(bf16[64,4096]{1,0:T(8,128)(2,1)S(1)} %collective-permute-done.7, bf16[384,4096]{1,0:T(8,128)(2,1)S(1)} %copy-done), kind=kOutput, calls=%fused_computation.126 | convolution fusion | flops 201326592 | bytes 3768320 | tf_op jit(solution)/shard_map/dot_general | solution.py:18
  48.5 0.7 fusion.19
  49.2 2.1 %collective-permute-start.11 = (bf16[32,4096]{1,0:T(8,128)(2,1)S(1)}, bf16[32,4096]{1,0:T(8,128)(2,1)S(1)}, u32[]{:S(2)}, u32[]{:S(2)}) collective-permute-start(bf16[32,4096]{1,0:T(8,128)(2,1)S(1)} %get-tuple-element.23), channel_id=1, source_target_pairs={{0,8},{4,12},{8,0},{12,4},{16,24},{20,28},{24,16},{28,20},{1,9},{5... | collective-permute-start | bytes 786440 | tf_op jit(solution)/shard_map/ppermute | solution.py:65
  51.3 0.1 fusion.11
  51.4 0.6 collective-permute-start.23
  52.0 1.0 %multiply_convert_fusion.5 = (bf16[32,384]{1,0:T(8,128)(2,1)S(1)}, bf16[32,384]{1,0:T(8,128)(2,1)S(1)}) fusion(f32[64,384]{1,0:T(8,128)S(1)} %fusion.54, pred[384]{0:T(512)(128)(4,1)S(1)} %get-tuple-element.43, bf16[32,4096]{1,0:T(8,128)(2,1)S(1)} %collective-permute-done.5, bf16[384,4096]{1,0:T(8,128)(2,1)S(1)} %constant_dynamic-update-slice_fusion), kind=kOutput, calls=%fused_computation.67 | convolution fusion | flops 100847616 | bytes 3555712 | tf_op jit(solution)/shard_map/dot_general | solution.py:18
  53.1 0.7 fusion.12
  53.8 4.2 %collective-permute-done.16 = bf16[32,4096]{1,0:T(8,128)(2,1)S(1)} collective-permute-done((bf16[32,4096]{1,0:T(8,128)(2,1)S(1)}, bf16[32,4096]{1,0:T(8,128)(2,1)S(1)}, u32[]{:S(2)}, u32[]{:S(2)}) %collective-permute-start.16) | collective-permute-done | bytes 262176 | tf_op jit(solution)/shard_map/ppermute | solution.py:65
  58.0 0.1 fusion.7
  58.1 1.5 %collective-permute-start.17 = (bf16[32,4096]{1,0:T(8,128)(2,1)S(1)}, bf16[32,4096]{1,0:T(8,128)(2,1)S(1)}, u32[]{:S(2)}, u32[]{:S(2)}) collective-permute-start(bf16[32,4096]{1,0:T(8,128)(2,1)S(1)} %fusion.7), channel_id=1, source_target_pairs={{0,16},{4,20},{8,24},{12,28},{16,0},{20,4},{24,8},{28,12},{1,17},{... | collective-permute-start | bytes 786440 | tf_op jit(solution)/shard_map/ppermute | solution.py:65
  59.6 0.1 fusion.9
  59.8 2.3 %collective-permute-start.24 = (bf16[16,4096]{1,0:T(8,128)(2,1)S(1)}, bf16[16,4096]{1,0:T(8,128)(2,1)S(1)}, u32[]{:S(2)}, u32[]{:S(2)}) collective-permute-start(bf16[16,4096]{1,0:T(8,128)(2,1)S(1)} %select_convert_fusion), channel_id=1, source_target_pairs={{0,1},{1,0},{2,3},{3,2},{4,5},{5,4},{6,7},{7,6},{8,9},{9,8},{10,11... | collective-permute-start | bytes 393224 | tf_op jit(solution)/shard_map/ppermute | solution.py:69
  62.1 2.4 %collective-permute-done.17 = bf16[32,4096]{1,0:T(8,128)(2,1)S(1)} collective-permute-done((bf16[32,4096]{1,0:T(8,128)(2,1)S(1)}, bf16[32,4096]{1,0:T(8,128)(2,1)S(1)}, u32[]{:S(2)}, u32[]{:S(2)}) %collective-permute-start.17) | collective-permute-done | bytes 262176 | tf_op jit(solution)/shard_map/ppermute | solution.py:65
  64.5 0.2 fusion.5
  64.8 1.6 %collective-permute-start.18 = (bf16[16,4096]{1,0:T(8,128)(2,1)S(1)}, bf16[16,4096]{1,0:T(8,128)(2,1)S(1)}, u32[]{:S(2)}, u32[]{:S(2)}) collective-permute-start(bf16[16,4096]{1,0:T(8,128)(2,1)S(1)} %select_convert_fusion.1), channel_id=1, source_target_pairs={{0,1},{1,0},{2,3},{3,2},{4,5},{5,4},{6,7},{7,6},{8,9},{9,8},{10,11... | collective-permute-start | bytes 393224 | tf_op jit(solution)/shard_map/ppermute | solution.py:69
  66.4 1.5 %collective-permute-start.12 = (bf16[32,4096]{1,0:T(8,128)(2,1)S(1)}, bf16[32,4096]{1,0:T(8,128)(2,1)S(1)}, u32[]{:S(2)}, u32[]{:S(2)}) collective-permute-start(bf16[32,4096]{1,0:T(8,128)(2,1)S(1)} %get-tuple-element.21), channel_id=1, source_target_pairs={{0,16},{4,20},{8,24},{12,28},{16,0},{20,4},{24,8},{28,12},{1,17},{... | collective-permute-start | bytes 786440 | tf_op jit(solution)/shard_map/ppermute | solution.py:65
  68.0 2.6 %collective-permute-start.25 = (bf16[16,4096]{1,0:T(8,128)(2,1)S(1)}, bf16[16,4096]{1,0:T(8,128)(2,1)S(1)}, u32[]{:S(2)}, u32[]{:S(2)}) collective-permute-start(bf16[16,4096]{1,0:T(8,128)(2,1)S(1)} %fusion.50), channel_id=1, source_target_pairs={{0,3},{3,0},{1,2},{2,1},{4,7},{7,4},{5,6},{6,5},{8,11},{11,8},{9,1... | collective-permute-start | bytes 393224 | tf_op jit(solution)/shard_map/ppermute | solution.py:69
  70.5 0.2 collective-permute-done.18
  70.8 3.5 %collective-permute-start.19 = (bf16[16,4096]{1,0:T(8,128)(2,1)S(1)}, bf16[16,4096]{1,0:T(8,128)(2,1)S(1)}, u32[]{:S(2)}, u32[]{:S(2)}) collective-permute-start(bf16[16,4096]{1,0:T(8,128)(2,1)S(1)} %fusion.49), channel_id=1, source_target_pairs={{0,3},{3,0},{1,2},{2,1},{4,7},{7,4},{5,6},{6,5},{8,11},{11,8},{9,1... | collective-permute-start | bytes 393224 | tf_op jit(solution)/shard_map/ppermute | solution.py:69
  74.3 0.1 fusion.1
  74.5 0.3 collective-permute-start.13
  74.8 0.7 collective-permute-done.25
  75.5 0.1 add_convert_fusion
  75.6 1.4 %collective-permute-start.26 = (bf16[16,4096]{1,0:T(8,128)(2,1)S(1)}, bf16[16,4096]{1,0:T(8,128)(2,1)S(1)}, u32[]{:S(2)}, u32[]{:S(2)}) collective-permute-start(bf16[16,4096]{1,0:T(8,128)(2,1)S(1)} %add_convert_fusion), channel_id=1, source_target_pairs={{0,1},{1,0},{2,3},{3,2},{4,5},{5,4},{6,7},{7,6},{8,9},{9,8},{10,11... | collective-permute-start | bytes 393224 | tf_op jit(solution)/shard_map/ppermute | solution.py:69
  77.0 1.9 %collective-permute-done.19 = bf16[16,4096]{1,0:T(8,128)(2,1)S(1)} collective-permute-done((bf16[16,4096]{1,0:T(8,128)(2,1)S(1)}, bf16[16,4096]{1,0:T(8,128)(2,1)S(1)}, u32[]{:S(2)}, u32[]{:S(2)}) %collective-permute-start.19) | collective-permute-done | bytes 131104 | tf_op jit(solution)/shard_map/ppermute | solution.py:69
  78.9 0.1 add_convert_fusion.1
  79.0 0.8 collective-permute-start.20
  79.8 1.2 %collective-permute-done.13 = bf16[16,4096]{1,0:T(8,128)(2,1)S(1)} collective-permute-done((bf16[16,4096]{1,0:T(8,128)(2,1)S(1)}, bf16[16,4096]{1,0:T(8,128)(2,1)S(1)}, u32[]{:S(2)}, u32[]{:S(2)}) %collective-permute-start.13) | collective-permute-done | bytes 131104 | tf_op jit(solution)/shard_map/ppermute | solution.py:69
  81.0 1.7 %collective-permute-start.14 = (bf16[16,4096]{1,0:T(8,128)(2,1)S(1)}, bf16[16,4096]{1,0:T(8,128)(2,1)S(1)}, u32[]{:S(2)}, u32[]{:S(2)}) collective-permute-start(bf16[16,4096]{1,0:T(8,128)(2,1)S(1)} %fusion.48), channel_id=1, source_target_pairs={{0,3},{3,0},{1,2},{2,1},{4,7},{7,4},{5,6},{6,5},{8,11},{11,8},{9,1... | collective-permute-start | bytes 393224 | tf_op jit(solution)/shard_map/ppermute | solution.py:69
  82.8 1.2 %collective-permute-done.20 = bf16[16,4096]{1,0:T(8,128)(2,1)S(1)} collective-permute-done((bf16[16,4096]{1,0:T(8,128)(2,1)S(1)}, bf16[16,4096]{1,0:T(8,128)(2,1)S(1)}, u32[]{:S(2)}, u32[]{:S(2)}) %collective-permute-start.20) | collective-permute-done | bytes 131104 | tf_op jit(solution)/shard_map/ppermute | solution.py:69
  84.0 0.7 pad_maximum_fusion.3
  84.7 3.2 %collective-permute-done.14 = bf16[16,4096]{1,0:T(8,128)(2,1)S(1)} collective-permute-done((bf16[16,4096]{1,0:T(8,128)(2,1)S(1)}, bf16[16,4096]{1,0:T(8,128)(2,1)S(1)}, u32[]{:S(2)}, u32[]{:S(2)}) %collective-permute-start.14) | collective-permute-done | bytes 131104 | tf_op jit(solution)/shard_map/ppermute | solution.py:69
  88.0 0.7 pad_maximum_fusion.2
  88.8 4.2 %collective-permute-done.15 = bf16[16,4096]{1,0:T(8,128)(2,1)S(1)} collective-permute-done((bf16[16,4096]{1,0:T(8,128)(2,1)S(1)}, bf16[16,4096]{1,0:T(8,128)(2,1)S(1)}, u32[]{:S(2)}, u32[]{:S(2)}) %collective-permute-start.15) | collective-permute-done | bytes 131104 | tf_op jit(solution)/shard_map/ppermute | solution.py:69
  93.0 0.7 pad_maximum_fusion.1
  (39 shorter events, 0.7 us)
Async XLA Ops:
  0.6 9.5 %copy-start.1 = (bf16[192,4096]{1,0:T(8,128)(2,1)S(1)}, bf16[192,4096]{1,0:T(8,128)(2,1)}, u32[]{:S(2)}) copy-start(bf16[192,4096]{1,0:T(8,128)(2,1)} %param.6) | copy-start | bytes 4718596
  2.6 13.6 %collective-permute-start.4 = (bf16[192,4096]{1,0:T(8,128)(2,1)}, bf16[192,4096]{1,0:T(8,128)(2,1)}, u32[]{:S(2)}, u32[]{:S(2)}) collective-permute-start(bf16[192,4096]{1,0:T(8,128)(2,1)} %param.5), channel_id=1, source_target_pairs={{0,4},{4,0},{8,12},{12,8},{16,20},{20,16},{24,28},{28,24},{1,5},{5... | collective-permute-start | bytes 4718600 | tf_op jit(solution)/shard_map/ppermute | solution.py:65
  3.1 11.4 %collective-permute-start.3 = (bf16[64,4096]{1,0:T(8,128)(2,1)}, bf16[64,4096]{1,0:T(8,128)(2,1)}, u32[]{:S(2)}, u32[]{:S(2)}) collective-permute-start(bf16[64,4096]{1,0:T(8,128)(2,1)} %bitcast.2), channel_id=1, source_target_pairs={{0,4},{4,0},{8,28},{12,8},{16,20},{20,16},{24,12},{28,24},{1,5},{5... | collective-permute-start | bytes 1572872 | tf_op jit(solution)/shard_map/ppermute | solution.py:99
  3.2 9.1 %collective-permute-start.1 = (bf16[32,4096]{1,0:T(8,128)(2,1)}, bf16[32,4096]{1,0:T(8,128)(2,1)}, u32[]{:S(2)}, u32[]{:S(2)}) collective-permute-start(bf16[32,4096]{1,0:T(8,128)(2,1)} %param.9), channel_id=1, source_target_pairs={{0,4},{4,0},{8,28},{12,8},{16,20},{20,16},{24,12},{28,24},{1,5},{5... | collective-permute-start | bytes 786440 | tf_op jit(solution)/shard_map/ppermute | solution.py:99
  3.6 8.0 %collective-permute-start = (bf16[32,4096]{1,0:T(8,128)(2,1)}, bf16[32,4096]{1,0:T(8,128)(2,1)S(1)}, u32[]{:S(2)}, u32[]{:S(2)}) collective-permute-start(bf16[32,4096]{1,0:T(8,128)(2,1)} %param.9), channel_id=1, source_target_pairs={{0,20},{4,8},{8,12},{12,0},{16,4},{20,24},{24,28},{28,16},{1,21},{... | collective-permute-start | bytes 786440 | tf_op jit(solution)/shard_map/ppermute | solution.py:99
  6.2 13.1 %collective-permute-start.2 = (bf16[192,4096]{1,0:T(8,128)(2,1)}, bf16[192,4096]{1,0:T(8,128)(2,1)}, u32[]{:S(2)}, u32[]{:S(2)}) collective-permute-start(bf16[192,4096]{1,0:T(8,128)(2,1)} %param.6), channel_id=1, source_target_pairs={{0,4},{4,0},{8,12},{12,8},{16,20},{20,16},{24,28},{28,24},{1,5},{5... | collective-permute-start | bytes 4718600 | tf_op jit(solution)/shard_map/ppermute | solution.py:65
  11.6 14.2 %collective-permute-start.6 = (bf16[64,4096]{1,0:T(8,128)(2,1)}, bf16[64,4096]{1,0:T(8,128)(2,1)S(1)}, u32[]{:S(2)}, u32[]{:S(2)}) collective-permute-start(bf16[64,4096]{1,0:T(8,128)(2,1)} %bitcast.2), channel_id=1, source_target_pairs={{0,20},{4,8},{8,12},{12,0},{16,4},{20,24},{24,28},{28,16},{1,21},{... | collective-permute-start | bytes 1572872 | tf_op jit(solution)/shard_map/ppermute | solution.py:99
  12.2 39.7 %collective-permute-start.5 = (bf16[32,4096]{1,0:T(8,128)(2,1)S(1)}, bf16[32,4096]{1,0:T(8,128)(2,1)S(1)}, u32[]{:S(2)}, u32[]{:S(2)}) collective-permute-start(bf16[32,4096]{1,0:T(8,128)(2,1)S(1)} %collective-permute-done), channel_id=1, source_target_pairs={{0,16},{8,24},{16,0},{24,8},{1,17},{9,25},{17,1},{25,9},{2,18},{10... | collective-permute-start | bytes 786440 | tf_op jit(solution)/shard_map/ppermute | solution.py:65
  14.5 24.7 %collective-permute-start.9 = (bf16[32,4096]{1,0:T(8,128)(2,1)}, bf16[32,4096]{1,0:T(8,128)(2,1)S(1)}, u32[]{:S(2)}, u32[]{:S(2)}) collective-permute-start(bf16[32,4096]{1,0:T(8,128)(2,1)} %collective-permute-done.1), channel_id=1, source_target_pairs={{0,16},{4,12},{8,24},{12,4},{16,0},{20,28},{24,8},{28,20},{1,17},{... | collective-permute-start | bytes 786440 | tf_op jit(solution)/shard_map/ppermute | solution.py:65
  16.3 20.5 %collective-permute-start.10 = (bf16[64,4096]{1,0:T(8,128)(2,1)}, bf16[64,4096]{1,0:T(8,128)(2,1)S(1)}, u32[]{:S(2)}, u32[]{:S(2)}) collective-permute-start(bf16[64,4096]{1,0:T(8,128)(2,1)} %collective-permute-done.3), channel_id=1, source_target_pairs={{0,16},{4,12},{8,24},{12,4},{16,0},{20,28},{24,8},{28,20},{1,17},{... | collective-permute-start | bytes 1572872 | tf_op jit(solution)/shard_map/ppermute | solution.py:65
  19.3 2.4 %copy-start = (bf16[384,4096]{1,0:T(8,128)(2,1)S(1)}, bf16[384,4096]{1,0:T(8,128)(2,1)}, u32[]{:S(2)}) copy-start(bf16[384,4096]{1,0:T(8,128)(2,1)} %constant_dynamic-update-slice_fusion.2) | copy-start | bytes 9437188
  25.8 21.4 %collective-permute-start.7 = (bf16[64,4096]{1,0:T(8,128)(2,1)S(1)}, bf16[64,4096]{1,0:T(8,128)(2,1)S(1)}, u32[]{:S(2)}, u32[]{:S(2)}) collective-permute-start(bf16[64,4096]{1,0:T(8,128)(2,1)S(1)} %collective-permute-done.6), channel_id=1, source_target_pairs={{0,16},{8,24},{16,0},{24,8},{1,17},{9,25},{17,1},{25,9},{2,18},{10... | collective-permute-start | bytes 1572872 | tf_op jit(solution)/shard_map/ppermute | solution.py:65
  30.1 19.2 %collective-permute-start.21 = (bf16[32,4096]{1,0:T(8,128)(2,1)S(1)}, bf16[32,4096]{1,0:T(8,128)(2,1)S(1)}, u32[]{:S(2)}, u32[]{:S(2)}) collective-permute-start(bf16[32,4096]{1,0:T(8,128)(2,1)S(1)} %convolution_convert_fusion.3), channel_id=1, source_target_pairs={{0,8},{8,0},{16,24},{24,16},{1,9},{9,1},{17,25},{25,17},{2,10},{10... | collective-permute-start | bytes 786440 | tf_op jit(solution)/shard_map/ppermute | solution.py:65
  38.5 12.8 %collective-permute-start.22 = (bf16[32,4096]{1,0:T(8,128)(2,1)S(1)}, bf16[32,4096]{1,0:T(8,128)(2,1)S(1)}, u32[]{:S(2)}, u32[]{:S(2)}) collective-permute-start(bf16[32,4096]{1,0:T(8,128)(2,1)S(1)} %convolution_convert_fusion.2), channel_id=1, source_target_pairs={{0,8},{4,12},{8,0},{12,4},{16,24},{20,28},{24,16},{28,20},{1,9},{5... | collective-permute-start | bytes 786440 | tf_op jit(solution)/shard_map/ppermute | solution.py:65
  39.3 18.7 %collective-permute-start.8 = (bf16[64,4096]{1,0:T(8,128)(2,1)S(1)}, bf16[64,4096]{1,0:T(8,128)(2,1)S(1)}, u32[]{:S(2)}, u32[]{:S(2)}) collective-permute-start(bf16[64,4096]{1,0:T(8,128)(2,1)S(1)} %convolution_convert_fusion.1), channel_id=1, source_target_pairs={{0,8},{8,0},{16,24},{24,16},{1,9},{9,1},{17,25},{25,17},{2,10},{10... | collective-permute-start | bytes 1572872 | tf_op jit(solution)/shard_map/ppermute | solution.py:65
  47.3 10.7 %collective-permute-start.16 = (bf16[32,4096]{1,0:T(8,128)(2,1)S(1)}, bf16[32,4096]{1,0:T(8,128)(2,1)S(1)}, u32[]{:S(2)}, u32[]{:S(2)}) collective-permute-start(bf16[32,4096]{1,0:T(8,128)(2,1)S(1)} %get-tuple-element.22), channel_id=1, source_target_pairs={{0,8},{4,12},{8,0},{12,4},{16,24},{20,28},{24,16},{28,20},{1,9},{5... | collective-permute-start | bytes 786440 | tf_op jit(solution)/shard_map/ppermute | solution.py:65
  49.2 12.9 %collective-permute-start.11 = (bf16[32,4096]{1,0:T(8,128)(2,1)S(1)}, bf16[32,4096]{1,0:T(8,128)(2,1)S(1)}, u32[]{:S(2)}, u32[]{:S(2)}) collective-permute-start(bf16[32,4096]{1,0:T(8,128)(2,1)S(1)} %get-tuple-element.23), channel_id=1, source_target_pairs={{0,8},{4,12},{8,0},{12,4},{16,24},{20,28},{24,16},{28,20},{1,9},{5... | collective-permute-start | bytes 786440 | tf_op jit(solution)/shard_map/ppermute | solution.py:65
  51.4 8.2 %collective-permute-start.23 = (bf16[32,4096]{1,0:T(8,128)(2,1)S(1)}, bf16[32,4096]{1,0:T(8,128)(2,1)S(1)}, u32[]{:S(2)}, u32[]{:S(2)}) collective-permute-start(bf16[32,4096]{1,0:T(8,128)(2,1)S(1)} %fusion.11), channel_id=1, source_target_pairs={{0,16},{4,20},{8,24},{12,28},{16,0},{20,4},{24,8},{28,12},{1,17},{... | collective-permute-start | bytes 786440 | tf_op jit(solution)/shard_map/ppermute | solution.py:65
  58.1 6.4 %collective-permute-start.17 = (bf16[32,4096]{1,0:T(8,128)(2,1)S(1)}, bf16[32,4096]{1,0:T(8,128)(2,1)S(1)}, u32[]{:S(2)}, u32[]{:S(2)}) collective-permute-start(bf16[32,4096]{1,0:T(8,128)(2,1)S(1)} %fusion.7), channel_id=1, source_target_pairs={{0,16},{4,20},{8,24},{12,28},{16,0},{20,4},{24,8},{28,12},{1,17},{... | collective-permute-start | bytes 786440 | tf_op jit(solution)/shard_map/ppermute | solution.py:65
  59.8 8.1 %collective-permute-start.24 = (bf16[16,4096]{1,0:T(8,128)(2,1)S(1)}, bf16[16,4096]{1,0:T(8,128)(2,1)S(1)}, u32[]{:S(2)}, u32[]{:S(2)}) collective-permute-start(bf16[16,4096]{1,0:T(8,128)(2,1)S(1)} %select_convert_fusion), channel_id=1, source_target_pairs={{0,1},{1,0},{2,3},{3,2},{4,5},{5,4},{6,7},{7,6},{8,9},{9,8},{10,11... | collective-permute-start | bytes 393224 | tf_op jit(solution)/shard_map/ppermute | solution.py:69
  64.8 6.0 %collective-permute-start.18 = (bf16[16,4096]{1,0:T(8,128)(2,1)S(1)}, bf16[16,4096]{1,0:T(8,128)(2,1)S(1)}, u32[]{:S(2)}, u32[]{:S(2)}) collective-permute-start(bf16[16,4096]{1,0:T(8,128)(2,1)S(1)} %select_convert_fusion.1), channel_id=1, source_target_pairs={{0,1},{1,0},{2,3},{3,2},{4,5},{5,4},{6,7},{7,6},{8,9},{9,8},{10,11... | collective-permute-start | bytes 393224 | tf_op jit(solution)/shard_map/ppermute | solution.py:69
  66.4 7.9 %collective-permute-start.12 = (bf16[32,4096]{1,0:T(8,128)(2,1)S(1)}, bf16[32,4096]{1,0:T(8,128)(2,1)S(1)}, u32[]{:S(2)}, u32[]{:S(2)}) collective-permute-start(bf16[32,4096]{1,0:T(8,128)(2,1)S(1)} %get-tuple-element.21), channel_id=1, source_target_pairs={{0,16},{4,20},{8,24},{12,28},{16,0},{20,4},{24,8},{28,12},{1,17},{... | collective-permute-start | bytes 786440 | tf_op jit(solution)/shard_map/ppermute | solution.py:65
  68.0 7.6 %collective-permute-start.25 = (bf16[16,4096]{1,0:T(8,128)(2,1)S(1)}, bf16[16,4096]{1,0:T(8,128)(2,1)S(1)}, u32[]{:S(2)}, u32[]{:S(2)}) collective-permute-start(bf16[16,4096]{1,0:T(8,128)(2,1)S(1)} %fusion.50), channel_id=1, source_target_pairs={{0,3},{3,0},{1,2},{2,1},{4,7},{7,4},{5,6},{6,5},{8,11},{11,8},{9,1... | collective-permute-start | bytes 393224 | tf_op jit(solution)/shard_map/ppermute | solution.py:69
  70.8 8.1 %collective-permute-start.19 = (bf16[16,4096]{1,0:T(8,128)(2,1)S(1)}, bf16[16,4096]{1,0:T(8,128)(2,1)S(1)}, u32[]{:S(2)}, u32[]{:S(2)}) collective-permute-start(bf16[16,4096]{1,0:T(8,128)(2,1)S(1)} %fusion.49), channel_id=1, source_target_pairs={{0,3},{3,0},{1,2},{2,1},{4,7},{7,4},{5,6},{6,5},{8,11},{11,8},{9,1... | collective-permute-start | bytes 393224 | tf_op jit(solution)/shard_map/ppermute | solution.py:69
  74.5 6.5 %collective-permute-start.13 = (bf16[16,4096]{1,0:T(8,128)(2,1)S(1)}, bf16[16,4096]{1,0:T(8,128)(2,1)S(1)}, u32[]{:S(2)}, u32[]{:S(2)}) collective-permute-start(bf16[16,4096]{1,0:T(8,128)(2,1)S(1)} %select_convert_fusion.2), channel_id=1, source_target_pairs={{0,1},{1,0},{2,3},{3,2},{4,5},{5,4},{6,7},{7,6},{8,9},{9,8},{10,11... | collective-permute-start | bytes 393224 | tf_op jit(solution)/shard_map/ppermute | solution.py:69
  75.6 7.2 %collective-permute-start.26 = (bf16[16,4096]{1,0:T(8,128)(2,1)S(1)}, bf16[16,4096]{1,0:T(8,128)(2,1)S(1)}, u32[]{:S(2)}, u32[]{:S(2)}) collective-permute-start(bf16[16,4096]{1,0:T(8,128)(2,1)S(1)} %add_convert_fusion), channel_id=1, source_target_pairs={{0,1},{1,0},{2,3},{3,2},{4,5},{5,4},{6,7},{7,6},{8,9},{9,8},{10,11... | collective-permute-start | bytes 393224 | tf_op jit(solution)/shard_map/ppermute | solution.py:69
  79.0 5.0 %collective-permute-start.20 = (bf16[16,4096]{1,0:T(8,128)(2,1)S(1)}, bf16[16,4096]{1,0:T(8,128)(2,1)S(1)}, u32[]{:S(2)}, u32[]{:S(2)}) collective-permute-start(bf16[16,4096]{1,0:T(8,128)(2,1)S(1)} %add_convert_fusion.1), channel_id=1, source_target_pairs={{0,1},{1,0},{2,3},{3,2},{4,5},{5,4},{6,7},{7,6},{8,9},{9,8},{10,11... | collective-permute-start | bytes 393224 | tf_op jit(solution)/shard_map/ppermute | solution.py:69
  81.0 6.9 %collective-permute-start.14 = (bf16[16,4096]{1,0:T(8,128)(2,1)S(1)}, bf16[16,4096]{1,0:T(8,128)(2,1)S(1)}, u32[]{:S(2)}, u32[]{:S(2)}) collective-permute-start(bf16[16,4096]{1,0:T(8,128)(2,1)S(1)} %fusion.48), channel_id=1, source_target_pairs={{0,3},{3,0},{1,2},{2,1},{4,7},{7,4},{5,6},{6,5},{8,11},{11,8},{9,1... | collective-permute-start | bytes 393224 | tf_op jit(solution)/shard_map/ppermute | solution.py:69
  88.0 5.0 %collective-permute-start.15 = (bf16[16,4096]{1,0:T(8,128)(2,1)S(1)}, bf16[16,4096]{1,0:T(8,128)(2,1)S(1)}, u32[]{:S(2)}, u32[]{:S(2)}) collective-permute-start(bf16[16,4096]{1,0:T(8,128)(2,1)S(1)} %add_convert_fusion.2), channel_id=1, source_target_pairs={{0,1},{1,0},{2,3},{3,2},{4,5},{5,4},{6,7},{7,6},{8,9},{9,8},{10,11... | collective-permute-start | bytes 393224 | tf_op jit(solution)/shard_map/ppermute | solution.py:69

commit v3 on v2

v3 whole, which is shorter than its diff:
```python
import jax
import jax.numpy as jnp
from jax import lax
from jax.experimental import pallas as pl
from jax.experimental.pallas import tpu as pltpu
from jax.sharding import PartitionSpec as P

STEPS = 6
F32 = jnp.float32
BF16 = jnp.bfloat16


def from_behind(block, axis, distance):
    devices = range(lax.axis_size(axis))
    route = [((i - distance) % len(devices), i) for i in devices]
    return lax.ppermute(block, axis, route)


def contract(left, right):
    return lax.dot_general(
        left, right, (((1,), (1,)), ((), ())), preferred_element_type=F32
    )


def rows_dot(left, right):
    return jnp.dot(left, right, preferred_element_type=F32)


def activations(tokens, cotangent, gate, upper, down):
    gate_sum = contract(gate, tokens)
    up_sum = contract(upper, tokens)
    squash = jax.nn.sigmoid(gate_sum)
    activated = gate_sum * squash
    hidden = (activated * up_sum).astype(BF16)
    backward = contract(down, cotangent)
    gate_back = (backward * up_sum * squash * (1.0 + gate_sum * (1.0 - squash))).astype(
        BF16
    )
    up_back = (backward * activated).astype(BF16)
    return gate_back, up_back, hidden


def ring(tokens, cotangent, gate_weight, up_weight, down_weight):
    held = jnp.stack([gate_weight, up_weight, down_weight])
    summed = None
    for position in range(STEPS):
        if position > 0:
            held = from_behind(held, "section", 1)
        parts = activations(tokens, cotangent, held[0], held[1], held[2])
        piece = jnp.stack(
            [
                rows_dot(parts[0], tokens),
                rows_dot(parts[1], tokens),
                rows_dot(parts[2], cotangent),
            ]
        )
        if position > 0:
            summed = from_behind(summed, "section", 1) + piece
        else:
            summed = piece
    finished = lax.psum(summed, "dp").astype(BF16)
    return (finished[0], finished[1], finished[2])


def hop(block, step, only=None):
    route = [(i, i ^ step(i)) for i in range(8) if only is None or i % 2 == only]
    return lax.ppermute(block, "section", route)


def along(block, route):
    return lax.ppermute(block, "dp", route)


CORE, X, Y = 1, 2, 4
PAIRS = [(0, 1), (1, 0), (2, 3), (3, 2)]
ACROSS = [(0, 3), (3, 0), (1, 2), (2, 1)]
SPAN = 512
VMEM_LIMIT = 8 * 2**20


def after(value, *others):
    return lax.optimization_barrier((value, others))[0]


def on_chip(*parts):
    def kernel(*refs):
        sources, out, sems = refs[: len(parts)], refs[-2], refs[-1]
        copies, row = [], 0
        for at, source in enumerate(sources):
            rows = source.shape[0]
            spot = out.at[pl.ds(row, rows)]
            copies.append(pltpu.make_async_copy(source, spot, sems.at[at]))
            row += rows
        for copy in copies:
            copy.start()
        for copy in copies:
            copy.wait()

    rows = sum(part.shape[0] for part in parts)
    return pl.pallas_call(
        kernel,
        out_shape=pltpu.VMEM((rows, parts[0].shape[1]), parts[0].dtype),
        in_specs=[pl.BlockSpec(memory_space=pltpu.HBM)] * len(parts),
        out_specs=pl.BlockSpec(memory_space=pltpu.VMEM),
        scratch_shapes=[pltpu.SemaphoreType.DMA((len(parts),))],
        compiler_params=pltpu.CompilerParams(vmem_limit_bytes=2**20),
        cost_estimate=pl.CostEstimate(flops=1, bytes_accessed=1, transcendentals=0),
    )(*[pltpu.with_memory_space_constraint(part, pltpu.HBM) for part in parts])


def kernel_call(kernel, outs, flags, *arrays):
    held = [pltpu.with_memory_space_constraint(a, pltpu.VMEM) for a in arrays[-2:]]
    rows = held[0].shape[0] // 2

    def inner(*refs):
        at = len(arrays) - 1
        halves = [ref.at[pl.ds(k * rows, rows)] for ref in refs[at : at + 2] for k in (0, 1)]
        kernel(*refs[:at], *halves, *refs[at + 2 :])

    return pl.pallas_call(
        inner,
        out_shape=[jax.ShapeDtypeStruct(shape, dtype) for shape, dtype in outs],
        in_specs=[pl.BlockSpec(memory_space=pltpu.SMEM)]
        + [pl.BlockSpec(memory_space=pltpu.VMEM)] * len(arrays),
        out_specs=[pl.BlockSpec(memory_space=pltpu.VMEM)] * len(outs),
        compiler_params=pltpu.CompilerParams(vmem_limit_bytes=VMEM_LIMIT),
        cost_estimate=pl.CostEstimate(flops=1, bytes_accessed=1, transcendentals=0),
    )(flags, *arrays[:-2], *held)


def span_dot(weights, low, high, sources):
    totals = [None, None]
    for at in range(0, sources[0].shape[1], SPAN):
        columns = slice(at, at + SPAN)
        left = [ref[low:high, columns] for ref in weights]
        left = left[0] if len(left) == 1 else jnp.concatenate(left)
        for which, source in enumerate(sources):
            part = contract(left, source[:, columns])
            old = totals[which]
            totals[which] = part if old is None else old + part
    return totals


def sums_into(lefts, sources, outs):
    for at in range(0, sources[0].shape[1], SPAN):
        columns = slice(at, at + SPAN)
        part = rows_dot(lefts[0], sources[0][:, columns])
        part = part + rows_dot(lefts[1], sources[1][:, columns])
        row = 0
        for ref in outs:
            rows = ref.shape[0]
            ref[:, columns] = part[row : row + rows].astype(ref.dtype)
            row += rows


def products(flags, flag, weights, tokens, cotangent):
    block = weights[0].shape[0] // 3
    sums = span_dot(weights, 0, 2 * block, tokens)
    backs = span_dot(weights, 2 * block, 3 * block, cotangent)
    found = []
    for which in range(len(weights)):
        pair = []
        row = which * block
        for at in range(2):
            gate_sum = sums[at][2 * row : 2 * row + block]
            up_sum = sums[at][2 * row + block : 2 * row + 2 * block]
            back = backs[at][row : row + block]
            squash = jax.nn.sigmoid(gate_sum)
            activated = gate_sum * squash
            slope = up_sum * squash * (1.0 + gate_sum * (1.0 - squash))
            parts = [back * slope, back * activated, activated * up_sum]
            meets = flags[flag + 2 * which + at] != 0
            pair.append(jnp.where(meets, jnp.concatenate(parts), 0.0).astype(BF16))
        found.append(pair)
    return found


def square(tokens, cotangent, gate_weight, up_weight, down_weight):
    section = lax.axis_index("section")
    core = section % 2
    chip = section // 2
    line = lax.axis_index("dp")
    block = gate_weight.shape[0]
    half = block // 2
    tok, width = tokens.shape
    first = core == 0
    even = chip % 2 == 0
    keep_low = jnp.logical_or(line == 0, line == 3)

    def spread(own):
        v = [(i, i ^ (Y | CORE if i % 4 == 2 else CORE)) for i in range(8)]
        u = [
            (i, i ^ (X | CORE if i % 2 else (Y | CORE if i % 4 == 0 else CORE)))
            for i in range(8)
        ]
        return lax.ppermute(own, "section", v), lax.ppermute(own, "section", u)

    def other(i):
        return Y if i % 2 == 0 else X

    swapped = jnp.logical_and(core == 1, chip % 2 == 1)
    next_chip = jnp.where(first, chip ^ 1, chip ^ 2)
    holders = jnp.stack(
        [
            jnp.where(swapped, next_chip, chip),
            jnp.where(swapped, chip, next_chip),
            jnp.where(first, chip ^ 2, (chip + 3) % 4),
            chip ^ 3,
        ]
    )
    sections = jnp.stack([section, section ^ 1])
    meets = (sections[None, :] - (2 * holders + 1 - core)[:, None]) % 8 < STEPS
    flags = jnp.concatenate(
        [meets.reshape(8).astype(jnp.int32), jnp.stack([first, even]).astype(jnp.int32)]
    )

    low, high = slice(0, 2 * block), slice(2 * block, 3 * block)

    def of_v_u(flags, v, u, t0, t1, c0, c1, found, p_out):
        pairs = products(flags, 0, [v, u], (t0, t1), (c0, c1))
        for which in range(2):
            for at in range(2):
                found[2 * which + at] = pairs[which][at]
        sums_into([part[high] for part in pairs[0]], (c0, c1), [p_out.at[high]])
        sums_into([part[low] for part in pairs[0]], (t0, t1), [p_out.at[low]])

    def of_s(flags, s, t0, t1, c0, c1, gate, up, down):
        (pair,) = products(flags, 4, [s], (t0, t1), (c0, c1))
        sums_into([part[high] for part in pair], (c0, c1), [down])
        sums_into([part[low] for part in pair], (t0, t1), [gate, up])

    def of_e(flags, e, found, t0, t1, c0, c1, *outs):
        (pair,) = products(flags, 6, [e], (t0, t1), (c0, c1))
        leaving, staying = [], []
        for at in range(2):
            v, u = found[at], found[2 + at]
            mixed = jnp.where(flags[8] != 0, pair[at], v)
            leaving.append(jnp.where(flags[9] != 0, mixed, u))
            staying.append(jnp.where(flags[9] != 0, u, mixed))
        for rows, source, some in ((high, (c0, c1), (2, 5)), (low, (t0, t1), (0, 1, 3, 4))):
            lefts = [
                jnp.concatenate([leave[rows], stay[rows]])
                for leave, stay in zip(leaving, staying)
            ]
            sums_into(lefts, source, [outs[at] for at in some])

    narrow, wide = ((block, width), BF16), ((block, width), F32)

    tokens_in = hop(tokens, lambda i: CORE)
    cotangent_in = hop(cotangent, lambda i: CORE)
    own = on_chip(gate_weight, up_weight, down_weight)
    w_v, w_u = spread(own)
    here = [on_chip(tokens, tokens_in), on_chip(cotangent, cotangent_in)]
    w_s = hop(after(w_v, here), other)
    found, p = kernel_call(
        of_v_u,
        [((4, 3 * block, tok), BF16), ((3 * block, width), BF16)],
        flags, w_v, w_u, *here,
    )
    w_e = hop(after(w_u, found), lambda i: Y, 0)
    order = (2, 0, 1)
    p = hop(p, lambda i: X, 0)
    p_in = [p[k * block : (k + 1) * block] for k in range(3)]
    q = kernel_call(of_s, [narrow] * 3, flags, w_s, *here)
    there = {k: hop(q[k], lambda i: X) for k in order[:2]}
    sums = kernel_call(of_e, [wide] * 6, flags, w_e, found, *here)
    there[order[2]] = hop(after(q[order[2]], sums), lambda i: X)
    leave, stay = sums[:3], sums[3:]

    turn = (sums,)
    r, swap, across, back_in = {}, {}, {}, {}
    totals, kept, done, results = {}, {}, {}, {}

    def take(value):
        return after(value, turn)

    def leave_stage(k):
        p_got, q_got = p_in[k], take(there[k])
        out = (leave[k] + jnp.where(even, q_got, p_got).astype(F32)).astype(BF16)
        r[k] = hop(out, lambda i: Y)
        totals[k] = stay[k] + jnp.where(even, p_got, q_got).astype(F32)
        return out

    def swap_stage(k):
        total = totals[k] + take(r[k]).astype(F32)
        upper, lower = total[:half], total[half:]
        out = jnp.where(keep_low, lower, upper).astype(BF16)
        kept[k] = jnp.where(keep_low, upper, lower)
        swap[k] = along(out, PAIRS)
        return out

    def across_stage(k):
        kept[k] = lax.reduce_precision(kept[k] + take(swap[k]).astype(F32), 8, 7)
        out = kept[k].astype(BF16)
        across[k] = along(out, ACROSS)
        return out

    def back_stage(k):
        done[k] = (kept[k] + take(across[k]).astype(F32)).astype(BF16)
        back_in[k] = along(done[k], PAIRS)
        return done[k]

    def result_stage(k):
        mine, got = done[k], take(back_in[k])
        results[k] = jnp.concatenate(
            [jnp.where(keep_low, mine, got), jnp.where(keep_low, got, mine)]
        )
        return results[k]

    stages = [leave_stage, swap_stage, across_stage, back_stage, result_stage]
    steps = [(k, at) for at in range(5) for k in range(3)]
    for k, at in steps:
        turn = stages[at](order[k])
    return results[0], results[1], results[2]


def solution(mesh):
    fits = mesh.shape["section"] == 8 and mesh.shape["dp"] == 4
    return jax.shard_map(
        square if fits else ring,
        mesh=mesh,
        in_specs=(
            P(("section", "dp"), None),
            P(("section", "dp"), None),
            P("section", None),
            P("section", None),
            P("section", None),
        ),
        out_specs=(P("section", None), P("section", None), P("section", None)),
        check_vma=False,
    )
```

time: 94.1 us -> 89.9 us (0.955)
  Pallas kernels: 0 us -> 19.8 us
  matrix products: 14.5 us -> 0 us
  waiting for transfers between devices: 20.6 us -> 15.8 us
  local copies, waits for them, and re-layouts: 7.95 us -> 3.39 us
  other arithmetic: 5.4 us -> 9.31 us
  starting transfers between devices: 44.2 us -> 40.3 us
    pallas_call x0 -> x6, Pallas kernels: none -> 19.8 us  [the longest x3 14 us: kernel_call(): pl.pallas_call(inner, out_shape=[jax.ShapeDtypeStruct(shape, dtype) for s...]
    dot_general x14 -> x0, matrix products: 14.5 us -> none  [the longest x8 10.5 us: contract(): lax.dot_general(left, right, (((1,), (1,)), ((), ())), preferred_element_...]
    ppermute x9, waiting for transfers between devices: 12.7 us -> 2.92 us  [along(): return lax.ppermute(block, 'dp', route)]
    ppermute x14 -> x11, starting transfers between devices: 26.1 us -> 16.6 us  [hop(): return lax.ppermute(block, 'section', route)]
    ppermute x9, starting transfers between devices: 14.3 us -> 20.6 us  [along(): return lax.ppermute(block, 'dp', route)]
    concatenate x2 -> x0, local copies, waits for them, and re-layouts: 4.4 us -> none  [the longest x1 2.7 us: square(): tokens2 = jnp.concatenate([tokens, tokens_in])]
    ppermute x4 -> x2, waiting for transfers between devices: 1.26 us -> 4.6 us  [spread(): return (lax.ppermute(own, 'section', v), lax.ppermute(own, 'section', u))]
    convert_element_type x11 -> x12, other arithmetic: 0.61 us -> 3.59 us  [the longest x3 3.21 us: leave_stage(): out = (leave[k] + jnp.where(even, q_got, p_got).astype(F32)).astype(BF16)]
  transfers between devices with their start and end apart: 27 -> 22, of which waited for: 10 -> 10; matrix products, arithmetic and copies ran while one was open for 26% -> 10% of each run, Pallas kernels for 0% -> 22%
where the time goes in v3:
time: 89.9 us; the launch traced here: 89.4 us
  starting transfers between devices  40.3 us (45%)
  Pallas kernels  19.8 us (22%)
  waiting for transfers between devices  15.8 us (18%)
  other arithmetic  9.31 us (10%)
  local copies, waits for them, and re-layouts  3.39 us (4%)
    ppermute x9, starting transfers between devices, along(): return lax.ppermute(block, 'dp', route)  20.6 us
    ppermute x11, starting transfers between devices, hop(): return lax.ppermute(block, 'section', route)  16.6 us
    pallas_call x3, Pallas kernels, kernel_call(): pl.pallas_call(inner, out_shape=[jax.ShapeDtypeStruct(shape, dtype) for s...  14 us
    ppermute x11, waiting for transfers between devices, hop(): return lax.ppermute(block, 'section', route)  8.24 us
    pallas_call x3, Pallas kernels, on_chip(): pl.pallas_call(kernel, out_shape=pltpu.VMEM((rows, parts[0].shape[1]), pa...  5.84 us
    ppermute x2, waiting for transfers between devices, spread(): return (lax.ppermute(own, 'section', v), lax.ppermute(own, 'section', u))  4.6 us
    unnamed x10, local copies, waits for them, and re-layouts  3.3 us
    convert_element_type x3, other arithmetic, leave_stage(): out = (leave[k] + jnp.where(even, q_got, p_got).astype(F32)).astype(BF16)  3.21 us
  transfers between devices with their start and end apart: 22, of which 10 were waited for; matrix products, arithmetic and copies ran while one was open for 10% of the time, Pallas kernels for 22%

profile of v3, /device:TPU:0, one launch (start us, length us, event | category | flops | bytes accessed | tf_op | source)
XLA Modules:
  0.0 89.4 jit_solution(5036727567236041327)
XLA Ops:
  0.6 0.5 collective-permute-start.2
  1.1 0.1 collective-permute-start.3
  1.2 2.0 %shard_map.76 = bf16[96,4096]{1,0:T(8,128)(2,1)} custom-call(bf16[32,4096]{1,0:T(8,128)(2,1)} %refs_0_.3, bf16[32,4096]{1,0:T(8,128)(2,1)} %refs_1_.1, bf16[32,4096]{1,0:T(8,128)(2,1)} %refs_2_.1), custom_call_target="tpu_custom_call" | custom-call | flops 1 | bytes 1 | tf_op jit(solution)/shard_map/pallas_call | solution.py:100
  3.3 0.5 collective-permute-start.1
  3.8 2.6 %collective-permute-start = (bf16[96,4096]{1,0:T(8,128)(2,1)}, bf16[96,4096]{1,0:T(8,128)(2,1)}, u32[]{:S(2)}, u32[]{:S(2)}) collective-permute-start(bf16[96,4096]{1,0:T(8,128)(2,1)} %shard_map.76), channel_id=1, source_target_pairs={{0,20},{4,8},{8,12},{12,0},{16,4},{20,24},{24,28},{28,16},{1,21},{... | collective-permute-start | bytes 2359304 | tf_op jit(solution)/shard_map/ppermute | solution.py:196
  6.4 0.1 pad_add_fusion
  6.5 0.1 fusion.3
  6.5 0.1 broadcast_subtract_fusion
  6.6 0.1 sub.37
  6.7 0.0 collective-permute-done.2.refs_1_
  6.7 1.9 %shard_map.77.refs_3_.refs_2_ = bf16[384,4096]{1,0:T(8,128)(2,1)S(1)} custom-call(bf16[192,4096]{1,0:T(8,128)(2,1)} %refs_0_.4, bf16[192,4096]{1,0:T(8,128)(2,1)} %collective-permute-done.2.refs_1_), custom_call_target="tpu_custom_call" | custom-call | flops 1 | bytes 1 | tf_op jit(solution)/shard_map/pallas_call | solution.py:100
  8.6 0.0 collective-permute-done.3.refs_1_
  8.6 1.9 %shard_map.78.refs_4_.refs_3_ = bf16[384,4096]{1,0:T(8,128)(2,1)S(1)} custom-call(bf16[192,4096]{1,0:T(8,128)(2,1)} %refs_0_.5, bf16[192,4096]{1,0:T(8,128)(2,1)} %collective-permute-done.3.refs_1_), custom_call_target="tpu_custom_call" | custom-call | flops 1 | bytes 1 | tf_op jit(solution)/shard_map/pallas_call | solution.py:100
  10.6 1.1 %collective-permute-start.6 = (bf16[96,4096]{1,0:T(8,128)(2,1)}, bf16[96,4096]{1,0:T(8,128)(2,1)S(1)}, u32[]{:S(2)}, u32[]{:S(2)}) collective-permute-start(bf16[96,4096]{1,0:T(8,128)(2,1)} %collective-permute-done.1.refs_1_), channel_id=1, source_target_pairs={{0,16},{4,12},{8,24},{12,4},{16,0},{20,28},{24,8},{28,20},{1,17},{... | collective-permute-start | bytes 2359304 | tf_op jit(solution)/shard_map/ppermute | solution.py:67
  11.7 0.1 add_convert_fusion.6.refs_0_
  11.7 4.6 %collective-permute-done.refs_2_ = bf16[96,4096]{1,0:T(8,128)(2,1)} collective-permute-done((bf16[96,4096]{1,0:T(8,128)(2,1)}, bf16[96,4096]{1,0:T(8,128)(2,1)}, u32[]{:S(2)}, u32[]{:S(2)}) %collective-permute-start) | collective-permute-done | bytes 786464 | tf_op jit(solution)/shard_map/ppermute | solution.py:196
  16.3 5.6 %shard_map.79 = (bf16[4,96,192]{2,1,0:T(8,128)(2,1)S(1)}, bf16[96,4096]{1,0:T(8,128)(2,1)}) custom-call(s32[10]{0:T(128)S(1)} %add_convert_fusion.6.refs_0_, bf16[96,4096]{1,0:T(8,128)(2,1)} %collective-permute-done.1.refs_1_, bf16[96,4096]{1,0:T(8,128)(2,1)} %collective-permute-done.refs_2_, bf16[384,4096]{1,0:T(8,128)(2,1)S(1)} %shard_map.77.refs_3_.refs_2_, ...), custom_call_target="tpu_custom_call" | custom-call | flops 1 | bytes 1 | tf_op jit(solution)/shard_map/pallas_call | solution.py:120
  21.9 3.6 %collective-permute-start.4 = (bf16[96,4096]{1,0:T(8,128)(2,1)}, bf16[96,4096]{1,0:T(8,128)(2,1)}, u32[]{:S(2)}, u32[]{:S(2)}) collective-permute-start(bf16[96,4096]{1,0:T(8,128)(2,1)} %collective-permute-done.refs_2_), channel_id=1, source_target_pairs={{0,16},{8,24},{16,0},{24,8},{1,17},{9,25},{17,1},{25,9},{2,18},{10... | collective-permute-start | bytes 2359304 | tf_op jit(solution)/shard_map/ppermute | solution.py:67
  25.6 3.5 %collective-permute-start.5 = (bf16[96,4096]{1,0:T(8,128)(2,1)}, bf16[96,4096]{1,0:T(8,128)(2,1)}, u32[]{:S(2)}, u32[]{:S(2)}) collective-permute-start(bf16[96,4096]{1,0:T(8,128)(2,1)} %get-tuple-element.35), channel_id=1, source_target_pairs={{0,8},{8,0},{16,24},{24,16},{1,9},{9,1},{17,25},{25,17},{2,10},{10... | collective-permute-start | bytes 2359304 | tf_op jit(solution)/shard_map/ppermute | solution.py:67
  29.1 0.0 collective-permute-done.6.refs_1_
  29.1 3.9 %shard_map.81 = (bf16[32,4096]{1,0:T(8,128)(2,1)S(1)}, bf16[32,4096]{1,0:T(8,128)(2,1)S(1)}, bf16[32,4096]{1,0:T(8,128)(2,1)}) custom-call(s32[10]{0:T(128)S(1)} %add_convert_fusion.6.refs_0_, bf16[96,4096]{1,0:T(8,128)(2,1)S(1)} %collective-permute-done.6.refs_1_, bf16[384,4096]{1,0:T(8,128)(2,1)S(1)} %shard_map.77.refs_3_.refs_2_, ...), custom_call_target="tpu_custom_call" | custom-call | flops 1 | bytes 1 | tf_op jit(solution)/shard_map/pallas_call | solution.py:120
  33.1 0.7 copy-done.2
  33.8 0.7 copy-done.4
  34.5 0.4 collective-permute-start.8
  34.9 1.6 %collective-permute-start.7 = (bf16[32,4096]{1,0:T(8,128)(2,1)}, bf16[32,4096]{1,0:T(8,128)(2,1)S(1)}, u32[]{:S(2)}, u32[]{:S(2)}) collective-permute-start(bf16[32,4096]{1,0:T(8,128)(2,1)} %copy-done.4), channel_id=1, source_target_pairs={{0,8},{4,12},{8,0},{12,4},{16,24},{20,28},{24,16},{28,20},{1,9},{5... | collective-permute-start | bytes 786440 | tf_op jit(solution)/shard_map/ppermute | solution.py:67
  36.5 0.0 collective-permute-done.4.refs_1_
  36.5 1.9 %copy-done.1 = bf16[384,4096]{1,0:T(8,128)(2,1)S(1)} copy-done((bf16[384,4096]{1,0:T(8,128)(2,1)S(1)}, bf16[384,4096]{1,0:T(8,128)(2,1)}, u32[]{:S(2)}) %copy-start.1) | copy-done | bytes 3145752
  38.4 4.4 %shard_map.80 = (f32[32,4096]{1,0:T(8,128)S(1)}, f32[32,4096]{1,0:T(8,128)S(1)}, f32[32,4096]{1,0:T(8,128)S(1)}, f32[32,4096]{1,0:T(8,128)S(1)}, f32[32,4096]{1,0:T(8,128)S(1)}, /*index=5*/f32[32,4096]{1,0:T(8,128)S(1)}) custom-call(s32[10]{0:T(128)S(1)} %add_convert_fusion.6.refs_0_, bf16[96,4096]{1,0:T(8,128)(2,1)} %collective-permute-done.4.refs_1_, ...), custom_call_target="tpu_custom_call" | custom-call | flops 1 | bytes 1 | tf_op jit(solution)/shard_map/pallas_call | solution.py:120
  42.8 2.5 %collective-permute-start.11 = (bf16[32,4096]{1,0:T(8,128)(2,1)S(1)}, bf16[32,4096]{1,0:T(8,128)(2,1)S(1)}, u32[]{:S(2)}, u32[]{:S(2)}) collective-permute-start(bf16[32,4096]{1,0:T(8,128)(2,1)S(1)} %copy-done.3), channel_id=1, source_target_pairs={{0,8},{4,12},{8,0},{12,4},{16,24},{20,28},{24,16},{28,20},{1,9},{5... | collective-permute-start | bytes 786440 | tf_op jit(solution)/shard_map/ppermute | solution.py:67
  45.4 3.4 %collective-permute-done.8 = bf16[32,4096]{1,0:T(8,128)(2,1)} collective-permute-done((bf16[32,4096]{1,0:T(8,128)(2,1)}, bf16[32,4096]{1,0:T(8,128)(2,1)}, u32[]{:S(2)}, u32[]{:S(2)}) %collective-permute-start.8) | collective-permute-done | bytes 262176 | tf_op jit(solution)/shard_map/ppermute | solution.py:67
  48.8 0.0 collective-permute-done.5
  48.8 1.1 %add_convert_fusion.2 = bf16[32,4096]{1,0:T(8,128)(2,1)S(1)} fusion(f32[32,4096]{1,0:T(8,128)S(1)} %get-tuple-element.38, bf16[32,4096]{1,0:T(8,128)(2,1)} %collective-permute-done.8, pred[]{:T(512)} %eq.30, bf16[96,4096]{1,0:T(8,128)(2,1)} %collective-permute-done.5), kind=kLoop, calls=%fused_computation.5 | loop fusion | flops 524288 | bytes 1310721 | tf_op jit(solution)/shard_map/convert_element_type | solution.py:279
  49.9 0.8 collective-permute-start.10
  50.7 3.0 %collective-permute-done.7 = bf16[32,4096]{1,0:T(8,128)(2,1)S(1)} collective-permute-done((bf16[32,4096]{1,0:T(8,128)(2,1)}, bf16[32,4096]{1,0:T(8,128)(2,1)S(1)}, u32[]{:S(2)}, u32[]{:S(2)}) %collective-permute-start.7) | collective-permute-done | bytes 262176 | tf_op jit(solution)/shard_map/ppermute | solution.py:67
  53.7 1.1 %add_convert_fusion.1 = bf16[32,4096]{1,0:T(8,128)(2,1)S(1)} fusion(f32[32,4096]{1,0:T(8,128)S(1)} %get-tuple-element.40, bf16[32,4096]{1,0:T(8,128)(2,1)S(1)} %collective-permute-done.7, pred[]{:T(512)} %eq.30, bf16[96,4096]{1,0:T(8,128)(2,1)} %collective-permute-done.5), kind=kLoop, calls=%fused_computation.4 | loop fusion | flops 524288 | bytes 1310721 | tf_op jit(solution)/shard_map/convert_element_type | solution.py:279
  54.8 1.2 %collective-permute-start.9 = (bf16[32,4096]{1,0:T(8,128)(2,1)S(1)}, bf16[32,4096]{1,0:T(8,128)(2,1)S(1)}, u32[]{:S(2)}, u32[]{:S(2)}) collective-permute-start(bf16[32,4096]{1,0:T(8,128)(2,1)S(1)} %add_convert_fusion.1), channel_id=1, source_target_pairs={{0,16},{4,20},{8,24},{12,28},{16,0},{20,4},{24,8},{28,12},{1,17},{... | collective-permute-start | bytes 786440 | tf_op jit(solution)/shard_map/ppermute | solution.py:67
  55.9 0.6 collective-permute-done.11
  56.5 1.1 %add_convert_fusion = bf16[32,4096]{1,0:T(8,128)(2,1)S(1)} fusion(f32[32,4096]{1,0:T(8,128)S(1)} %get-tuple-element.41, bf16[32,4096]{1,0:T(8,128)(2,1)S(1)} %collective-permute-done.11, pred[]{:T(512)} %eq.30, bf16[96,4096]{1,0:T(8,128)(2,1)} %collective-permute-done.5), kind=kLoop, calls=%fused_computation.3 | loop fusion | flops 524288 | bytes 1310721 | tf_op jit(solution)/shard_map/convert_element_type | solution.py:279
  57.6 1.2 %collective-permute-start.14 = (bf16[32,4096]{1,0:T(8,128)(2,1)S(1)}, bf16[32,4096]{1,0:T(8,128)(2,1)S(1)}, u32[]{:S(2)}, u32[]{:S(2)}) collective-permute-start(bf16[32,4096]{1,0:T(8,128)(2,1)S(1)} %add_convert_fusion), channel_id=1, source_target_pairs={{0,16},{4,20},{8,24},{12,28},{16,0},{20,4},{24,8},{28,12},{1,17},{... | collective-permute-start | bytes 786440 | tf_op jit(solution)/shard_map/ppermute | solution.py:67
  58.8 1.1 %convert_add_fusion.2 = f32[32,4096]{1,0:T(8,128)S(1)} fusion(bf16[32,4096]{1,0:T(8,128)(2,1)S(1)} %collective-permute-done.10, f32[32,4096]{1,0:T(8,128)S(1)} %get-tuple-element.43, bf16[32,4096]{1,0:T(8,128)(2,1)} %collective-permute-done.8, pred[]{:T(512)} %eq.30, bf16[96,4096]{1,0:T(8,128)(2,1)} %collective-permute-done.5), kind=kLoop, calls=%fused_computation.2 | loop fusion | flops 655360 | bytes 1835009 | tf_op jit(solution)/shard_map/add | solution.py:285
  59.9 1.6 %collective-permute-start.13 = (bf16[16,4096]{1,0:T(8,128)(2,1)S(1)}, bf16[16,4096]{1,0:T(8,128)(2,1)S(1)}, u32[]{:S(2)}, u32[]{:S(2)}) collective-permute-start(bf16[16,4096]{1,0:T(8,128)(2,1)S(1)} %select_convert_fusion.2), channel_id=1, source_target_pairs={{0,1},{1,0},{2,3},{3,2},{4,5},{5,4},{6,7},{7,6},{8,9},{9,8},{10,11... | collective-permute-start | bytes 393224 | tf_op jit(solution)/shard_map/ppermute | solution.py:71
  61.5 1.2 %collective-permute-done.9 = bf16[32,4096]{1,0:T(8,128)(2,1)S(1)} collective-permute-done((bf16[32,4096]{1,0:T(8,128)(2,1)S(1)}, bf16[32,4096]{1,0:T(8,128)(2,1)S(1)}, u32[]{:S(2)}, u32[]{:S(2)}) %collective-permute-start.9) | collective-permute-done | bytes 262176 | tf_op jit(solution)/shard_map/ppermute | solution.py:67
  62.7 1.1 %convert_add_fusion.1 = f32[32,4096]{1,0:T(8,128)S(1)} fusion(bf16[32,4096]{1,0:T(8,128)(2,1)S(1)} %collective-permute-done.9, f32[32,4096]{1,0:T(8,128)S(1)} %get-tuple-element.34, bf16[32,4096]{1,0:T(8,128)(2,1)S(1)} %collective-permute-done.7, pred[]{:T(512)} %eq.30, bf16[96,4096]{1,0:T(8,128)(2,1)} %collective-permute-done.5), kind=kLoop, calls=%fused_computation.1 | loop fusion | flops 655360 | bytes 1835009 | tf_op jit(solution)/shard_map/add | solution.py:285
  63.8 1.6 %collective-permute-start.12 = (bf16[16,4096]{1,0:T(8,128)(2,1)S(1)}, bf16[16,4096]{1,0:T(8,128)(2,1)S(1)}, u32[]{:S(2)}, u32[]{:S(2)}) collective-permute-start(bf16[16,4096]{1,0:T(8,128)(2,1)S(1)} %select_convert_fusion.1), channel_id=1, source_target_pairs={{0,1},{1,0},{2,3},{3,2},{4,5},{5,4},{6,7},{7,6},{8,9},{9,8},{10,11... | collective-permute-start | bytes 393224 | tf_op jit(solution)/shard_map/ppermute | solution.py:71
  65.4 0.1 collective-permute-done.14
  65.5 1.1 %convert_add_fusion = f32[32,4096]{1,0:T(8,128)S(1)} fusion(bf16[32,4096]{1,0:T(8,128)(2,1)S(1)} %collective-permute-done.14, f32[32,4096]{1,0:T(8,128)S(1)} %get-tuple-element.42, bf16[32,4096]{1,0:T(8,128)(2,1)S(1)} %collective-permute-done.11, pred[]{:T(512)} %eq.30, bf16[96,4096]{1,0:T(8,128)(2,1)} %collective-permute-done.5), kind=kLoop, calls=%fused_computation | loop fusion | flops 655360 | bytes 1835009 | tf_op jit(solution)/shard_map/add | solution.py:285
  66.6 1.6 %collective-permute-start.17 = (bf16[16,4096]{1,0:T(8,128)(2,1)S(1)}, bf16[16,4096]{1,0:T(8,128)(2,1)S(1)}, u32[]{:S(2)}, u32[]{:S(2)}) collective-permute-start(bf16[16,4096]{1,0:T(8,128)(2,1)S(1)} %select_convert_fusion), channel_id=1, source_target_pairs={{0,1},{1,0},{2,3},{3,2},{4,5},{5,4},{6,7},{7,6},{8,9},{9,8},{10,11... | collective-permute-start | bytes 393224 | tf_op jit(solution)/shard_map/ppermute | solution.py:71
  68.3 2.5 %collective-permute-start.16 = (bf16[16,4096]{1,0:T(8,128)(2,1)S(1)}, bf16[16,4096]{1,0:T(8,128)(2,1)S(1)}, u32[]{:S(2)}, u32[]{:S(2)}) collective-permute-start(bf16[16,4096]{1,0:T(8,128)(2,1)S(1)} %fusion.4), channel_id=1, source_target_pairs={{0,3},{3,0},{1,2},{2,1},{4,7},{7,4},{5,6},{6,5},{8,11},{11,8},{9,1... | collective-permute-start | bytes 393224 | tf_op jit(solution)/shard_map/ppermute | solution.py:71
  70.8 0.0 collective-permute-done.12
  70.8 3.2 %collective-permute-start.15 = (bf16[16,4096]{1,0:T(8,128)(2,1)S(1)}, bf16[16,4096]{1,0:T(8,128)(2,1)S(1)}, u32[]{:S(2)}, u32[]{:S(2)}) collective-permute-start(bf16[16,4096]{1,0:T(8,128)(2,1)S(1)} %fusion.5), channel_id=1, source_target_pairs={{0,3},{3,0},{1,2},{2,1},{4,7},{7,4},{5,6},{6,5},{8,11},{11,8},{9,1... | collective-permute-start | bytes 393224 | tf_op jit(solution)/shard_map/ppermute | solution.py:71
  74.1 5.6 %collective-permute-start.20 = (bf16[16,4096]{1,0:T(8,128)(2,1)S(1)}, bf16[16,4096]{1,0:T(8,128)(2,1)S(1)}, u32[]{:S(2)}, u32[]{:S(2)}) collective-permute-start(bf16[16,4096]{1,0:T(8,128)(2,1)S(1)} %fusion.6), channel_id=1, source_target_pairs={{0,3},{3,0},{1,2},{2,1},{4,7},{7,4},{5,6},{6,5},{8,11},{11,8},{9,1... | collective-permute-start | bytes 393224 | tf_op jit(solution)/shard_map/ppermute | solution.py:71
  79.7 0.1 add_convert_fusion.5
  79.8 0.3 collective-permute-start.19
  80.0 0.7 collective-permute-done.15
  80.7 0.1 add_convert_fusion.4
  80.8 2.8 %collective-permute-start.18 = (bf16[16,4096]{1,0:T(8,128)(2,1)S(1)}, bf16[16,4096]{1,0:T(8,128)(2,1)S(1)}, u32[]{:S(2)}, u32[]{:S(2)}) collective-permute-start(bf16[16,4096]{1,0:T(8,128)(2,1)S(1)} %add_convert_fusion.4), channel_id=1, source_target_pairs={{0,1},{1,0},{2,3},{3,2},{4,5},{5,4},{6,7},{7,6},{8,9},{9,8},{10,11... | collective-permute-start | bytes 393224 | tf_op jit(solution)/shard_map/ppermute | solution.py:71
  83.6 0.1 add_convert_fusion.3
  83.6 1.3 %collective-permute-start.21 = (bf16[16,4096]{1,0:T(8,128)(2,1)S(1)}, bf16[16,4096]{1,0:T(8,128)(2,1)S(1)}, u32[]{:S(2)}, u32[]{:S(2)}) collective-permute-start(bf16[16,4096]{1,0:T(8,128)(2,1)S(1)} %add_convert_fusion.3), channel_id=1, source_target_pairs={{0,1},{1,0},{2,3},{3,2},{4,5},{5,4},{6,7},{7,6},{8,9},{9,8},{10,11... | collective-permute-start | bytes 393224 | tf_op jit(solution)/shard_map/ppermute | solution.py:71
  85.0 0.4 collective-permute-done.19
  85.4 0.7 pad_maximum_fusion
  86.1 0.7 collective-permute-done.18
  86.8 0.7 pad_maximum_fusion.1
  87.6 1.1 %collective-permute-done.21 = bf16[16,4096]{1,0:T(8,128)(2,1)S(1)} collective-permute-done((bf16[16,4096]{1,0:T(8,128)(2,1)S(1)}, bf16[16,4096]{1,0:T(8,128)(2,1)S(1)}, u32[]{:S(2)}, u32[]{:S(2)}) %collective-permute-start.21) | collective-permute-done | bytes 131104 | tf_op jit(solution)/shard_map/ppermute | solution.py:71
  88.7 0.7 pad_maximum_fusion.2
  (23 shorter events, 0.3 us)
Async XLA Ops:
  0.6 6.1 %collective-permute-start.2 = (bf16[192,4096]{1,0:T(8,128)(2,1)}, bf16[192,4096]{1,0:T(8,128)(2,1)}, u32[]{:S(2)}, u32[]{:S(2)}) collective-permute-start(bf16[192,4096]{1,0:T(8,128)(2,1)} %refs_0_.4), channel_id=1, source_target_pairs={{0,4},{4,0},{8,12},{12,8},{16,20},{20,16},{24,28},{28,24},{1,5},{5... | collective-permute-start | bytes 4718600 | tf_op jit(solution)/shard_map/ppermute | solution.py:67
  1.1 7.5 %collective-permute-start.3 = (bf16[192,4096]{1,0:T(8,128)(2,1)}, bf16[192,4096]{1,0:T(8,128)(2,1)}, u32[]{:S(2)}, u32[]{:S(2)}) collective-permute-start(bf16[192,4096]{1,0:T(8,128)(2,1)} %refs_0_.5), channel_id=1, source_target_pairs={{0,4},{4,0},{8,12},{12,8},{16,20},{20,16},{24,28},{28,24},{1,5},{5... | collective-permute-start | bytes 4718600 | tf_op jit(solution)/shard_map/ppermute | solution.py:67
  3.3 7.3 %collective-permute-start.1 = (bf16[96,4096]{1,0:T(8,128)(2,1)}, bf16[96,4096]{1,0:T(8,128)(2,1)}, u32[]{:S(2)}, u32[]{:S(2)}) collective-permute-start(bf16[96,4096]{1,0:T(8,128)(2,1)} %shard_map.76), channel_id=1, source_target_pairs={{0,4},{4,0},{8,28},{12,8},{16,20},{20,16},{24,12},{28,24},{1,5},{5... | collective-permute-start | bytes 2359304 | tf_op jit(solution)/shard_map/ppermute | solution.py:196
  3.8 12.6 %collective-permute-start = (bf16[96,4096]{1,0:T(8,128)(2,1)}, bf16[96,4096]{1,0:T(8,128)(2,1)}, u32[]{:S(2)}, u32[]{:S(2)}) collective-permute-start(bf16[96,4096]{1,0:T(8,128)(2,1)} %shard_map.76), channel_id=1, source_target_pairs={{0,20},{4,8},{8,12},{12,0},{16,4},{20,24},{24,28},{28,16},{1,21},{... | collective-permute-start | bytes 2359304 | tf_op jit(solution)/shard_map/ppermute | solution.py:196
  10.5 18.6 %copy-start = (bf16[384,4096]{1,0:T(8,128)(2,1)}, bf16[384,4096]{1,0:T(8,128)(2,1)S(1)}, u32[]{:S(2)}) copy-start(bf16[384,4096]{1,0:T(8,128)(2,1)S(1)} %shard_map.78.refs_4_.refs_3_) | copy-start | bytes 9437188
  10.6 18.5 %collective-permute-start.6 = (bf16[96,4096]{1,0:T(8,128)(2,1)}, bf16[96,4096]{1,0:T(8,128)(2,1)S(1)}, u32[]{:S(2)}, u32[]{:S(2)}) collective-permute-start(bf16[96,4096]{1,0:T(8,128)(2,1)} %collective-permute-done.1.refs_1_), channel_id=1, source_target_pairs={{0,16},{4,12},{8,24},{12,4},{16,0},{20,28},{24,8},{28,20},{1,17},{... | collective-permute-start | bytes 2359304 | tf_op jit(solution)/shard_map/ppermute | solution.py:67
  21.9 14.6 %collective-permute-start.4 = (bf16[96,4096]{1,0:T(8,128)(2,1)}, bf16[96,4096]{1,0:T(8,128)(2,1)}, u32[]{:S(2)}, u32[]{:S(2)}) collective-permute-start(bf16[96,4096]{1,0:T(8,128)(2,1)} %collective-permute-done.refs_2_), channel_id=1, source_target_pairs={{0,16},{8,24},{16,0},{24,8},{1,17},{9,25},{17,1},{25,9},{2,18},{10... | collective-permute-start | bytes 2359304 | tf_op jit(solution)/shard_map/ppermute | solution.py:67
  25.6 23.2 %collective-permute-start.5 = (bf16[96,4096]{1,0:T(8,128)(2,1)}, bf16[96,4096]{1,0:T(8,128)(2,1)}, u32[]{:S(2)}, u32[]{:S(2)}) collective-permute-start(bf16[96,4096]{1,0:T(8,128)(2,1)} %get-tuple-element.35), channel_id=1, source_target_pairs={{0,8},{8,0},{16,24},{24,16},{1,9},{9,1},{17,25},{25,17},{2,10},{10... | collective-permute-start | bytes 2359304 | tf_op jit(solution)/shard_map/ppermute | solution.py:67
  33.1 0.7 copy-start.2
  33.8 0.7 copy-start.4
  34.5 14.3 %collective-permute-start.8 = (bf16[32,4096]{1,0:T(8,128)(2,1)}, bf16[32,4096]{1,0:T(8,128)(2,1)}, u32[]{:S(2)}, u32[]{:S(2)}) collective-permute-start(bf16[32,4096]{1,0:T(8,128)(2,1)} %get-tuple-element.39), channel_id=1, source_target_pairs={{0,8},{4,12},{8,0},{12,4},{16,24},{20,28},{24,16},{28,20},{1,9},{5... | collective-permute-start | bytes 786440 | tf_op jit(solution)/shard_map/ppermute | solution.py:67
  34.9 18.8 %collective-permute-start.7 = (bf16[32,4096]{1,0:T(8,128)(2,1)}, bf16[32,4096]{1,0:T(8,128)(2,1)S(1)}, u32[]{:S(2)}, u32[]{:S(2)}) collective-permute-start(bf16[32,4096]{1,0:T(8,128)(2,1)} %copy-done.4), channel_id=1, source_target_pairs={{0,8},{4,12},{8,0},{12,4},{16,24},{20,28},{24,16},{28,20},{1,9},{5... | collective-permute-start | bytes 786440 | tf_op jit(solution)/shard_map/ppermute | solution.py:67
  36.5 1.9 %copy-start.1 = (bf16[384,4096]{1,0:T(8,128)(2,1)S(1)}, bf16[384,4096]{1,0:T(8,128)(2,1)}, u32[]{:S(2)}) copy-start(bf16[384,4096]{1,0:T(8,128)(2,1)} %copy-done) | copy-start | bytes 9437188
  38.4 4.5 %copy-start.3 = (bf16[32,4096]{1,0:T(8,128)(2,1)S(1)}, bf16[32,4096]{1,0:T(8,128)(2,1)}, u32[]{:S(2)}) copy-start(bf16[32,4096]{1,0:T(8,128)(2,1)} %copy-done.2) | copy-start | bytes 786436
  42.8 13.7 %collective-permute-start.11 = (bf16[32,4096]{1,0:T(8,128)(2,1)S(1)}, bf16[32,4096]{1,0:T(8,128)(2,1)S(1)}, u32[]{:S(2)}, u32[]{:S(2)}) collective-permute-start(bf16[32,4096]{1,0:T(8,128)(2,1)S(1)} %copy-done.3), channel_id=1, source_target_pairs={{0,8},{4,12},{8,0},{12,4},{16,24},{20,28},{24,16},{28,20},{1,9},{5... | collective-permute-start | bytes 786440 | tf_op jit(solution)/shard_map/ppermute | solution.py:67
  49.9 8.9 %collective-permute-start.10 = (bf16[32,4096]{1,0:T(8,128)(2,1)S(1)}, bf16[32,4096]{1,0:T(8,128)(2,1)S(1)}, u32[]{:S(2)}, u32[]{:S(2)}) collective-permute-start(bf16[32,4096]{1,0:T(8,128)(2,1)S(1)} %add_convert_fusion.2), channel_id=1, source_target_pairs={{0,16},{4,20},{8,24},{12,28},{16,0},{20,4},{24,8},{28,12},{1,17},{... | collective-permute-start | bytes 786440 | tf_op jit(solution)/shard_map/ppermute | solution.py:67
  54.8 7.9 %collective-permute-start.9 = (bf16[32,4096]{1,0:T(8,128)(2,1)S(1)}, bf16[32,4096]{1,0:T(8,128)(2,1)S(1)}, u32[]{:S(2)}, u32[]{:S(2)}) collective-permute-start(bf16[32,4096]{1,0:T(8,128)(2,1)S(1)} %add_convert_fusion.1), channel_id=1, source_target_pairs={{0,16},{4,20},{8,24},{12,28},{16,0},{20,4},{24,8},{28,12},{1,17},{... | collective-permute-start | bytes 786440 | tf_op jit(solution)/shard_map/ppermute | solution.py:67
  57.6 7.9 %collective-permute-start.14 = (bf16[32,4096]{1,0:T(8,128)(2,1)S(1)}, bf16[32,4096]{1,0:T(8,128)(2,1)S(1)}, u32[]{:S(2)}, u32[]{:S(2)}) collective-permute-start(bf16[32,4096]{1,0:T(8,128)(2,1)S(1)} %add_convert_fusion), channel_id=1, source_target_pairs={{0,16},{4,20},{8,24},{12,28},{16,0},{20,4},{24,8},{28,12},{1,17},{... | collective-permute-start | bytes 786440 | tf_op jit(solution)/shard_map/ppermute | solution.py:67
  59.9 8.4 %collective-permute-start.13 = (bf16[16,4096]{1,0:T(8,128)(2,1)S(1)}, bf16[16,4096]{1,0:T(8,128)(2,1)S(1)}, u32[]{:S(2)}, u32[]{:S(2)}) collective-permute-start(bf16[16,4096]{1,0:T(8,128)(2,1)S(1)} %select_convert_fusion.2), channel_id=1, source_target_pairs={{0,1},{1,0},{2,3},{3,2},{4,5},{5,4},{6,7},{7,6},{8,9},{9,8},{10,11... | collective-permute-start | bytes 393224 | tf_op jit(solution)/shard_map/ppermute | solution.py:71
  63.8 7.0 %collective-permute-start.12 = (bf16[16,4096]{1,0:T(8,128)(2,1)S(1)}, bf16[16,4096]{1,0:T(8,128)(2,1)S(1)}, u32[]{:S(2)}, u32[]{:S(2)}) collective-permute-start(bf16[16,4096]{1,0:T(8,128)(2,1)S(1)} %select_convert_fusion.1), channel_id=1, source_target_pairs={{0,1},{1,0},{2,3},{3,2},{4,5},{5,4},{6,7},{7,6},{8,9},{9,8},{10,11... | collective-permute-start | bytes 393224 | tf_op jit(solution)/shard_map/ppermute | solution.py:71
  66.6 7.4 %collective-permute-start.17 = (bf16[16,4096]{1,0:T(8,128)(2,1)S(1)}, bf16[16,4096]{1,0:T(8,128)(2,1)S(1)}, u32[]{:S(2)}, u32[]{:S(2)}) collective-permute-start(bf16[16,4096]{1,0:T(8,128)(2,1)S(1)} %select_convert_fusion), channel_id=1, source_target_pairs={{0,1},{1,0},{2,3},{3,2},{4,5},{5,4},{6,7},{7,6},{8,9},{9,8},{10,11... | collective-permute-start | bytes 393224 | tf_op jit(solution)/shard_map/ppermute | solution.py:71
  68.3 11.4 %collective-permute-start.16 = (bf16[16,4096]{1,0:T(8,128)(2,1)S(1)}, bf16[16,4096]{1,0:T(8,128)(2,1)S(1)}, u32[]{:S(2)}, u32[]{:S(2)}) collective-permute-start(bf16[16,4096]{1,0:T(8,128)(2,1)S(1)} %fusion.4), channel_id=1, source_target_pairs={{0,3},{3,0},{1,2},{2,1},{4,7},{7,4},{5,6},{6,5},{8,11},{11,8},{9,1... | collective-permute-start | bytes 393224 | tf_op jit(solution)/shard_map/ppermute | solution.py:71
  70.8 9.9 %collective-permute-start.15 = (bf16[16,4096]{1,0:T(8,128)(2,1)S(1)}, bf16[16,4096]{1,0:T(8,128)(2,1)S(1)}, u32[]{:S(2)}, u32[]{:S(2)}) collective-permute-start(bf16[16,4096]{1,0:T(8,128)(2,1)S(1)} %fusion.5), channel_id=1, source_target_pairs={{0,3},{3,0},{1,2},{2,1},{4,7},{7,4},{5,6},{6,5},{8,11},{11,8},{9,1... | collective-permute-start | bytes 393224 | tf_op jit(solution)/shard_map/ppermute | solution.py:71
  74.1 9.5 %collective-permute-start.20 = (bf16[16,4096]{1,0:T(8,128)(2,1)S(1)}, bf16[16,4096]{1,0:T(8,128)(2,1)S(1)}, u32[]{:S(2)}, u32[]{:S(2)}) collective-permute-start(bf16[16,4096]{1,0:T(8,128)(2,1)S(1)} %fusion.6), channel_id=1, source_target_pairs={{0,3},{3,0},{1,2},{2,1},{4,7},{7,4},{5,6},{6,5},{8,11},{11,8},{9,1... | collective-permute-start | bytes 393224 | tf_op jit(solution)/shard_map/ppermute | solution.py:71
  79.8 5.6 %collective-permute-start.19 = (bf16[16,4096]{1,0:T(8,128)(2,1)S(1)}, bf16[16,4096]{1,0:T(8,128)(2,1)S(1)}, u32[]{:S(2)}, u32[]{:S(2)}) collective-permute-start(bf16[16,4096]{1,0:T(8,128)(2,1)S(1)} %add_convert_fusion.5), channel_id=1, source_target_pairs={{0,1},{1,0},{2,3},{3,2},{4,5},{5,4},{6,7},{7,6},{8,9},{9,8},{10,11... | collective-permute-start | bytes 393224 | tf_op jit(solution)/shard_map/ppermute | solution.py:71
  80.8 6.0 %collective-permute-start.18 = (bf16[16,4096]{1,0:T(8,128)(2,1)S(1)}, bf16[16,4096]{1,0:T(8,128)(2,1)S(1)}, u32[]{:S(2)}, u32[]{:S(2)}) collective-permute-start(bf16[16,4096]{1,0:T(8,128)(2,1)S(1)} %add_convert_fusion.4), channel_id=1, source_target_pairs={{0,1},{1,0},{2,3},{3,2},{4,5},{5,4},{6,7},{7,6},{8,9},{9,8},{10,11... | collective-permute-start | bytes 393224 | tf_op jit(solution)/shard_map/ppermute | solution.py:71
  83.6 5.0 %collective-permute-start.21 = (bf16[16,4096]{1,0:T(8,128)(2,1)S(1)}, bf16[16,4096]{1,0:T(8,128)(2,1)S(1)}, u32[]{:S(2)}, u32[]{:S(2)}) collective-permute-start(bf16[16,4096]{1,0:T(8,128)(2,1)S(1)} %add_convert_fusion.3), channel_id=1, source_target_pairs={{0,1},{1,0},{2,3},{3,2},{4,5},{5,4},{6,7},{7,6},{8,9},{9,8},{10,11... | collective-permute-start | bytes 393224 | tf_op jit(solution)/shard_map/ppermute | solution.py:71

commit v4 on v3

--- a/solution.py
+++ b/solution.py
@@ -124,12 +124,12 @@
         + [pl.BlockSpec(memory_space=pltpu.VMEM)] * len(arrays),
         out_specs=[pl.BlockSpec(memory_space=pltpu.VMEM)] * len(outs),
         compiler_params=pltpu.CompilerParams(vmem_limit_bytes=VMEM_LIMIT),
-        cost_estimate=pl.CostEstimate(flops=1, bytes_accessed=1, transcendentals=0),
+        cost_estimate=pl.CostEstimate(flops=1, bytes_accessed=8388608, transcendentals=0),
     )(flags, *arrays[:-2], *held)
 
 
 def span_dot(weights, low, high, sources):
-    totals = [None, None]
+    totals = [None] * len(sources)
     for at in range(0, sources[0].shape[1], SPAN):
         columns = slice(at, at + SPAN)
         left = [ref[low:high, columns] for ref in weights]
@@ -144,8 +144,10 @@
 def sums_into(lefts, sources, outs):
     for at in range(0, sources[0].shape[1], SPAN):
         columns = slice(at, at + SPAN)
-        part = rows_dot(lefts[0], sources[0][:, columns])
-        part = part + rows_dot(lefts[1], sources[1][:, columns])
+        part = None
+        for left, source in zip(lefts, sources):
+            one = rows_dot(left, source[:, columns])
+            part = one if part is None else part + one
         row = 0
         for ref in outs:
             rows = ref.shape[0]
@@ -161,7 +163,7 @@
     for which in range(len(weights)):
         pair = []
         row = which * block
-        for at in range(2):
+        for at in range(len(tokens)):
             gate_sum = sums[at][2 * row : 2 * row + block]
             up_sum = sums[at][2 * row + block : 2 * row + 2 * block]
             back = backs[at][row : row + block]
@@ -169,8 +171,10 @@
             activated = gate_sum * squash
             slope = up_sum * squash * (1.0 + gate_sum * (1.0 - squash))
             parts = [back * slope, back * activated, activated * up_sum]
-            meets = flags[flag + 2 * which + at] != 0
-            pair.append(jnp.where(meets, jnp.concatenate(parts), 0.0).astype(BF16))
+            part = jnp.concatenate(parts)
+            if flag is not None:
+                part = jnp.where(flags[flag + 2 * which + at] != 0, part, 0.0)
+            pair.append(part.astype(BF16))
         found.append(pair)
     return found
 
@@ -216,13 +220,16 @@
 
     low, high = slice(0, 2 * block), slice(2 * block, 3 * block)
 
-    def of_v_u(flags, v, u, t0, t1, c0, c1, found, p_out):
+    def of_pair(flags, own, t0, t1, c0, c1, p_out):
+        (pair,) = products(flags, None, [own], (t1,), (c1,))
+        sums_into([pair[0][high]], (c1,), [p_out.at[high]])
+        sums_into([pair[0][low]], (t1,), [p_out.at[low]])
+
+    def of_v_u(flags, v, u, t0, t1, c0, c1, found):
         pairs = products(flags, 0, [v, u], (t0, t1), (c0, c1))
         for which in range(2):
             for at in range(2):
                 found[2 * which + at] = pairs[which][at]
-        sums_into([part[high] for part in pairs[0]], (c0, c1), [p_out.at[high]])
-        sums_into([part[low] for part in pairs[0]], (t0, t1), [p_out.at[low]])
 
     def of_s(flags, s, t0, t1, c0, c1, gate, up, down):
         (pair,) = products(flags, 4, [s], (t0, t1), (c0, c1))
@@ -249,22 +256,22 @@
     tokens_in = hop(tokens, lambda i: CORE)
     cotangent_in = hop(cotangent, lambda i: CORE)
     own = on_chip(gate_weight, up_weight, down_weight)
+    w_p = hop(own, lambda i: CORE)
     w_v, w_u = spread(own)
     here = [on_chip(tokens, tokens_in), on_chip(cotangent, cotangent_in)]
-    w_s = hop(after(w_v, here), other)
-    found, p = kernel_call(
-        of_v_u,
-        [((4, 3 * block, tok), BF16), ((3 * block, width), BF16)],
-        flags, w_v, w_u, *here,
+    (p,) = kernel_call(of_pair, [((3 * block, width), BF16)], flags, w_p, *here)
+    w_s = hop(after(w_v, p), other)
+    p = hop(p, lambda i: X, 0)
+    (found,) = kernel_call(
+        of_v_u, [((4, 3 * block, tok), BF16)], flags, w_v, w_u, *here
     )
     w_e = hop(after(w_u, found), lambda i: Y, 0)
     order = (2, 0, 1)
-    p = hop(p, lambda i: X, 0)
     p_in = [p[k * block : (k + 1) * block] for k in range(3)]
     q = kernel_call(of_s, [narrow] * 3, flags, w_s, *here)
     there = {k: hop(q[k], lambda i: X) for k in order[:2]}
     sums = kernel_call(of_e, [wide] * 6, flags, w_e, found, *here)
-    there[order[2]] = hop(after(q[order[2]], sums), lambda i: X)
+    there[order[2]] = hop(q[order[2]], lambda i: X)
     leave, stay = sums[:3], sums[3:]
 
     turn = (sums,)
@@ -279,6 +286,7 @@
         out = (leave[k] + jnp.where(even, q_got, p_got).astype(F32)).astype(BF16)
         r[k] = hop(out, lambda i: Y)
         totals[k] = stay[k] + jnp.where(even, p_got, q_got).astype(F32)
+        totals[k] = lax.optimization_barrier(totals[k])
         return out
 
     def swap_stage(k):
@@ -308,7 +316,7 @@
         return results[k]
 
     stages = [leave_stage, swap_stage, across_stage, back_stage, result_stage]
-    steps = [(k, at) for at in range(5) for k in range(3)]
+    steps = ((0, 0), (1, 0), (0, 1), (2, 0), (1, 1), (0, 2), (2, 1), (1, 2), (2, 2), (0, 3), (1, 3), (2, 3), (0, 4), (1, 4), (2, 4))
     for k, at in steps:
         turn = stages[at](order[k])
     return results[0], results[1], results[2]

time: 89.9 us -> 86.3 us (0.960)
  starting transfers between devices: 40.3 us -> 32.6 us
  waiting for transfers between devices: 15.8 us -> 20.5 us
  other arithmetic: 9.31 us -> 6.37 us
  Pallas kernels: 19.8 us -> 22.1 us
    ppermute x9, waiting for transfers between devices: 2.92 us -> 11 us  [along(): return lax.ppermute(block, 'dp', route)]
    ppermute x9, starting transfers between devices: 20.6 us -> 13.6 us  [along(): return lax.ppermute(block, 'dp', route)]
    ppermute x2, waiting for transfers between devices: 4.6 us -> 0.01 us  [spread(): return (lax.ppermute(own, 'section', v), lax.ppermute(own, 'section', u))]
    add x3, other arithmetic: 3.17 us -> 0.14 us  [swap_stage(): total = totals[k] + take(r[k]).astype(F32)]
    pallas_call x3 -> x4, Pallas kernels: 14 us -> 16.3 us  [kernel_call(): pl.pallas_call(inner, out_shape=[jax.ShapeDtypeStruct(shape, dtype) for s...]
    add x0 -> x2, other arithmetic: none -> 2.21 us  [leave_stage(): totals[k] = stay[k] + jnp.where(even, p_got, q_got).astype(F32)]
    convert_element_type x3 -> x1, other arithmetic: 3.21 us -> 1.07 us  [leave_stage(): out = (leave[k] + jnp.where(even, q_got, p_got).astype(F32)).astype(BF16)]
    ppermute x11 -> x12, waiting for transfers between devices: 8.24 us -> 9.48 us  [hop(): return lax.ppermute(block, 'section', route)]
  transfers between devices with their start and end apart: 22 -> 23, of which waited for: 10 -> 12; matrix products, arithmetic and copies ran while one was open for 10% -> 7% of each run, Pallas kernels for 22% -> 26%
where the time goes in v4:
time: 86.3 us; the launch traced here: 85.8 us
  starting transfers between devices  32.6 us (38%)
  Pallas kernels  22.1 us (26%)
  waiting for transfers between devices  20.5 us (24%)
  other arithmetic  6.37 us (7%)
  local copies, waits for them, and re-layouts  3.38 us (4%)
    pallas_call x4, Pallas kernels, kernel_call(): pl.pallas_call(inner, out_shape=[jax.ShapeDtypeStruct(shape, dtype) for s...  16.3 us
    ppermute x12, starting transfers between devices, hop(): return lax.ppermute(block, 'section', route)  15.9 us
    ppermute x9, starting transfers between devices, along(): return lax.ppermute(block, 'dp', route)  13.6 us
    ppermute x9, waiting for transfers between devices, along(): return lax.ppermute(block, 'dp', route)  11 us
    ppermute x12, waiting for transfers between devices, hop(): return lax.ppermute(block, 'section', route)  9.48 us
    pallas_call x3, Pallas kernels, on_chip(): pl.pallas_call(kernel, out_shape=pltpu.VMEM((rows, parts[0].shape[1]), pa...  5.85 us
    unnamed x8, local copies, waits for them, and re-layouts  3.3 us
    ppermute x2, starting transfers between devices, spread(): return (lax.ppermute(own, 'section', v), lax.ppermute(own, 'section', u))  3.08 us
  transfers between devices with their start and end apart: 23, of which 12 were waited for; matrix products, arithmetic and copies ran while one was open for 7% of the time, Pallas kernels for 26%

profile of v4, /device:TPU:0, one launch (start us, length us, event | category | flops | bytes accessed | tf_op | source)
XLA Modules:
  0.0 85.8 jit_solution(610012272632134804)
XLA Ops:
  0.6 0.5 collective-permute-start.2
  1.1 0.1 collective-permute-start.3
  1.2 2.0 %shard_map.76 = bf16[96,4096]{1,0:T(8,128)(2,1)} custom-call(bf16[32,4096]{1,0:T(8,128)(2,1)} %refs_0_.3, bf16[32,4096]{1,0:T(8,128)(2,1)} %refs_1_.1, bf16[32,4096]{1,0:T(8,128)(2,1)} %refs_2_.1), custom_call_target="tpu_custom_call" | custom-call | flops 1 | bytes 1 | tf_op jit(solution)/shard_map/pallas_call | solution.py:100
  3.3 2.7 %collective-permute-start = (bf16[96,4096]{1,0:T(8,128)(2,1)}, bf16[96,4096]{1,0:T(8,128)(2,1)}, u32[]{:S(2)}, u32[]{:S(2)}) collective-permute-start(bf16[96,4096]{1,0:T(8,128)(2,1)} %shard_map.76), channel_id=1, source_target_pairs={{0,20},{4,8},{8,12},{12,0},{16,4},{20,24},{24,28},{28,16},{1,21},{... | collective-permute-start | bytes 2359304 | tf_op jit(solution)/shard_map/ppermute | solution.py:200
  6.0 0.4 collective-permute-start.1
  6.4 0.1 collective-permute-start.5
  6.5 0.1 pad_add_fusion
  6.6 0.1 fusion.3
  6.6 0.1 broadcast_subtract_fusion
  6.7 0.1 sub.37
  6.8 0.1 add_convert_fusion.6.refs_0_
  6.9 1.9 %shard_map.77.refs_3_.refs_2_ = bf16[384,4096]{1,0:T(8,128)(2,1)S(1)} custom-call(bf16[192,4096]{1,0:T(8,128)(2,1)} %refs_0_.4, bf16[192,4096]{1,0:T(8,128)(2,1)} %collective-permute-done.2.refs_1_), custom_call_target="tpu_custom_call" | custom-call | flops 1 | bytes 1 | tf_op jit(solution)/shard_map/pallas_call | solution.py:100
  8.8 0.0 collective-permute-done.3.refs_1_
  8.8 1.9 %shard_map.78.refs_4_.refs_3_ = bf16[384,4096]{1,0:T(8,128)(2,1)S(1)} custom-call(bf16[192,4096]{1,0:T(8,128)(2,1)} %refs_0_.5, bf16[192,4096]{1,0:T(8,128)(2,1)} %collective-permute-done.3.refs_1_), custom_call_target="tpu_custom_call" | custom-call | flops 1 | bytes 1 | tf_op jit(solution)/shard_map/pallas_call | solution.py:100
  10.7 4.4 %shard_map.81 = bf16[96,4096]{1,0:T(8,128)(2,1)} custom-call(s32[10]{0:T(128)S(1)} %add_convert_fusion.6.refs_0_, bf16[96,4096]{1,0:T(8,128)(2,1)} %collective-permute-done.5.refs_1_, bf16[384,4096]{1,0:T(8,128)(2,1)S(1)} %shard_map.77.refs_3_.refs_2_, bf16[384,4096]{1,0:T(8,128)(2,1)S(1)} %shard_map.78.refs_4_.refs_3_), custom_call_target="tpu_custom_call" | custom-call | flops 1 | bytes 8388608 | tf_op jit(solution)/shard_map/pallas_call | solution.py:120
  15.1 0.0 collective-permute-done.1.refs_1_
  15.2 1.4 %collective-permute-start.7 = (bf16[96,4096]{1,0:T(8,128)(2,1)}, bf16[96,4096]{1,0:T(8,128)(2,1)S(1)}, u32[]{:S(2)}, u32[]{:S(2)}) collective-permute-start(bf16[96,4096]{1,0:T(8,128)(2,1)} %collective-permute-done.1.refs_1_), channel_id=1, source_target_pairs={{0,16},{4,12},{8,24},{12,4},{16,0},{20,28},{24,8},{28,20},{1,17},{... | collective-permute-start | bytes 2359304 | tf_op jit(solution)/shard_map/ppermute | solution.py:67
  16.6 3.5 %shard_map.79.refs_2_ = bf16[4,96,192]{2,1,0:T(8,128)(2,1)S(1)} custom-call(s32[10]{0:T(128)S(1)} %add_convert_fusion.6.refs_0_, bf16[96,4096]{1,0:T(8,128)(2,1)} %collective-permute-done.1.refs_1_, bf16[96,4096]{1,0:T(8,128)(2,1)} %collective-permute-done.refs_2_, bf16[384,4096]{1,0:T(8,128)(2,1)S(1)} %shard_map.77.refs_3_.refs_2_, ...), custom_call_target="tpu_custom_call" | custom-call | flops 1 | bytes 8388608 | tf_op jit(solution)/shard_map/pallas_call | solution.py:120
  20.1 3.3 %collective-permute-start.4 = (bf16[96,4096]{1,0:T(8,128)(2,1)}, bf16[96,4096]{1,0:T(8,128)(2,1)}, u32[]{:S(2)}, u32[]{:S(2)}) collective-permute-start(bf16[96,4096]{1,0:T(8,128)(2,1)} %collective-permute-done.refs_2_), channel_id=1, source_target_pairs={{0,16},{8,24},{16,0},{24,8},{1,17},{9,25},{17,1},{25,9},{2,18},{10... | collective-permute-start | bytes 2359304 | tf_op jit(solution)/shard_map/ppermute | solution.py:67
  23.5 3.8 %collective-permute-start.6 = (bf16[96,4096]{1,0:T(8,128)(2,1)}, bf16[96,4096]{1,0:T(8,128)(2,1)}, u32[]{:S(2)}, u32[]{:S(2)}) collective-permute-start(bf16[96,4096]{1,0:T(8,128)(2,1)} %shard_map.81), channel_id=1, source_target_pairs={{0,8},{8,0},{16,24},{24,16},{1,9},{9,1},{17,25},{25,17},{2,10},{10... | collective-permute-start | bytes 2359304 | tf_op jit(solution)/shard_map/ppermute | solution.py:67
  27.3 0.1 collective-permute-done.7.refs_1_
  27.4 3.9 %shard_map.82 = (bf16[32,4096]{1,0:T(8,128)(2,1)S(1)}, bf16[32,4096]{1,0:T(8,128)(2,1)S(1)}, bf16[32,4096]{1,0:T(8,128)(2,1)}) custom-call(s32[10]{0:T(128)S(1)} %add_convert_fusion.6.refs_0_, bf16[96,4096]{1,0:T(8,128)(2,1)S(1)} %collective-permute-done.7.refs_1_, bf16[384,4096]{1,0:T(8,128)(2,1)S(1)} %shard_map.77.refs_3_.refs_2_, ...), custom_call_target="tpu_custom_call" | custom-call | flops 1 | bytes 8388608 | tf_op jit(solution)/shard_map/pallas_call | solution.py:120
  31.3 0.7 copy-done.2
  32.0 0.7 copy-done.3
  32.7 2.7 %collective-permute-start.9 = (bf16[32,4096]{1,0:T(8,128)(2,1)}, bf16[32,4096]{1,0:T(8,128)(2,1)}, u32[]{:S(2)}, u32[]{:S(2)}) collective-permute-start(bf16[32,4096]{1,0:T(8,128)(2,1)} %get-tuple-element.34), channel_id=1, source_target_pairs={{0,8},{4,12},{8,0},{12,4},{16,24},{20,28},{24,16},{28,20},{1,9},{5... | collective-permute-start | bytes 786440 | tf_op jit(solution)/shard_map/ppermute | solution.py:67
  35.4 0.0 collective-permute-start.8
  35.4 2.0 %collective-permute-start.11 = (bf16[32,4096]{1,0:T(8,128)(2,1)}, bf16[32,4096]{1,0:T(8,128)(2,1)S(1)}, u32[]{:S(2)}, u32[]{:S(2)}) collective-permute-start(bf16[32,4096]{1,0:T(8,128)(2,1)} %copy-done.2), channel_id=1, source_target_pairs={{0,8},{4,12},{8,0},{12,4},{16,24},{20,28},{24,16},{28,20},{1,9},{5... | collective-permute-start | bytes 786440 | tf_op jit(solution)/shard_map/ppermute | solution.py:67
  37.4 1.9 %copy-done.1 = bf16[384,4096]{1,0:T(8,128)(2,1)S(1)} copy-done((bf16[384,4096]{1,0:T(8,128)(2,1)S(1)}, bf16[384,4096]{1,0:T(8,128)(2,1)}, u32[]{:S(2)}) %copy-start.1) | copy-done | bytes 3145752
  39.3 4.4 %shard_map.80 = (f32[32,4096]{1,0:T(8,128)S(1)}, f32[32,4096]{1,0:T(8,128)S(1)}, f32[32,4096]{1,0:T(8,128)S(1)}, f32[32,4096]{1,0:T(8,128)S(1)}, f32[32,4096]{1,0:T(8,128)S(1)}, /*index=5*/f32[32,4096]{1,0:T(8,128)S(1)}) custom-call(s32[10]{0:T(128)S(1)} %add_convert_fusion.6.refs_0_, bf16[96,4096]{1,0:T(8,128)(2,1)} %collective-permute-done.4.refs_1_, ...), custom_call_target="tpu_custom_call" | custom-call | flops 1 | bytes 8388608 | tf_op jit(solution)/shard_map/pallas_call | solution.py:120
  43.7 1.1 %collective-permute-done.9 = bf16[32,4096]{1,0:T(8,128)(2,1)} collective-permute-done((bf16[32,4096]{1,0:T(8,128)(2,1)}, bf16[32,4096]{1,0:T(8,128)(2,1)}, u32[]{:S(2)}, u32[]{:S(2)}) %collective-permute-start.9) | collective-permute-done | bytes 262176 | tf_op jit(solution)/shard_map/ppermute | solution.py:67
  44.8 1.1 %convert_add_fusion.4 = (f32[32,4096]{1,0:T(8,128)S(1)}, bf16[32,4096]{1,0:T(8,128)(2,1)S(1)}) fusion(f32[32,4096]{1,0:T(8,128)S(1)} %get-tuple-element.38, bf16[32,4096]{1,0:T(8,128)(2,1)} %collective-permute-done.9, pred[]{:T(512)} %eq.30, bf16[96,4096]{1,0:T(8,128)(2,1)} %collective-permute-done.6, f32[32,4096]{1,0:T(8,128)S(1)} %get-tuple-element.33), kind=kLoop, calls=%fused_computation.5 | loop fusion | flops 917504 | bytes 2359297 | tf_op jit(solution)/shard_map/add | solution.py:288
  45.9 0.1 collective-permute-start.12
  46.0 4.3 %collective-permute-done.8 = bf16[32,4096]{1,0:T(8,128)(2,1)S(1)} collective-permute-done((bf16[32,4096]{1,0:T(8,128)(2,1)}, bf16[32,4096]{1,0:T(8,128)(2,1)S(1)}, u32[]{:S(2)}, u32[]{:S(2)}) %collective-permute-start.8) | collective-permute-done | bytes 262176 | tf_op jit(solution)/shard_map/ppermute | solution.py:67
  50.3 1.1 %add_convert_fusion.1 = (bf16[32,4096]{1,0:T(8,128)(2,1)S(1)}, f32[32,4096]{1,0:T(8,128)S(1)}) fusion(f32[32,4096]{1,0:T(8,128)S(1)} %get-tuple-element.35, bf16[32,4096]{1,0:T(8,128)(2,1)S(1)} %collective-permute-done.8, pred[]{:T(512)} %eq.30, bf16[96,4096]{1,0:T(8,128)(2,1)} %collective-permute-done.6, f32[32,4096]{1,0:T(8,128)S(1)} %get-tuple-element.30), kind=kLoop, calls=%fused_computation.6 | loop fusion | flops 917504 | bytes 2359297 | tf_op jit(solution)/shard_map/convert_element_type | solution.py:286
  51.4 0.1 collective-permute-start.10
  51.4 1.6 %collective-permute-done.12 = bf16[32,4096]{1,0:T(8,128)(2,1)S(1)} collective-permute-done((bf16[32,4096]{1,0:T(8,128)(2,1)S(1)}, bf16[32,4096]{1,0:T(8,128)(2,1)S(1)}, u32[]{:S(2)}, u32[]{:S(2)}) %collective-permute-start.12) | collective-permute-done | bytes 262176 | tf_op jit(solution)/shard_map/ppermute | solution.py:67
  53.2 1.4 %collective-permute-start.15 = (bf16[16,4096]{1,0:T(8,128)(2,1)S(1)}, bf16[16,4096]{1,0:T(8,128)(2,1)S(1)}, u32[]{:S(2)}, u32[]{:S(2)}) collective-permute-start(bf16[16,4096]{1,0:T(8,128)(2,1)S(1)} %select_convert_fusion.2), channel_id=1, source_target_pairs={{0,1},{1,0},{2,3},{3,2},{4,5},{5,4},{6,7},{7,6},{8,9},{9,8},{10,11... | collective-permute-start | bytes 393224 | tf_op jit(solution)/shard_map/ppermute | solution.py:71
  54.5 0.0 collective-permute-done.11
  54.6 1.1 %convert_add_fusion.1 = (f32[32,4096]{1,0:T(8,128)S(1)}, bf16[32,4096]{1,0:T(8,128)(2,1)S(1)}) fusion(f32[32,4096]{1,0:T(8,128)S(1)} %get-tuple-element.37, bf16[32,4096]{1,0:T(8,128)(2,1)S(1)} %collective-permute-done.11, pred[]{:T(512)} %eq.30, bf16[96,4096]{1,0:T(8,128)(2,1)} %collective-permute-done.6, f32[32,4096]{1,0:T(8,128)S(1)} %get-tuple-element.36), kind=kLoop, calls=%fused_computation.1 | loop fusion | flops 917504 | bytes 2359297 | tf_op jit(solution)/shard_map/add | solution.py:288
  55.6 1.8 %collective-permute-start.14 = (bf16[32,4096]{1,0:T(8,128)(2,1)S(1)}, bf16[32,4096]{1,0:T(8,128)(2,1)S(1)}, u32[]{:S(2)}, u32[]{:S(2)}) collective-permute-start(bf16[32,4096]{1,0:T(8,128)(2,1)S(1)} %get-tuple-element.56), channel_id=1, source_target_pairs={{0,16},{4,20},{8,24},{12,28},{16,0},{20,4},{24,8},{28,12},{1,17},{... | collective-permute-start | bytes 786440 | tf_op jit(solution)/shard_map/ppermute | solution.py:67
  57.4 1.5 %collective-permute-done.10 = bf16[32,4096]{1,0:T(8,128)(2,1)S(1)} collective-permute-done((bf16[32,4096]{1,0:T(8,128)(2,1)S(1)}, bf16[32,4096]{1,0:T(8,128)(2,1)S(1)}, u32[]{:S(2)}, u32[]{:S(2)}) %collective-permute-start.10) | collective-permute-done | bytes 262176 | tf_op jit(solution)/shard_map/ppermute | solution.py:67
  59.0 1.1 %collective-permute-start.13 = (bf16[16,4096]{1,0:T(8,128)(2,1)S(1)}, bf16[16,4096]{1,0:T(8,128)(2,1)S(1)}, u32[]{:S(2)}, u32[]{:S(2)}) collective-permute-start(bf16[16,4096]{1,0:T(8,128)(2,1)S(1)} %select_convert_fusion.1), channel_id=1, source_target_pairs={{0,1},{1,0},{2,3},{3,2},{4,5},{5,4},{6,7},{7,6},{8,9},{9,8},{10,11... | collective-permute-start | bytes 393224 | tf_op jit(solution)/shard_map/ppermute | solution.py:71
  60.2 0.0 collective-permute-done.15
  60.2 2.5 %collective-permute-start.17 = (bf16[16,4096]{1,0:T(8,128)(2,1)S(1)}, bf16[16,4096]{1,0:T(8,128)(2,1)S(1)}, u32[]{:S(2)}, u32[]{:S(2)}) collective-permute-start(bf16[16,4096]{1,0:T(8,128)(2,1)S(1)} %fusion.4), channel_id=1, source_target_pairs={{0,3},{3,0},{1,2},{2,1},{4,7},{7,4},{5,6},{6,5},{8,11},{11,8},{9,1... | collective-permute-start | bytes 393224 | tf_op jit(solution)/shard_map/ppermute | solution.py:71
  62.8 0.9 %collective-permute-done.14 = bf16[32,4096]{1,0:T(8,128)(2,1)S(1)} collective-permute-done((bf16[32,4096]{1,0:T(8,128)(2,1)S(1)}, bf16[32,4096]{1,0:T(8,128)(2,1)S(1)}, u32[]{:S(2)}, u32[]{:S(2)}) %collective-permute-start.14) | collective-permute-done | bytes 262176 | tf_op jit(solution)/shard_map/ppermute | solution.py:67
  63.7 1.5 %collective-permute-start.18 = (bf16[16,4096]{1,0:T(8,128)(2,1)S(1)}, bf16[16,4096]{1,0:T(8,128)(2,1)S(1)}, u32[]{:S(2)}, u32[]{:S(2)}) collective-permute-start(bf16[16,4096]{1,0:T(8,128)(2,1)S(1)} %select_convert_fusion), channel_id=1, source_target_pairs={{0,1},{1,0},{2,3},{3,2},{4,5},{5,4},{6,7},{7,6},{8,9},{9,8},{10,11... | collective-permute-start | bytes 393224 | tf_op jit(solution)/shard_map/ppermute | solution.py:71
  65.2 0.5 collective-permute-done.13
  65.7 2.2 %collective-permute-start.16 = (bf16[16,4096]{1,0:T(8,128)(2,1)S(1)}, bf16[16,4096]{1,0:T(8,128)(2,1)S(1)}, u32[]{:S(2)}, u32[]{:S(2)}) collective-permute-start(bf16[16,4096]{1,0:T(8,128)(2,1)S(1)} %fusion.5), channel_id=1, source_target_pairs={{0,3},{3,0},{1,2},{2,1},{4,7},{7,4},{5,6},{6,5},{8,11},{11,8},{9,1... | collective-permute-start | bytes 393224 | tf_op jit(solution)/shard_map/ppermute | solution.py:71
  68.0 3.1 %collective-permute-done.18 = bf16[16,4096]{1,0:T(8,128)(2,1)S(1)} collective-permute-done((bf16[16,4096]{1,0:T(8,128)(2,1)S(1)}, bf16[16,4096]{1,0:T(8,128)(2,1)S(1)}, u32[]{:S(2)}, u32[]{:S(2)}) %collective-permute-start.18) | collective-permute-done | bytes 131104 | tf_op jit(solution)/shard_map/ppermute | solution.py:71
  71.1 2.6 %collective-permute-start.21 = (bf16[16,4096]{1,0:T(8,128)(2,1)S(1)}, bf16[16,4096]{1,0:T(8,128)(2,1)S(1)}, u32[]{:S(2)}, u32[]{:S(2)}) collective-permute-start(bf16[16,4096]{1,0:T(8,128)(2,1)S(1)} %fusion.6), channel_id=1, source_target_pairs={{0,3},{3,0},{1,2},{2,1},{4,7},{7,4},{5,6},{6,5},{8,11},{11,8},{9,1... | collective-permute-start | bytes 393224 | tf_op jit(solution)/shard_map/ppermute | solution.py:71
  73.7 0.1 add_convert_fusion.5
  73.8 0.1 collective-permute-start.20
  73.9 0.0 collective-permute-done.16
  73.9 0.1 add_convert_fusion.4
  74.0 2.1 %collective-permute-start.19 = (bf16[16,4096]{1,0:T(8,128)(2,1)S(1)}, bf16[16,4096]{1,0:T(8,128)(2,1)S(1)}, u32[]{:S(2)}, u32[]{:S(2)}) collective-permute-start(bf16[16,4096]{1,0:T(8,128)(2,1)S(1)} %add_convert_fusion.4), channel_id=1, source_target_pairs={{0,1},{1,0},{2,3},{3,2},{4,5},{5,4},{6,7},{7,6},{8,9},{9,8},{10,11... | collective-permute-start | bytes 393224 | tf_op jit(solution)/shard_map/ppermute | solution.py:71
  76.0 3.4 %collective-permute-done.21 = bf16[16,4096]{1,0:T(8,128)(2,1)S(1)} collective-permute-done((bf16[16,4096]{1,0:T(8,128)(2,1)S(1)}, bf16[16,4096]{1,0:T(8,128)(2,1)S(1)}, u32[]{:S(2)}, u32[]{:S(2)}) %collective-permute-start.21) | collective-permute-done | bytes 131104 | tf_op jit(solution)/shard_map/ppermute | solution.py:71
  79.4 0.1 add_convert_fusion.3
  79.5 0.1 collective-permute-start.22
  79.6 1.7 %collective-permute-done.20 = bf16[16,4096]{1,0:T(8,128)(2,1)S(1)} collective-permute-done((bf16[16,4096]{1,0:T(8,128)(2,1)S(1)}, bf16[16,4096]{1,0:T(8,128)(2,1)S(1)}, u32[]{:S(2)}, u32[]{:S(2)}) %collective-permute-start.20) | collective-permute-done | bytes 131104 | tf_op jit(solution)/shard_map/ppermute | solution.py:71
  81.3 0.7 pad_maximum_fusion
  82.0 1.6 %collective-permute-done.19 = bf16[16,4096]{1,0:T(8,128)(2,1)S(1)} collective-permute-done((bf16[16,4096]{1,0:T(8,128)(2,1)S(1)}, bf16[16,4096]{1,0:T(8,128)(2,1)S(1)}, u32[]{:S(2)}, u32[]{:S(2)}) %collective-permute-start.19) | collective-permute-done | bytes 131104 | tf_op jit(solution)/shard_map/ppermute | solution.py:71
  83.7 0.7 pad_maximum_fusion.1
  84.4 0.7 collective-permute-done.22
  85.1 0.7 pad_maximum_fusion.2
  (24 shorter events, 0.4 us)
Async XLA Ops:
  0.6 6.3 %collective-permute-start.2 = (bf16[192,4096]{1,0:T(8,128)(2,1)}, bf16[192,4096]{1,0:T(8,128)(2,1)}, u32[]{:S(2)}, u32[]{:S(2)}) collective-permute-start(bf16[192,4096]{1,0:T(8,128)(2,1)} %refs_0_.4), channel_id=1, source_target_pairs={{0,4},{4,0},{8,12},{12,8},{16,20},{20,16},{24,28},{28,24},{1,5},{5... | collective-permute-start | bytes 4718600 | tf_op jit(solution)/shard_map/ppermute | solution.py:67
  1.1 7.7 %collective-permute-start.3 = (bf16[192,4096]{1,0:T(8,128)(2,1)}, bf16[192,4096]{1,0:T(8,128)(2,1)}, u32[]{:S(2)}, u32[]{:S(2)}) collective-permute-start(bf16[192,4096]{1,0:T(8,128)(2,1)} %refs_0_.5), channel_id=1, source_target_pairs={{0,4},{4,0},{8,12},{12,8},{16,20},{20,16},{24,28},{28,24},{1,5},{5... | collective-permute-start | bytes 4718600 | tf_op jit(solution)/shard_map/ppermute | solution.py:67
  3.3 13.3 %collective-permute-start = (bf16[96,4096]{1,0:T(8,128)(2,1)}, bf16[96,4096]{1,0:T(8,128)(2,1)}, u32[]{:S(2)}, u32[]{:S(2)}) collective-permute-start(bf16[96,4096]{1,0:T(8,128)(2,1)} %shard_map.76), channel_id=1, source_target_pairs={{0,20},{4,8},{8,12},{12,0},{16,4},{20,24},{24,28},{28,16},{1,21},{... | collective-permute-start | bytes 2359304 | tf_op jit(solution)/shard_map/ppermute | solution.py:200
  6.0 9.2 %collective-permute-start.1 = (bf16[96,4096]{1,0:T(8,128)(2,1)}, bf16[96,4096]{1,0:T(8,128)(2,1)}, u32[]{:S(2)}, u32[]{:S(2)}) collective-permute-start(bf16[96,4096]{1,0:T(8,128)(2,1)} %shard_map.76), channel_id=1, source_target_pairs={{0,4},{4,0},{8,28},{12,8},{16,20},{20,16},{24,12},{28,24},{1,5},{5... | collective-permute-start | bytes 2359304 | tf_op jit(solution)/shard_map/ppermute | solution.py:200
  6.4 4.4 %collective-permute-start.5 = (bf16[96,4096]{1,0:T(8,128)(2,1)}, bf16[96,4096]{1,0:T(8,128)(2,1)}, u32[]{:S(2)}, u32[]{:S(2)}) collective-permute-start(bf16[96,4096]{1,0:T(8,128)(2,1)} %shard_map.76), channel_id=1, source_target_pairs={{0,4},{4,0},{8,12},{12,8},{16,20},{20,16},{24,28},{28,24},{1,5},{5... | collective-permute-start | bytes 2359304 | tf_op jit(solution)/shard_map/ppermute | solution.py:67
  10.7 16.6 %copy-start = (bf16[384,4096]{1,0:T(8,128)(2,1)}, bf16[384,4096]{1,0:T(8,128)(2,1)S(1)}, u32[]{:S(2)}) copy-start(bf16[384,4096]{1,0:T(8,128)(2,1)S(1)} %shard_map.78.refs_4_.refs_3_) | copy-start | bytes 9437188
  15.2 12.2 %collective-permute-start.7 = (bf16[96,4096]{1,0:T(8,128)(2,1)}, bf16[96,4096]{1,0:T(8,128)(2,1)S(1)}, u32[]{:S(2)}, u32[]{:S(2)}) collective-permute-start(bf16[96,4096]{1,0:T(8,128)(2,1)} %collective-permute-done.1.refs_1_), channel_id=1, source_target_pairs={{0,16},{4,12},{8,24},{12,4},{16,0},{20,28},{24,8},{28,20},{1,17},{... | collective-permute-start | bytes 2359304 | tf_op jit(solution)/shard_map/ppermute | solution.py:67
  20.1 17.3 %collective-permute-start.4 = (bf16[96,4096]{1,0:T(8,128)(2,1)}, bf16[96,4096]{1,0:T(8,128)(2,1)}, u32[]{:S(2)}, u32[]{:S(2)}) collective-permute-start(bf16[96,4096]{1,0:T(8,128)(2,1)} %collective-permute-done.refs_2_), channel_id=1, source_target_pairs={{0,16},{8,24},{16,0},{24,8},{1,17},{9,25},{17,1},{25,9},{2,18},{10... | collective-permute-start | bytes 2359304 | tf_op jit(solution)/shard_map/ppermute | solution.py:67
  23.5 21.3 %collective-permute-start.6 = (bf16[96,4096]{1,0:T(8,128)(2,1)}, bf16[96,4096]{1,0:T(8,128)(2,1)}, u32[]{:S(2)}, u32[]{:S(2)}) collective-permute-start(bf16[96,4096]{1,0:T(8,128)(2,1)} %shard_map.81), channel_id=1, source_target_pairs={{0,8},{8,0},{16,24},{24,16},{1,9},{9,1},{17,25},{25,17},{2,10},{10... | collective-permute-start | bytes 2359304 | tf_op jit(solution)/shard_map/ppermute | solution.py:67
  31.3 0.7 copy-start.2
  32.0 0.7 copy-start.3
  32.7 12.1 %collective-permute-start.9 = (bf16[32,4096]{1,0:T(8,128)(2,1)}, bf16[32,4096]{1,0:T(8,128)(2,1)}, u32[]{:S(2)}, u32[]{:S(2)}) collective-permute-start(bf16[32,4096]{1,0:T(8,128)(2,1)} %get-tuple-element.34), channel_id=1, source_target_pairs={{0,8},{4,12},{8,0},{12,4},{16,24},{20,28},{24,16},{28,20},{1,9},{5... | collective-permute-start | bytes 786440 | tf_op jit(solution)/shard_map/ppermute | solution.py:67
  35.4 14.9 %collective-permute-start.8 = (bf16[32,4096]{1,0:T(8,128)(2,1)}, bf16[32,4096]{1,0:T(8,128)(2,1)S(1)}, u32[]{:S(2)}, u32[]{:S(2)}) collective-permute-start(bf16[32,4096]{1,0:T(8,128)(2,1)} %copy-done.3), channel_id=1, source_target_pairs={{0,8},{4,12},{8,0},{12,4},{16,24},{20,28},{24,16},{28,20},{1,9},{5... | collective-permute-start | bytes 786440 | tf_op jit(solution)/shard_map/ppermute | solution.py:67
  35.4 19.1 %collective-permute-start.11 = (bf16[32,4096]{1,0:T(8,128)(2,1)}, bf16[32,4096]{1,0:T(8,128)(2,1)S(1)}, u32[]{:S(2)}, u32[]{:S(2)}) collective-permute-start(bf16[32,4096]{1,0:T(8,128)(2,1)} %copy-done.2), channel_id=1, source_target_pairs={{0,8},{4,12},{8,0},{12,4},{16,24},{20,28},{24,16},{28,20},{1,9},{5... | collective-permute-start | bytes 786440 | tf_op jit(solution)/shard_map/ppermute | solution.py:67
  37.4 1.9 %copy-start.1 = (bf16[384,4096]{1,0:T(8,128)(2,1)S(1)}, bf16[384,4096]{1,0:T(8,128)(2,1)}, u32[]{:S(2)}) copy-start(bf16[384,4096]{1,0:T(8,128)(2,1)} %copy-done) | copy-start | bytes 9437188
  45.9 7.1 %collective-permute-start.12 = (bf16[32,4096]{1,0:T(8,128)(2,1)S(1)}, bf16[32,4096]{1,0:T(8,128)(2,1)S(1)}, u32[]{:S(2)}, u32[]{:S(2)}) collective-permute-start(bf16[32,4096]{1,0:T(8,128)(2,1)S(1)} %get-tuple-element.58), channel_id=1, source_target_pairs={{0,16},{4,20},{8,24},{12,28},{16,0},{20,4},{24,8},{28,12},{1,17},{... | collective-permute-start | bytes 786440 | tf_op jit(solution)/shard_map/ppermute | solution.py:67
  51.4 7.6 %collective-permute-start.10 = (bf16[32,4096]{1,0:T(8,128)(2,1)S(1)}, bf16[32,4096]{1,0:T(8,128)(2,1)S(1)}, u32[]{:S(2)}, u32[]{:S(2)}) collective-permute-start(bf16[32,4096]{1,0:T(8,128)(2,1)S(1)} %get-tuple-element.59), channel_id=1, source_target_pairs={{0,16},{4,20},{8,24},{12,28},{16,0},{20,4},{24,8},{28,12},{1,17},{... | collective-permute-start | bytes 786440 | tf_op jit(solution)/shard_map/ppermute | solution.py:67
  53.2 7.0 %collective-permute-start.15 = (bf16[16,4096]{1,0:T(8,128)(2,1)S(1)}, bf16[16,4096]{1,0:T(8,128)(2,1)S(1)}, u32[]{:S(2)}, u32[]{:S(2)}) collective-permute-start(bf16[16,4096]{1,0:T(8,128)(2,1)S(1)} %select_convert_fusion.2), channel_id=1, source_target_pairs={{0,1},{1,0},{2,3},{3,2},{4,5},{5,4},{6,7},{7,6},{8,9},{9,8},{10,11... | collective-permute-start | bytes 393224 | tf_op jit(solution)/shard_map/ppermute | solution.py:71
  55.6 8.0 %collective-permute-start.14 = (bf16[32,4096]{1,0:T(8,128)(2,1)S(1)}, bf16[32,4096]{1,0:T(8,128)(2,1)S(1)}, u32[]{:S(2)}, u32[]{:S(2)}) collective-permute-start(bf16[32,4096]{1,0:T(8,128)(2,1)S(1)} %get-tuple-element.56), channel_id=1, source_target_pairs={{0,16},{4,20},{8,24},{12,28},{16,0},{20,4},{24,8},{28,12},{1,17},{... | collective-permute-start | bytes 786440 | tf_op jit(solution)/shard_map/ppermute | solution.py:67
  59.0 6.7 %collective-permute-start.13 = (bf16[16,4096]{1,0:T(8,128)(2,1)S(1)}, bf16[16,4096]{1,0:T(8,128)(2,1)S(1)}, u32[]{:S(2)}, u32[]{:S(2)}) collective-permute-start(bf16[16,4096]{1,0:T(8,128)(2,1)S(1)} %select_convert_fusion.1), channel_id=1, source_target_pairs={{0,1},{1,0},{2,3},{3,2},{4,5},{5,4},{6,7},{7,6},{8,9},{9,8},{10,11... | collective-permute-start | bytes 393224 | tf_op jit(solution)/shard_map/ppermute | solution.py:71
  60.2 13.5 %collective-permute-start.17 = (bf16[16,4096]{1,0:T(8,128)(2,1)S(1)}, bf16[16,4096]{1,0:T(8,128)(2,1)S(1)}, u32[]{:S(2)}, u32[]{:S(2)}) collective-permute-start(bf16[16,4096]{1,0:T(8,128)(2,1)S(1)} %fusion.4), channel_id=1, source_target_pairs={{0,3},{3,0},{1,2},{2,1},{4,7},{7,4},{5,6},{6,5},{8,11},{11,8},{9,1... | collective-permute-start | bytes 393224 | tf_op jit(solution)/shard_map/ppermute | solution.py:71
  63.7 7.4 %collective-permute-start.18 = (bf16[16,4096]{1,0:T(8,128)(2,1)S(1)}, bf16[16,4096]{1,0:T(8,128)(2,1)S(1)}, u32[]{:S(2)}, u32[]{:S(2)}) collective-permute-start(bf16[16,4096]{1,0:T(8,128)(2,1)S(1)} %select_convert_fusion), channel_id=1, source_target_pairs={{0,1},{1,0},{2,3},{3,2},{4,5},{5,4},{6,7},{7,6},{8,9},{9,8},{10,11... | collective-permute-start | bytes 393224 | tf_op jit(solution)/shard_map/ppermute | solution.py:71
  65.7 8.1 %collective-permute-start.16 = (bf16[16,4096]{1,0:T(8,128)(2,1)S(1)}, bf16[16,4096]{1,0:T(8,128)(2,1)S(1)}, u32[]{:S(2)}, u32[]{:S(2)}) collective-permute-start(bf16[16,4096]{1,0:T(8,128)(2,1)S(1)} %fusion.5), channel_id=1, source_target_pairs={{0,3},{3,0},{1,2},{2,1},{4,7},{7,4},{5,6},{6,5},{8,11},{11,8},{9,1... | collective-permute-start | bytes 393224 | tf_op jit(solution)/shard_map/ppermute | solution.py:71
  71.1 8.3 %collective-permute-start.21 = (bf16[16,4096]{1,0:T(8,128)(2,1)S(1)}, bf16[16,4096]{1,0:T(8,128)(2,1)S(1)}, u32[]{:S(2)}, u32[]{:S(2)}) collective-permute-start(bf16[16,4096]{1,0:T(8,128)(2,1)S(1)} %fusion.6), channel_id=1, source_target_pairs={{0,3},{3,0},{1,2},{2,1},{4,7},{7,4},{5,6},{6,5},{8,11},{11,8},{9,1... | collective-permute-start | bytes 393224 | tf_op jit(solution)/shard_map/ppermute | solution.py:71
  73.8 7.5 %collective-permute-start.20 = (bf16[16,4096]{1,0:T(8,128)(2,1)S(1)}, bf16[16,4096]{1,0:T(8,128)(2,1)S(1)}, u32[]{:S(2)}, u32[]{:S(2)}) collective-permute-start(bf16[16,4096]{1,0:T(8,128)(2,1)S(1)} %add_convert_fusion.5), channel_id=1, source_target_pairs={{0,1},{1,0},{2,3},{3,2},{4,5},{5,4},{6,7},{7,6},{8,9},{9,8},{10,11... | collective-permute-start | bytes 393224 | tf_op jit(solution)/shard_map/ppermute | solution.py:71
  74.0 9.7 %collective-permute-start.19 = (bf16[16,4096]{1,0:T(8,128)(2,1)S(1)}, bf16[16,4096]{1,0:T(8,128)(2,1)S(1)}, u32[]{:S(2)}, u32[]{:S(2)}) collective-permute-start(bf16[16,4096]{1,0:T(8,128)(2,1)S(1)} %add_convert_fusion.4), channel_id=1, source_target_pairs={{0,1},{1,0},{2,3},{3,2},{4,5},{5,4},{6,7},{7,6},{8,9},{9,8},{10,11... | collective-permute-start | bytes 393224 | tf_op jit(solution)/shard_map/ppermute | solution.py:71
  79.5 5.6 %collective-permute-start.22 = (bf16[16,4096]{1,0:T(8,128)(2,1)S(1)}, bf16[16,4096]{1,0:T(8,128)(2,1)S(1)}, u32[]{:S(2)}, u32[]{:S(2)}) collective-permute-start(bf16[16,4096]{1,0:T(8,128)(2,1)S(1)} %add_convert_fusion.3), channel_id=1, source_target_pairs={{0,1},{1,0},{2,3},{3,2},{4,5},{5,4},{6,7},{7,6},{8,9},{9,8},{10,11... | collective-permute-start | bytes 393224 | tf_op jit(solution)/shard_map/ppermute | solution.py:71

commit v5 on v4

--- a/solution.py
+++ b/solution.py
@@ -109,23 +109,29 @@
 
 
 def kernel_call(kernel, outs, flags, *arrays):
-    held = [pltpu.with_memory_space_constraint(a, pltpu.VMEM) for a in arrays[-2:]]
-    rows = held[0].shape[0] // 2
+    held = pltpu.with_memory_space_constraint(arrays[-1], pltpu.VMEM)
+    rows = held.shape[0] // 4
+    width, sent = held.shape[1], pltpu.HBM
 
     def inner(*refs):
-        at = len(arrays) - 1
-        halves = [ref.at[pl.ds(k * rows, rows)] for ref in refs[at : at + 2] for k in (0, 1)]
-        kernel(*refs[:at], *halves, *refs[at + 2 :])
+        at = len(arrays)
+        parts = [refs[at].at[pl.ds(k * rows, rows)] for k in range(4)]
+        kernel(*refs[:at], *parts, *refs[at + 1 :])
 
     return pl.pallas_call(
         inner,
-        out_shape=[jax.ShapeDtypeStruct(shape, dtype) for shape, dtype in outs],
+        out_shape=[
+            sent(shape, dtype)
+            if shape[-1] == width and dtype == BF16
+            else jax.ShapeDtypeStruct(shape, dtype)
+            for shape, dtype in outs
+        ],
         in_specs=[pl.BlockSpec(memory_space=pltpu.SMEM)]
         + [pl.BlockSpec(memory_space=pltpu.VMEM)] * len(arrays),
         out_specs=[pl.BlockSpec(memory_space=pltpu.VMEM)] * len(outs),
         compiler_params=pltpu.CompilerParams(vmem_limit_bytes=VMEM_LIMIT),
         cost_estimate=pl.CostEstimate(flops=1, bytes_accessed=8388608, transcendentals=0),
-    )(flags, *arrays[:-2], *held)
+    )(flags, *arrays[:-1], held)
 
 
 def span_dot(weights, low, high, sources):
@@ -258,7 +264,7 @@
     own = on_chip(gate_weight, up_weight, down_weight)
     w_p = hop(own, lambda i: CORE)
     w_v, w_u = spread(own)
-    here = [on_chip(tokens, tokens_in), on_chip(cotangent, cotangent_in)]
+    here = [on_chip(tokens, tokens_in, cotangent, cotangent_in)]
     (p,) = kernel_call(of_pair, [((3 * block, width), BF16)], flags, w_p, *here)
     w_s = hop(after(w_v, p), other)
     p = hop(p, lambda i: X, 0)
@@ -316,7 +322,7 @@
         return results[k]
 
     stages = [leave_stage, swap_stage, across_stage, back_stage, result_stage]
-    steps = ((0, 0), (1, 0), (0, 1), (2, 0), (1, 1), (0, 2), (2, 1), (1, 2), (2, 2), (0, 3), (1, 3), (2, 3), (0, 4), (1, 4), (2, 4))
+    steps = ((0, 0), (1, 0), (0, 1), (2, 0), (1, 1), (0, 2), (2, 1), (1, 2), (2, 2), (0, 3), (1, 3), (2, 3), (1, 4), (0, 4), (2, 4))
     for k, at in steps:
         turn = stages[at](order[k])
     return results[0], results[1], results[2]

time: 86.3 us -> 85.4 us (0.990)
  starting transfers between devices: 32.6 us -> 43.2 us
  waiting for transfers between devices: 20.5 us -> 13.5 us
  Pallas kernels: 22.1 us -> 18.3 us
    ppermute x12, starting transfers between devices: 15.9 us -> 21.8 us  [hop(): return lax.ppermute(block, 'section', route)]
    ppermute x9, starting transfers between devices: 13.6 us -> 18.3 us  [along(): return lax.ppermute(block, 'dp', route)]
    ppermute x9, waiting for transfers between devices: 11 us -> 7.09 us  [along(): return lax.ppermute(block, 'dp', route)]
    ppermute x12, waiting for transfers between devices: 9.48 us -> 6.45 us  [hop(): return lax.ppermute(block, 'section', route)]
    pallas_call x4, Pallas kernels: 16.3 us -> 14.4 us  [kernel_call(): pl.pallas_call(inner, out_shape=[sent(shape, dtype) if shape[-1] == width...]
    pallas_call x3 -> x2, Pallas kernels: 5.85 us -> 4 us  [on_chip(): pl.pallas_call(kernel, out_shape=pltpu.VMEM((rows, parts[0].shape[1]), pa...]
    unnamed x8 -> x4, local copies, waits for them, and re-layouts: 3.3 us -> 2.79 us
  transfers between devices with their start and end apart: 23 -> 23, of which waited for: 12 -> 8; matrix products, arithmetic and copies ran while one was open for 7% -> 7% of each run, Pallas kernels for 26% -> 22%
where the time goes in v5:
time: 85.4 us; the launch traced here: 85.1 us
  starting transfers between devices  43.2 us (51%)
  Pallas kernels  18.3 us (21%)
  waiting for transfers between devices  13.5 us (16%)
  other arithmetic  6.31 us (7%)
  local copies, waits for them, and re-layouts  2.87 us (3%)
    ppermute x12, starting transfers between devices, hop(): return lax.ppermute(block, 'section', route)  21.8 us
    ppermute x9, starting transfers between devices, along(): return lax.ppermute(block, 'dp', route)  18.3 us
    pallas_call x4, Pallas kernels, kernel_call(): pl.pallas_call(inner, out_shape=[sent(shape, dtype) if shape[-1] == width...  14.4 us
    ppermute x9, waiting for transfers between devices, along(): return lax.ppermute(block, 'dp', route)  7.09 us
    ppermute x12, waiting for transfers between devices, hop(): return lax.ppermute(block, 'section', route)  6.45 us
    pallas_call x2, Pallas kernels, on_chip(): pl.pallas_call(kernel, out_shape=pltpu.VMEM((rows, parts[0].shape[1]), pa...  4 us
    ppermute x2, starting transfers between devices, spread(): return (lax.ppermute(own, 'section', v), lax.ppermute(own, 'section', u))  3.08 us
    unnamed x4, local copies, waits for them, and re-layouts  2.79 us
  transfers between devices with their start and end apart: 23, of which 8 were waited for; matrix products, arithmetic and copies ran while one was open for 7% of the time, Pallas kernels for 22%

profile of v5, /device:TPU:0, one launch (start us, length us, event | category | flops | bytes accessed | tf_op | source)
XLA Modules:
  0.0 85.1 jit_solution(4353264700083813490)
XLA Ops:
  0.6 0.5 collective-permute-start.2
  1.1 0.1 collective-permute-start.3
  1.2 1.1 %shard_map.76 = bf16[96,4096]{1,0:T(8,128)(2,1)S(1)} custom-call(bf16[32,4096]{1,0:T(8,128)(2,1)} %refs_0_.2, bf16[32,4096]{1,0:T(8,128)(2,1)} %refs_1_.1, bf16[32,4096]{1,0:T(8,128)(2,1)} %refs_2_.2), custom_call_target="tpu_custom_call" | custom-call | flops 1 | bytes 1 | tf_op jit(solution)/shard_map/pallas_call | solution.py:100
  2.4 2.7 %collective-permute-start = (bf16[96,4096]{1,0:T(8,128)(2,1)S(1)}, bf16[96,4096]{1,0:T(8,128)(2,1)S(1)}, u32[]{:S(2)}, u32[]{:S(2)}) collective-permute-start(bf16[96,4096]{1,0:T(8,128)(2,1)S(1)} %shard_map.76), channel_id=1, source_target_pairs={{0,20},{4,8},{8,12},{12,0},{16,4},{20,24},{24,28},{28,16},{1,21},{... | collective-permute-start | bytes 2359304 | tf_op jit(solution)/shard_map/ppermute | solution.py:206
  5.1 0.4 collective-permute-start.1
  5.5 0.1 collective-permute-start.5
  5.6 0.1 pad_add_fusion
  5.6 0.1 fusion.3
  5.7 0.1 broadcast_subtract_fusion
  5.8 0.1 sub.37
  5.9 0.1 add_convert_fusion.6.refs_0_
  6.0 0.0 collective-permute-done.2.refs_1_
  6.0 0.8 collective-permute-done.3.refs_3_
  6.8 2.9 %shard_map.77.refs_3_.refs_2_ = bf16[768,4096]{1,0:T(8,128)(2,1)S(1)} custom-call(bf16[192,4096]{1,0:T(8,128)(2,1)} %refs_0_.3, bf16[192,4096]{1,0:T(8,128)(2,1)} %collective-permute-done.2.refs_1_, bf16[192,4096]{1,0:T(8,128)(2,1)} %refs_2_.3, bf16[192,4096]{1,0:T(8,128)(2,1)} %collective-permute-done.3.refs_3_), custom_call_target="tpu_custom_call" | custom-call | flops 1 | bytes 1 | tf_op jit(solution)/shard_map/pallas_call | solution.py:100
  9.7 0.0 collective-permute-done.5.refs_1_
  9.7 3.2 %shard_map.80 = bf16[96,4096]{1,0:T(8,128)(2,1)} custom-call(s32[10]{0:T(128)S(1)} %add_convert_fusion.6.refs_0_, bf16[96,4096]{1,0:T(8,128)(2,1)S(1)} %collective-permute-done.5.refs_1_, bf16[768,4096]{1,0:T(8,128)(2,1)S(1)} %shard_map.77.refs_3_.refs_2_), custom_call_target="tpu_custom_call" | custom-call | flops 1 | bytes 8388608 | tf_op jit(solution)/shard_map/pallas_call | solution.py:121
  12.9 0.0 collective-permute-done.1.refs_1_
  12.9 2.9 %collective-permute-start.7 = (bf16[96,4096]{1,0:T(8,128)(2,1)S(1)}, bf16[96,4096]{1,0:T(8,128)(2,1)S(1)}, u32[]{:S(2)}, u32[]{:S(2)}) collective-permute-start(bf16[96,4096]{1,0:T(8,128)(2,1)S(1)} %collective-permute-done.1.refs_1_), channel_id=1, source_target_pairs={{0,16},{4,12},{8,24},{12,4},{16,0},{20,28},{24,8},{28,20},{1,17},{... | collective-permute-start | bytes 2359304 | tf_op jit(solution)/shard_map/ppermute | solution.py:67
  15.8 0.0 collective-permute-done.refs_2_
  15.8 2.7 %shard_map.78.refs_2_ = bf16[4,96,192]{2,1,0:T(8,128)(2,1)S(1)} custom-call(s32[10]{0:T(128)S(1)} %add_convert_fusion.6.refs_0_, bf16[96,4096]{1,0:T(8,128)(2,1)S(1)} %collective-permute-done.1.refs_1_, bf16[96,4096]{1,0:T(8,128)(2,1)S(1)} %collective-permute-done.refs_2_, bf16[768,4096]{1,0:T(8,128)(2,1)S(1)} %shard_map.77.refs_3_.refs_2_), custom_call_target="tpu_custom_call" | custom-call | flops 1 | bytes 8388608 | tf_op jit(solution)/shard_map/pallas_call | solution.py:121
  18.5 2.9 %collective-permute-start.4 = (bf16[96,4096]{1,0:T(8,128)(2,1)S(1)}, bf16[96,4096]{1,0:T(8,128)(2,1)S(1)}, u32[]{:S(2)}, u32[]{:S(2)}) collective-permute-start(bf16[96,4096]{1,0:T(8,128)(2,1)S(1)} %collective-permute-done.refs_2_), channel_id=1, source_target_pairs={{0,16},{8,24},{16,0},{24,8},{1,17},{9,25},{17,1},{25,9},{2,18},{10... | collective-permute-start | bytes 2359304 | tf_op jit(solution)/shard_map/ppermute | solution.py:67
  21.4 5.2 %collective-permute-start.6 = (bf16[96,4096]{1,0:T(8,128)(2,1)}, bf16[96,4096]{1,0:T(8,128)(2,1)}, u32[]{:S(2)}, u32[]{:S(2)}) collective-permute-start(bf16[96,4096]{1,0:T(8,128)(2,1)} %shard_map.80), channel_id=1, source_target_pairs={{0,8},{8,0},{16,24},{24,16},{1,9},{9,1},{17,25},{25,17},{2,10},{10... | collective-permute-start | bytes 2359304 | tf_op jit(solution)/shard_map/ppermute | solution.py:67
  26.6 4.6 %shard_map.81 = (bf16[32,4096]{1,0:T(8,128)(2,1)}, bf16[32,4096]{1,0:T(8,128)(2,1)}, bf16[32,4096]{1,0:T(8,128)(2,1)}) custom-call(s32[10]{0:T(128)S(1)} %add_convert_fusion.6.refs_0_, bf16[96,4096]{1,0:T(8,128)(2,1)S(1)} %collective-permute-done.7.refs_1_, bf16[768,4096]{1,0:T(8,128)(2,1)S(1)} %shard_map.77.refs_3_.refs_2_), custom_call_target="tpu_custom_call" | custom-call | flops 1 | bytes 8388608 | tf_op jit(solution)/shard_map/pallas_call | solution.py:121
  31.2 3.4 %collective-permute-start.9 = (bf16[32,4096]{1,0:T(8,128)(2,1)}, bf16[32,4096]{1,0:T(8,128)(2,1)S(1)}, u32[]{:S(2)}, u32[]{:S(2)}) collective-permute-start(bf16[32,4096]{1,0:T(8,128)(2,1)} %get-tuple-element.34), channel_id=1, source_target_pairs={{0,8},{4,12},{8,0},{12,4},{16,24},{20,28},{24,16},{28,20},{1,9},{5... | collective-permute-start | bytes 786440 | tf_op jit(solution)/shard_map/ppermute | solution.py:67
  34.6 0.0 collective-permute-start.8
  34.7 2.0 %collective-permute-start.11 = (bf16[32,4096]{1,0:T(8,128)(2,1)}, bf16[32,4096]{1,0:T(8,128)(2,1)S(1)}, u32[]{:S(2)}, u32[]{:S(2)}) collective-permute-start(bf16[32,4096]{1,0:T(8,128)(2,1)} %get-tuple-element.41), channel_id=1, source_target_pairs={{0,8},{4,12},{8,0},{12,4},{16,24},{20,28},{24,16},{28,20},{1,9},{5... | collective-permute-start | bytes 786440 | tf_op jit(solution)/shard_map/ppermute | solution.py:67
  36.7 0.0 collective-permute-done.4.refs_1_
  36.7 2.8 %copy-done.1 = bf16[768,4096]{1,0:T(8,128)(2,1)S(1)} copy-done((bf16[768,4096]{1,0:T(8,128)(2,1)S(1)}, bf16[768,4096]{1,0:T(8,128)(2,1)}, u32[]{:S(2)}) %copy-start.1) | copy-done | bytes 6291480
  39.5 3.8 %shard_map.79 = (f32[32,4096]{1,0:T(8,128)S(1)}, f32[32,4096]{1,0:T(8,128)S(1)}, f32[32,4096]{1,0:T(8,128)S(1)}, f32[32,4096]{1,0:T(8,128)S(1)}, f32[32,4096]{1,0:T(8,128)S(1)}, /*index=5*/f32[32,4096]{1,0:T(8,128)S(1)}) custom-call(s32[10]{0:T(128)S(1)} %add_convert_fusion.6.refs_0_, bf16[96,4096]{1,0:T(8,128)(2,1)S(1)} %collective-permute-done.4.refs_1_, ...), custom_call_target="tpu_custom_call" | custom-call | flops 1 | bytes 8388608 | tf_op jit(solution)/shard_map/pallas_call | solution.py:121
  43.3 0.8 collective-permute-done.9
  44.1 0.0 collective-permute-done.6
  44.1 1.1 %convert_add_fusion.4 = (f32[32,4096]{1,0:T(8,128)S(1)}, bf16[32,4096]{1,0:T(8,128)(2,1)S(1)}) fusion(f32[32,4096]{1,0:T(8,128)S(1)} %get-tuple-element.38, bf16[32,4096]{1,0:T(8,128)(2,1)S(1)} %collective-permute-done.9, pred[]{:T(512)} %eq.30, bf16[96,4096]{1,0:T(8,128)(2,1)} %collective-permute-done.6, f32[32,4096]{1,0:T(8,128)S(1)} %get-tuple-element.33), kind=kLoop, calls=%fused_computation.5 | loop fusion | flops 917504 | bytes 2359297 | tf_op jit(solution)/shard_map/add | solution.py:294
  45.1 1.6 %collective-permute-start.12 = (bf16[32,4096]{1,0:T(8,128)(2,1)S(1)}, bf16[32,4096]{1,0:T(8,128)(2,1)S(1)}, u32[]{:S(2)}, u32[]{:S(2)}) collective-permute-start(bf16[32,4096]{1,0:T(8,128)(2,1)S(1)} %get-tuple-element.58), channel_id=1, source_target_pairs={{0,16},{4,20},{8,24},{12,28},{16,0},{20,4},{24,8},{28,12},{1,17},{... | collective-permute-start | bytes 786440 | tf_op jit(solution)/shard_map/ppermute | solution.py:67
  46.7 3.0 %collective-permute-done.8 = bf16[32,4096]{1,0:T(8,128)(2,1)S(1)} collective-permute-done((bf16[32,4096]{1,0:T(8,128)(2,1)}, bf16[32,4096]{1,0:T(8,128)(2,1)S(1)}, u32[]{:S(2)}, u32[]{:S(2)}) %collective-permute-start.8) | collective-permute-done | bytes 262176 | tf_op jit(solution)/shard_map/ppermute | solution.py:67
  49.7 1.1 %add_convert_fusion.1 = (bf16[32,4096]{1,0:T(8,128)(2,1)S(1)}, f32[32,4096]{1,0:T(8,128)S(1)}) fusion(f32[32,4096]{1,0:T(8,128)S(1)} %get-tuple-element.35, bf16[32,4096]{1,0:T(8,128)(2,1)S(1)} %collective-permute-done.8, pred[]{:T(512)} %eq.30, bf16[96,4096]{1,0:T(8,128)(2,1)} %collective-permute-done.6, f32[32,4096]{1,0:T(8,128)S(1)} %get-tuple-element.30), kind=kLoop, calls=%fused_computation.6 | loop fusion | flops 917504 | bytes 2359297 | tf_op jit(solution)/shard_map/convert_element_type | solution.py:292
  50.8 1.6 %collective-permute-start.10 = (bf16[32,4096]{1,0:T(8,128)(2,1)S(1)}, bf16[32,4096]{1,0:T(8,128)(2,1)S(1)}, u32[]{:S(2)}, u32[]{:S(2)}) collective-permute-start(bf16[32,4096]{1,0:T(8,128)(2,1)S(1)} %get-tuple-element.59), channel_id=1, source_target_pairs={{0,16},{4,20},{8,24},{12,28},{16,0},{20,4},{24,8},{28,12},{1,17},{... | collective-permute-start | bytes 786440 | tf_op jit(solution)/shard_map/ppermute | solution.py:67
  52.3 0.6 collective-permute-done.12
  53.1 1.6 %collective-permute-start.15 = (bf16[16,4096]{1,0:T(8,128)(2,1)S(1)}, bf16[16,4096]{1,0:T(8,128)(2,1)S(1)}, u32[]{:S(2)}, u32[]{:S(2)}) collective-permute-start(bf16[16,4096]{1,0:T(8,128)(2,1)S(1)} %select_convert_fusion.2), channel_id=1, source_target_pairs={{0,1},{1,0},{2,3},{3,2},{4,5},{5,4},{6,7},{7,6},{8,9},{9,8},{10,11... | collective-permute-start | bytes 393224 | tf_op jit(solution)/shard_map/ppermute | solution.py:71
  54.7 0.0 collective-permute-done.11
  54.7 1.1 %convert_add_fusion.1 = (f32[32,4096]{1,0:T(8,128)S(1)}, bf16[32,4096]{1,0:T(8,128)(2,1)S(1)}) fusion(f32[32,4096]{1,0:T(8,128)S(1)} %get-tuple-element.37, bf16[32,4096]{1,0:T(8,128)(2,1)S(1)} %collective-permute-done.11, pred[]{:T(512)} %eq.30, bf16[96,4096]{1,0:T(8,128)(2,1)} %collective-permute-done.6, f32[32,4096]{1,0:T(8,128)S(1)} %get-tuple-element.36), kind=kLoop, calls=%fused_computation.1 | loop fusion | flops 917504 | bytes 2359297 | tf_op jit(solution)/shard_map/add | solution.py:294
  55.8 1.6 %collective-permute-start.14 = (bf16[32,4096]{1,0:T(8,128)(2,1)S(1)}, bf16[32,4096]{1,0:T(8,128)(2,1)S(1)}, u32[]{:S(2)}, u32[]{:S(2)}) collective-permute-start(bf16[32,4096]{1,0:T(8,128)(2,1)S(1)} %get-tuple-element.56), channel_id=1, source_target_pairs={{0,16},{4,20},{8,24},{12,28},{16,0},{20,4},{24,8},{28,12},{1,17},{... | collective-permute-start | bytes 786440 | tf_op jit(solution)/shard_map/ppermute | solution.py:67
  57.3 1.3 %collective-permute-done.10 = bf16[32,4096]{1,0:T(8,128)(2,1)S(1)} collective-permute-done((bf16[32,4096]{1,0:T(8,128)(2,1)S(1)}, bf16[32,4096]{1,0:T(8,128)(2,1)S(1)}, u32[]{:S(2)}, u32[]{:S(2)}) %collective-permute-start.10) | collective-permute-done | bytes 262176 | tf_op jit(solution)/shard_map/ppermute | solution.py:67
  58.6 0.1 convert_add_fusion.2
  58.7 1.6 %collective-permute-start.13 = (bf16[16,4096]{1,0:T(8,128)(2,1)S(1)}, bf16[16,4096]{1,0:T(8,128)(2,1)S(1)}, u32[]{:S(2)}, u32[]{:S(2)}) collective-permute-start(bf16[16,4096]{1,0:T(8,128)(2,1)S(1)} %select_convert_fusion.1), channel_id=1, source_target_pairs={{0,1},{1,0},{2,3},{3,2},{4,5},{5,4},{6,7},{7,6},{8,9},{9,8},{10,11... | collective-permute-start | bytes 393224 | tf_op jit(solution)/shard_map/ppermute | solution.py:71
  60.4 2.5 %collective-permute-start.17 = (bf16[16,4096]{1,0:T(8,128)(2,1)S(1)}, bf16[16,4096]{1,0:T(8,128)(2,1)S(1)}, u32[]{:S(2)}, u32[]{:S(2)}) collective-permute-start(bf16[16,4096]{1,0:T(8,128)(2,1)S(1)} %fusion.4), channel_id=1, source_target_pairs={{0,3},{3,0},{1,2},{2,1},{4,7},{7,4},{5,6},{6,5},{8,11},{11,8},{9,1... | collective-permute-start | bytes 393224 | tf_op jit(solution)/shard_map/ppermute | solution.py:71
  62.9 0.0 collective-permute-done.14
  63.0 1.6 %collective-permute-start.18 = (bf16[16,4096]{1,0:T(8,128)(2,1)S(1)}, bf16[16,4096]{1,0:T(8,128)(2,1)S(1)}, u32[]{:S(2)}, u32[]{:S(2)}) collective-permute-start(bf16[16,4096]{1,0:T(8,128)(2,1)S(1)} %select_convert_fusion), channel_id=1, source_target_pairs={{0,1},{1,0},{2,3},{3,2},{4,5},{5,4},{6,7},{7,6},{8,9},{9,8},{10,11... | collective-permute-start | bytes 393224 | tf_op jit(solution)/shard_map/ppermute | solution.py:71
  64.5 0.0 collective-permute-done.13
  64.6 2.9 %collective-permute-start.16 = (bf16[16,4096]{1,0:T(8,128)(2,1)S(1)}, bf16[16,4096]{1,0:T(8,128)(2,1)S(1)}, u32[]{:S(2)}, u32[]{:S(2)}) collective-permute-start(bf16[16,4096]{1,0:T(8,128)(2,1)S(1)} %fusion.5), channel_id=1, source_target_pairs={{0,3},{3,0},{1,2},{2,1},{4,7},{7,4},{5,6},{6,5},{8,11},{11,8},{9,1... | collective-permute-start | bytes 393224 | tf_op jit(solution)/shard_map/ppermute | solution.py:71
  67.5 1.7 %collective-permute-done.18 = bf16[16,4096]{1,0:T(8,128)(2,1)S(1)} collective-permute-done((bf16[16,4096]{1,0:T(8,128)(2,1)S(1)}, bf16[16,4096]{1,0:T(8,128)(2,1)S(1)}, u32[]{:S(2)}, u32[]{:S(2)}) %collective-permute-start.18) | collective-permute-done | bytes 131104 | tf_op jit(solution)/shard_map/ppermute | solution.py:71
  69.2 5.8 %collective-permute-start.20 = (bf16[16,4096]{1,0:T(8,128)(2,1)S(1)}, bf16[16,4096]{1,0:T(8,128)(2,1)S(1)}, u32[]{:S(2)}, u32[]{:S(2)}) collective-permute-start(bf16[16,4096]{1,0:T(8,128)(2,1)S(1)} %fusion.6), channel_id=1, source_target_pairs={{0,3},{3,0},{1,2},{2,1},{4,7},{7,4},{5,6},{6,5},{8,11},{11,8},{9,1... | collective-permute-start | bytes 393224 | tf_op jit(solution)/shard_map/ppermute | solution.py:71
  75.0 0.0 collective-permute-done.17
  75.0 0.1 add_convert_fusion.5
  75.1 0.1 collective-permute-start.22
  75.2 0.1 add_convert_fusion.4
  75.2 2.1 %collective-permute-start.19 = (bf16[16,4096]{1,0:T(8,128)(2,1)S(1)}, bf16[16,4096]{1,0:T(8,128)(2,1)S(1)}, u32[]{:S(2)}, u32[]{:S(2)}) collective-permute-start(bf16[16,4096]{1,0:T(8,128)(2,1)S(1)} %add_convert_fusion.4), channel_id=1, source_target_pairs={{0,1},{1,0},{2,3},{3,2},{4,5},{5,4},{6,7},{7,6},{8,9},{9,8},{10,11... | collective-permute-start | bytes 393224 | tf_op jit(solution)/shard_map/ppermute | solution.py:71
  77.3 1.8 %collective-permute-done.20 = bf16[16,4096]{1,0:T(8,128)(2,1)S(1)} collective-permute-done((bf16[16,4096]{1,0:T(8,128)(2,1)S(1)}, bf16[16,4096]{1,0:T(8,128)(2,1)S(1)}, u32[]{:S(2)}, u32[]{:S(2)}) %collective-permute-start.20) | collective-permute-done | bytes 131104 | tf_op jit(solution)/shard_map/ppermute | solution.py:71
  79.1 0.1 add_convert_fusion.3
  79.2 0.1 collective-permute-start.21
  79.2 3.6 %collective-permute-done.19 = bf16[16,4096]{1,0:T(8,128)(2,1)S(1)} collective-permute-done((bf16[16,4096]{1,0:T(8,128)(2,1)S(1)}, bf16[16,4096]{1,0:T(8,128)(2,1)S(1)}, u32[]{:S(2)}, u32[]{:S(2)}) %collective-permute-start.19) | collective-permute-done | bytes 131104 | tf_op jit(solution)/shard_map/ppermute | solution.py:71
  82.9 0.7 pad_maximum_fusion
  83.6 0.7 pad_maximum_fusion.1
  84.4 0.0 collective-permute-done.21
  84.4 0.7 pad_maximum_fusion.2
  (19 shorter events, 0.4 us)
Async XLA Ops:
  0.6 5.3 %collective-permute-start.2 = (bf16[192,4096]{1,0:T(8,128)(2,1)}, bf16[192,4096]{1,0:T(8,128)(2,1)}, u32[]{:S(2)}, u32[]{:S(2)}) collective-permute-start(bf16[192,4096]{1,0:T(8,128)(2,1)} %refs_0_.3), channel_id=1, source_target_pairs={{0,4},{4,0},{8,12},{12,8},{16,20},{20,16},{24,28},{28,24},{1,5},{5... | collective-permute-start | bytes 4718600 | tf_op jit(solution)/shard_map/ppermute | solution.py:67
  1.1 5.6 %collective-permute-start.3 = (bf16[192,4096]{1,0:T(8,128)(2,1)}, bf16[192,4096]{1,0:T(8,128)(2,1)}, u32[]{:S(2)}, u32[]{:S(2)}) collective-permute-start(bf16[192,4096]{1,0:T(8,128)(2,1)} %refs_2_.3), channel_id=1, source_target_pairs={{0,4},{4,0},{8,12},{12,8},{16,20},{20,16},{24,28},{28,24},{1,5},{5... | collective-permute-start | bytes 4718600 | tf_op jit(solution)/shard_map/ppermute | solution.py:67
  2.4 13.4 %collective-permute-start = (bf16[96,4096]{1,0:T(8,128)(2,1)S(1)}, bf16[96,4096]{1,0:T(8,128)(2,1)S(1)}, u32[]{:S(2)}, u32[]{:S(2)}) collective-permute-start(bf16[96,4096]{1,0:T(8,128)(2,1)S(1)} %shard_map.76), channel_id=1, source_target_pairs={{0,20},{4,8},{8,12},{12,0},{16,4},{20,24},{24,28},{28,16},{1,21},{... | collective-permute-start | bytes 2359304 | tf_op jit(solution)/shard_map/ppermute | solution.py:206
  5.1 7.8 %collective-permute-start.1 = (bf16[96,4096]{1,0:T(8,128)(2,1)S(1)}, bf16[96,4096]{1,0:T(8,128)(2,1)S(1)}, u32[]{:S(2)}, u32[]{:S(2)}) collective-permute-start(bf16[96,4096]{1,0:T(8,128)(2,1)S(1)} %shard_map.76), channel_id=1, source_target_pairs={{0,4},{4,0},{8,28},{12,8},{16,20},{20,16},{24,12},{28,24},{1,5},{5... | collective-permute-start | bytes 2359304 | tf_op jit(solution)/shard_map/ppermute | solution.py:206
  5.5 4.2 %collective-permute-start.5 = (bf16[96,4096]{1,0:T(8,128)(2,1)S(1)}, bf16[96,4096]{1,0:T(8,128)(2,1)S(1)}, u32[]{:S(2)}, u32[]{:S(2)}) collective-permute-start(bf16[96,4096]{1,0:T(8,128)(2,1)S(1)} %shard_map.76), channel_id=1, source_target_pairs={{0,4},{4,0},{8,12},{12,8},{16,20},{20,16},{24,28},{28,24},{1,5},{5... | collective-permute-start | bytes 2359304 | tf_op jit(solution)/shard_map/ppermute | solution.py:67
  9.7 16.9 %copy-start = (bf16[768,4096]{1,0:T(8,128)(2,1)}, bf16[768,4096]{1,0:T(8,128)(2,1)S(1)}, u32[]{:S(2)}) copy-start(bf16[768,4096]{1,0:T(8,128)(2,1)S(1)} %shard_map.77.refs_3_.refs_2_) | copy-start | bytes 18874372
  12.9 13.7 %collective-permute-start.7 = (bf16[96,4096]{1,0:T(8,128)(2,1)S(1)}, bf16[96,4096]{1,0:T(8,128)(2,1)S(1)}, u32[]{:S(2)}, u32[]{:S(2)}) collective-permute-start(bf16[96,4096]{1,0:T(8,128)(2,1)S(1)} %collective-permute-done.1.refs_1_), channel_id=1, source_target_pairs={{0,16},{4,12},{8,24},{12,4},{16,0},{20,28},{24,8},{28,20},{1,17},{... | collective-permute-start | bytes 2359304 | tf_op jit(solution)/shard_map/ppermute | solution.py:67
  18.5 18.2 %collective-permute-start.4 = (bf16[96,4096]{1,0:T(8,128)(2,1)S(1)}, bf16[96,4096]{1,0:T(8,128)(2,1)S(1)}, u32[]{:S(2)}, u32[]{:S(2)}) collective-permute-start(bf16[96,4096]{1,0:T(8,128)(2,1)S(1)} %collective-permute-done.refs_2_), channel_id=1, source_target_pairs={{0,16},{8,24},{16,0},{24,8},{1,17},{9,25},{17,1},{25,9},{2,18},{10... | collective-permute-start | bytes 2359304 | tf_op jit(solution)/shard_map/ppermute | solution.py:67
  21.4 22.7 %collective-permute-start.6 = (bf16[96,4096]{1,0:T(8,128)(2,1)}, bf16[96,4096]{1,0:T(8,128)(2,1)}, u32[]{:S(2)}, u32[]{:S(2)}) collective-permute-start(bf16[96,4096]{1,0:T(8,128)(2,1)} %shard_map.80), channel_id=1, source_target_pairs={{0,8},{8,0},{16,24},{24,16},{1,9},{9,1},{17,25},{25,17},{2,10},{10... | collective-permute-start | bytes 2359304 | tf_op jit(solution)/shard_map/ppermute | solution.py:67
  31.2 12.8 %collective-permute-start.9 = (bf16[32,4096]{1,0:T(8,128)(2,1)}, bf16[32,4096]{1,0:T(8,128)(2,1)S(1)}, u32[]{:S(2)}, u32[]{:S(2)}) collective-permute-start(bf16[32,4096]{1,0:T(8,128)(2,1)} %get-tuple-element.34), channel_id=1, source_target_pairs={{0,8},{4,12},{8,0},{12,4},{16,24},{20,28},{24,16},{28,20},{1,9},{5... | collective-permute-start | bytes 786440 | tf_op jit(solution)/shard_map/ppermute | solution.py:67
  34.6 15.0 %collective-permute-start.8 = (bf16[32,4096]{1,0:T(8,128)(2,1)}, bf16[32,4096]{1,0:T(8,128)(2,1)S(1)}, u32[]{:S(2)}, u32[]{:S(2)}) collective-permute-start(bf16[32,4096]{1,0:T(8,128)(2,1)} %get-tuple-element.32), channel_id=1, source_target_pairs={{0,8},{4,12},{8,0},{12,4},{16,24},{20,28},{24,16},{28,20},{1,9},{5... | collective-permute-start | bytes 786440 | tf_op jit(solution)/shard_map/ppermute | solution.py:67
  34.7 20.0 %collective-permute-start.11 = (bf16[32,4096]{1,0:T(8,128)(2,1)}, bf16[32,4096]{1,0:T(8,128)(2,1)S(1)}, u32[]{:S(2)}, u32[]{:S(2)}) collective-permute-start(bf16[32,4096]{1,0:T(8,128)(2,1)} %get-tuple-element.41), channel_id=1, source_target_pairs={{0,8},{4,12},{8,0},{12,4},{16,24},{20,28},{24,16},{28,20},{1,9},{5... | collective-permute-start | bytes 786440 | tf_op jit(solution)/shard_map/ppermute | solution.py:67
  36.7 2.8 %copy-start.1 = (bf16[768,4096]{1,0:T(8,128)(2,1)S(1)}, bf16[768,4096]{1,0:T(8,128)(2,1)}, u32[]{:S(2)}) copy-start(bf16[768,4096]{1,0:T(8,128)(2,1)} %copy-done) | copy-start | bytes 18874372
  45.1 7.8 %collective-permute-start.12 = (bf16[32,4096]{1,0:T(8,128)(2,1)S(1)}, bf16[32,4096]{1,0:T(8,128)(2,1)S(1)}, u32[]{:S(2)}, u32[]{:S(2)}) collective-permute-start(bf16[32,4096]{1,0:T(8,128)(2,1)S(1)} %get-tuple-element.58), channel_id=1, source_target_pairs={{0,16},{4,20},{8,24},{12,28},{16,0},{20,4},{24,8},{28,12},{1,17},{... | collective-permute-start | bytes 786440 | tf_op jit(solution)/shard_map/ppermute | solution.py:67
  50.8 7.8 %collective-permute-start.10 = (bf16[32,4096]{1,0:T(8,128)(2,1)S(1)}, bf16[32,4096]{1,0:T(8,128)(2,1)S(1)}, u32[]{:S(2)}, u32[]{:S(2)}) collective-permute-start(bf16[32,4096]{1,0:T(8,128)(2,1)S(1)} %get-tuple-element.59), channel_id=1, source_target_pairs={{0,16},{4,20},{8,24},{12,28},{16,0},{20,4},{24,8},{28,12},{1,17},{... | collective-permute-start | bytes 786440 | tf_op jit(solution)/shard_map/ppermute | solution.py:67
  53.1 7.3 %collective-permute-start.15 = (bf16[16,4096]{1,0:T(8,128)(2,1)S(1)}, bf16[16,4096]{1,0:T(8,128)(2,1)S(1)}, u32[]{:S(2)}, u32[]{:S(2)}) collective-permute-start(bf16[16,4096]{1,0:T(8,128)(2,1)S(1)} %select_convert_fusion.2), channel_id=1, source_target_pairs={{0,1},{1,0},{2,3},{3,2},{4,5},{5,4},{6,7},{7,6},{8,9},{9,8},{10,11... | collective-permute-start | bytes 393224 | tf_op jit(solution)/shard_map/ppermute | solution.py:71
  55.8 7.1 %collective-permute-start.14 = (bf16[32,4096]{1,0:T(8,128)(2,1)S(1)}, bf16[32,4096]{1,0:T(8,128)(2,1)S(1)}, u32[]{:S(2)}, u32[]{:S(2)}) collective-permute-start(bf16[32,4096]{1,0:T(8,128)(2,1)S(1)} %get-tuple-element.56), channel_id=1, source_target_pairs={{0,16},{4,20},{8,24},{12,28},{16,0},{20,4},{24,8},{28,12},{1,17},{... | collective-permute-start | bytes 786440 | tf_op jit(solution)/shard_map/ppermute | solution.py:67
  58.7 5.9 %collective-permute-start.13 = (bf16[16,4096]{1,0:T(8,128)(2,1)S(1)}, bf16[16,4096]{1,0:T(8,128)(2,1)S(1)}, u32[]{:S(2)}, u32[]{:S(2)}) collective-permute-start(bf16[16,4096]{1,0:T(8,128)(2,1)S(1)} %select_convert_fusion.1), channel_id=1, source_target_pairs={{0,1},{1,0},{2,3},{3,2},{4,5},{5,4},{6,7},{7,6},{8,9},{9,8},{10,11... | collective-permute-start | bytes 393224 | tf_op jit(solution)/shard_map/ppermute | solution.py:71
  60.4 14.6 %collective-permute-start.17 = (bf16[16,4096]{1,0:T(8,128)(2,1)S(1)}, bf16[16,4096]{1,0:T(8,128)(2,1)S(1)}, u32[]{:S(2)}, u32[]{:S(2)}) collective-permute-start(bf16[16,4096]{1,0:T(8,128)(2,1)S(1)} %fusion.4), channel_id=1, source_target_pairs={{0,3},{3,0},{1,2},{2,1},{4,7},{7,4},{5,6},{6,5},{8,11},{11,8},{9,1... | collective-permute-start | bytes 393224 | tf_op jit(solution)/shard_map/ppermute | solution.py:71
  63.0 6.1 %collective-permute-start.18 = (bf16[16,4096]{1,0:T(8,128)(2,1)S(1)}, bf16[16,4096]{1,0:T(8,128)(2,1)S(1)}, u32[]{:S(2)}, u32[]{:S(2)}) collective-permute-start(bf16[16,4096]{1,0:T(8,128)(2,1)S(1)} %select_convert_fusion), channel_id=1, source_target_pairs={{0,1},{1,0},{2,3},{3,2},{4,5},{5,4},{6,7},{7,6},{8,9},{9,8},{10,11... | collective-permute-start | bytes 393224 | tf_op jit(solution)/shard_map/ppermute | solution.py:71
  64.6 10.6 %collective-permute-start.16 = (bf16[16,4096]{1,0:T(8,128)(2,1)S(1)}, bf16[16,4096]{1,0:T(8,128)(2,1)S(1)}, u32[]{:S(2)}, u32[]{:S(2)}) collective-permute-start(bf16[16,4096]{1,0:T(8,128)(2,1)S(1)} %fusion.5), channel_id=1, source_target_pairs={{0,3},{3,0},{1,2},{2,1},{4,7},{7,4},{5,6},{6,5},{8,11},{11,8},{9,1... | collective-permute-start | bytes 393224 | tf_op jit(solution)/shard_map/ppermute | solution.py:71
  69.2 10.0 %collective-permute-start.20 = (bf16[16,4096]{1,0:T(8,128)(2,1)S(1)}, bf16[16,4096]{1,0:T(8,128)(2,1)S(1)}, u32[]{:S(2)}, u32[]{:S(2)}) collective-permute-start(bf16[16,4096]{1,0:T(8,128)(2,1)S(1)} %fusion.6), channel_id=1, source_target_pairs={{0,3},{3,0},{1,2},{2,1},{4,7},{7,4},{5,6},{6,5},{8,11},{11,8},{9,1... | collective-permute-start | bytes 393224 | tf_op jit(solution)/shard_map/ppermute | solution.py:71
  75.1 8.5 %collective-permute-start.22 = (bf16[16,4096]{1,0:T(8,128)(2,1)S(1)}, bf16[16,4096]{1,0:T(8,128)(2,1)S(1)}, u32[]{:S(2)}, u32[]{:S(2)}) collective-permute-start(bf16[16,4096]{1,0:T(8,128)(2,1)S(1)} %add_convert_fusion.5), channel_id=1, source_target_pairs={{0,1},{1,0},{2,3},{3,2},{4,5},{5,4},{6,7},{7,6},{8,9},{9,8},{10,11... | collective-permute-start | bytes 393224 | tf_op jit(solution)/shard_map/ppermute | solution.py:71
  75.2 7.6 %collective-permute-start.19 = (bf16[16,4096]{1,0:T(8,128)(2,1)S(1)}, bf16[16,4096]{1,0:T(8,128)(2,1)S(1)}, u32[]{:S(2)}, u32[]{:S(2)}) collective-permute-start(bf16[16,4096]{1,0:T(8,128)(2,1)S(1)} %add_convert_fusion.4), channel_id=1, source_target_pairs={{0,1},{1,0},{2,3},{3,2},{4,5},{5,4},{6,7},{7,6},{8,9},{9,8},{10,11... | collective-permute-start | bytes 393224 | tf_op jit(solution)/shard_map/ppermute | solution.py:71
  79.2 5.2 %collective-permute-start.21 = (bf16[16,4096]{1,0:T(8,128)(2,1)S(1)}, bf16[16,4096]{1,0:T(8,128)(2,1)S(1)}, u32[]{:S(2)}, u32[]{:S(2)}) collective-permute-start(bf16[16,4096]{1,0:T(8,128)(2,1)S(1)} %add_convert_fusion.3), channel_id=1, source_target_pairs={{0,1},{1,0},{2,3},{3,2},{4,5},{5,4},{6,7},{7,6},{8,9},{9,8},{10,11... | collective-permute-start | bytes 393224 | tf_op jit(solution)/shard_map/ppermute | solution.py:71

commit v6 on v5

--- a/solution.py
+++ b/solution.py
@@ -74,7 +74,7 @@
 CORE, X, Y = 1, 2, 4
 PAIRS = [(0, 1), (1, 0), (2, 3), (3, 2)]
 ACROSS = [(0, 3), (3, 0), (1, 2), (2, 1)]
-SPAN = 512
+SPAN = 1024
 VMEM_LIMIT = 8 * 2**20
 
 
@@ -141,10 +141,10 @@
         left = [ref[low:high, columns] for ref in weights]
         left = left[0] if len(left) == 1 else jnp.concatenate(left)
         for which, source in enumerate(sources):
-            part = contract(left, source[:, columns])
+            part = contract(source[:, columns], left)
             old = totals[which]
             totals[which] = part if old is None else old + part
-    return totals
+    return [total.T for total in totals]
 
 
 def sums_into(lefts, sources, outs):
@@ -322,7 +322,7 @@
         return results[k]
 
     stages = [leave_stage, swap_stage, across_stage, back_stage, result_stage]
-    steps = ((0, 0), (1, 0), (0, 1), (2, 0), (1, 1), (0, 2), (2, 1), (1, 2), (2, 2), (0, 3), (1, 3), (2, 3), (1, 4), (0, 4), (2, 4))
+    steps = ((0, 0), (1, 0), (0, 1), (2, 0), (1, 1), (0, 2), (2, 1), (1, 2), (2, 2), (0, 3), (1, 3), (2, 3), (0, 4), (1, 4), (2, 4))
     for k, at in steps:
         turn = stages[at](order[k])
     return results[0], results[1], results[2]

time: 85.4 us -> 85.1 us (level)
  Pallas kernels: 18.3 us -> 17.4 us
    pallas_call x4, Pallas kernels: 14.4 us -> 13.4 us  [kernel_call(): pl.pallas_call(inner, out_shape=[sent(shape, dtype) if shape[-1] == width...]
  transfers between devices with their start and end apart: 23 -> 23, of which waited for: 8 -> 11; matrix products, arithmetic and copies ran while one was open for 7% -> 7% of each run, Pallas kernels for 22% -> 20%
where the time goes in v6:
time: 85.1 us; the launch traced here: 84.8 us
  starting transfers between devices  43.6 us (51%)
  Pallas kernels  17.4 us (20%)
  waiting for transfers between devices  13.8 us (16%)
  other arithmetic  6.31 us (7%)
  local copies, waits for them, and re-layouts  2.87 us (3%)
    ppermute x12, starting transfers between devices, hop(): return lax.ppermute(block, 'section', route)  22.1 us
    ppermute x9, starting transfers between devices, along(): return lax.ppermute(block, 'dp', route)  18.4 us
    pallas_call x4, Pallas kernels, kernel_call(): pl.pallas_call(inner, out_shape=[sent(shape, dtype) if shape[-1] == width...  13.4 us
    ppermute x12, waiting for transfers between devices, hop(): return lax.ppermute(block, 'section', route)  6.97 us
    ppermute x9, waiting for transfers between devices, along(): return lax.ppermute(block, 'dp', route)  6.8 us
    pallas_call x2, Pallas kernels, on_chip(): pl.pallas_call(kernel, out_shape=pltpu.VMEM((rows, parts[0].shape[1]), pa...  4 us
    ppermute x2, starting transfers between devices, spread(): return (lax.ppermute(own, 'section', v), lax.ppermute(own, 'section', u))  3.08 us
    unnamed x4, local copies, waits for them, and re-layouts  2.79 us
  transfers between devices with their start and end apart: 23, of which 11 were waited for; matrix products, arithmetic and copies ran while one was open for 7% of the time, Pallas kernels for 20%

profile of v6, /device:TPU:0, one launch (start us, length us, event | category | flops | bytes accessed | tf_op | source)
XLA Modules:
  0.0 84.8 jit_solution(12340665231628398034)
XLA Ops:
  0.6 0.5 collective-permute-start.2
  1.1 0.1 collective-permute-start.3
  1.2 1.1 %shard_map.76 = bf16[96,4096]{1,0:T(8,128)(2,1)S(1)} custom-call(bf16[32,4096]{1,0:T(8,128)(2,1)} %refs_0_.2, bf16[32,4096]{1,0:T(8,128)(2,1)} %refs_1_.1, bf16[32,4096]{1,0:T(8,128)(2,1)} %refs_2_.2), custom_call_target="tpu_custom_call" | custom-call | flops 1 | bytes 1 | tf_op jit(solution)/shard_map/pallas_call | solution.py:100
  2.4 2.7 %collective-permute-start = (bf16[96,4096]{1,0:T(8,128)(2,1)S(1)}, bf16[96,4096]{1,0:T(8,128)(2,1)S(1)}, u32[]{:S(2)}, u32[]{:S(2)}) collective-permute-start(bf16[96,4096]{1,0:T(8,128)(2,1)S(1)} %shard_map.76), channel_id=1, source_target_pairs={{0,20},{4,8},{8,12},{12,0},{16,4},{20,24},{24,28},{28,16},{1,21},{... | collective-permute-start | bytes 2359304 | tf_op jit(solution)/shard_map/ppermute | solution.py:206
  5.1 0.4 collective-permute-start.1
  5.5 0.1 collective-permute-start.5
  5.6 0.1 pad_add_fusion
  5.6 0.1 fusion.3
  5.7 0.1 broadcast_subtract_fusion
  5.8 0.1 sub.37
  5.9 0.1 add_convert_fusion.6.refs_0_
  6.0 0.8 collective-permute-done.3.refs_3_
  6.8 2.9 %shard_map.77.refs_3_.refs_2_ = bf16[768,4096]{1,0:T(8,128)(2,1)S(1)} custom-call(bf16[192,4096]{1,0:T(8,128)(2,1)} %refs_0_.3, bf16[192,4096]{1,0:T(8,128)(2,1)} %collective-permute-done.2.refs_1_, bf16[192,4096]{1,0:T(8,128)(2,1)} %refs_2_.3, bf16[192,4096]{1,0:T(8,128)(2,1)} %collective-permute-done.3.refs_3_), custom_call_target="tpu_custom_call" | custom-call | flops 1 | bytes 1 | tf_op jit(solution)/shard_map/pallas_call | solution.py:100
  9.7 0.0 collective-permute-done.5.refs_1_
  9.7 3.2 %shard_map.80 = bf16[96,4096]{1,0:T(8,128)(2,1)} custom-call(s32[10]{0:T(128)S(1)} %add_convert_fusion.6.refs_0_, bf16[96,4096]{1,0:T(8,128)(2,1)S(1)} %collective-permute-done.5.refs_1_, bf16[768,4096]{1,0:T(8,128)(2,1)S(1)} %shard_map.77.refs_3_.refs_2_), custom_call_target="tpu_custom_call" | custom-call | flops 1 | bytes 8388608 | tf_op jit(solution)/shard_map/pallas_call | solution.py:121
  12.8 0.0 collective-permute-done.1.refs_1_
  12.8 2.9 %collective-permute-start.7 = (bf16[96,4096]{1,0:T(8,128)(2,1)S(1)}, bf16[96,4096]{1,0:T(8,128)(2,1)S(1)}, u32[]{:S(2)}, u32[]{:S(2)}) collective-permute-start(bf16[96,4096]{1,0:T(8,128)(2,1)S(1)} %collective-permute-done.1.refs_1_), channel_id=1, source_target_pairs={{0,16},{4,12},{8,24},{12,4},{16,0},{20,28},{24,8},{28,20},{1,17},{... | collective-permute-start | bytes 2359304 | tf_op jit(solution)/shard_map/ppermute | solution.py:67
  15.7 2.4 %shard_map.78.refs_2_ = bf16[4,96,192]{2,1,0:T(8,128)(2,1)S(1)} custom-call(s32[10]{0:T(128)S(1)} %add_convert_fusion.6.refs_0_, bf16[96,4096]{1,0:T(8,128)(2,1)S(1)} %collective-permute-done.1.refs_1_, bf16[96,4096]{1,0:T(8,128)(2,1)S(1)} %collective-permute-done.refs_2_, bf16[768,4096]{1,0:T(8,128)(2,1)S(1)} %shard_map.77.refs_3_.refs_2_), custom_call_target="tpu_custom_call" | custom-call | flops 1 | bytes 8388608 | tf_op jit(solution)/shard_map/pallas_call | solution.py:121
  18.2 3.0 %collective-permute-start.4 = (bf16[96,4096]{1,0:T(8,128)(2,1)S(1)}, bf16[96,4096]{1,0:T(8,128)(2,1)S(1)}, u32[]{:S(2)}, u32[]{:S(2)}) collective-permute-start(bf16[96,4096]{1,0:T(8,128)(2,1)S(1)} %collective-permute-done.refs_2_), channel_id=1, source_target_pairs={{0,16},{8,24},{16,0},{24,8},{1,17},{9,25},{17,1},{25,9},{2,18},{10... | collective-permute-start | bytes 2359304 | tf_op jit(solution)/shard_map/ppermute | solution.py:67
  21.1 5.1 %collective-permute-start.6 = (bf16[96,4096]{1,0:T(8,128)(2,1)}, bf16[96,4096]{1,0:T(8,128)(2,1)}, u32[]{:S(2)}, u32[]{:S(2)}) collective-permute-start(bf16[96,4096]{1,0:T(8,128)(2,1)} %shard_map.80), channel_id=1, source_target_pairs={{0,8},{8,0},{16,24},{24,16},{1,9},{9,1},{17,25},{25,17},{2,10},{10... | collective-permute-start | bytes 2359304 | tf_op jit(solution)/shard_map/ppermute | solution.py:67
  26.3 0.0 collective-permute-done.7.refs_1_
  26.3 4.3 %shard_map.81 = (bf16[32,4096]{1,0:T(8,128)(2,1)}, bf16[32,4096]{1,0:T(8,128)(2,1)}, bf16[32,4096]{1,0:T(8,128)(2,1)}) custom-call(s32[10]{0:T(128)S(1)} %add_convert_fusion.6.refs_0_, bf16[96,4096]{1,0:T(8,128)(2,1)S(1)} %collective-permute-done.7.refs_1_, bf16[768,4096]{1,0:T(8,128)(2,1)S(1)} %shard_map.77.refs_3_.refs_2_), custom_call_target="tpu_custom_call" | custom-call | flops 1 | bytes 8388608 | tf_op jit(solution)/shard_map/pallas_call | solution.py:121
  30.6 3.7 %collective-permute-start.9 = (bf16[32,4096]{1,0:T(8,128)(2,1)}, bf16[32,4096]{1,0:T(8,128)(2,1)S(1)}, u32[]{:S(2)}, u32[]{:S(2)}) collective-permute-start(bf16[32,4096]{1,0:T(8,128)(2,1)} %get-tuple-element.34), channel_id=1, source_target_pairs={{0,8},{4,12},{8,0},{12,4},{16,24},{20,28},{24,16},{28,20},{1,9},{5... | collective-permute-start | bytes 786440 | tf_op jit(solution)/shard_map/ppermute | solution.py:67
  34.3 0.0 collective-permute-start.8
  34.3 2.0 %collective-permute-start.11 = (bf16[32,4096]{1,0:T(8,128)(2,1)}, bf16[32,4096]{1,0:T(8,128)(2,1)S(1)}, u32[]{:S(2)}, u32[]{:S(2)}) collective-permute-start(bf16[32,4096]{1,0:T(8,128)(2,1)} %get-tuple-element.41), channel_id=1, source_target_pairs={{0,8},{4,12},{8,0},{12,4},{16,24},{20,28},{24,16},{28,20},{1,9},{5... | collective-permute-start | bytes 786440 | tf_op jit(solution)/shard_map/ppermute | solution.py:67
  36.3 0.0 collective-permute-done.4.refs_1_
  36.3 2.8 %copy-done.1 = bf16[768,4096]{1,0:T(8,128)(2,1)S(1)} copy-done((bf16[768,4096]{1,0:T(8,128)(2,1)S(1)}, bf16[768,4096]{1,0:T(8,128)(2,1)}, u32[]{:S(2)}) %copy-start.1) | copy-done | bytes 6291480
  39.1 3.5 %shard_map.79 = (f32[32,4096]{1,0:T(8,128)S(1)}, f32[32,4096]{1,0:T(8,128)S(1)}, f32[32,4096]{1,0:T(8,128)S(1)}, f32[32,4096]{1,0:T(8,128)S(1)}, f32[32,4096]{1,0:T(8,128)S(1)}, /*index=5*/f32[32,4096]{1,0:T(8,128)S(1)}) custom-call(s32[10]{0:T(128)S(1)} %add_convert_fusion.6.refs_0_, bf16[96,4096]{1,0:T(8,128)(2,1)S(1)} %collective-permute-done.4.refs_1_, ...), custom_call_target="tpu_custom_call" | custom-call | flops 1 | bytes 8388608 | tf_op jit(solution)/shard_map/pallas_call | solution.py:121
  42.6 1.2 %collective-permute-done.9 = bf16[32,4096]{1,0:T(8,128)(2,1)S(1)} collective-permute-done((bf16[32,4096]{1,0:T(8,128)(2,1)}, bf16[32,4096]{1,0:T(8,128)(2,1)S(1)}, u32[]{:S(2)}, u32[]{:S(2)}) %collective-permute-start.9) | collective-permute-done | bytes 262176 | tf_op jit(solution)/shard_map/ppermute | solution.py:67
  43.8 0.0 collective-permute-done.6
  43.8 1.1 %convert_add_fusion.4 = (f32[32,4096]{1,0:T(8,128)S(1)}, bf16[32,4096]{1,0:T(8,128)(2,1)S(1)}) fusion(f32[32,4096]{1,0:T(8,128)S(1)} %get-tuple-element.38, bf16[32,4096]{1,0:T(8,128)(2,1)S(1)} %collective-permute-done.9, pred[]{:T(512)} %eq.30, bf16[96,4096]{1,0:T(8,128)(2,1)} %collective-permute-done.6, f32[32,4096]{1,0:T(8,128)S(1)} %get-tuple-element.33), kind=kLoop, calls=%fused_computation.5 | loop fusion | flops 917504 | bytes 2359297 | tf_op jit(solution)/shard_map/add | solution.py:294
  44.9 1.6 %collective-permute-start.12 = (bf16[32,4096]{1,0:T(8,128)(2,1)S(1)}, bf16[32,4096]{1,0:T(8,128)(2,1)S(1)}, u32[]{:S(2)}, u32[]{:S(2)}) collective-permute-start(bf16[32,4096]{1,0:T(8,128)(2,1)S(1)} %get-tuple-element.58), channel_id=1, source_target_pairs={{0,16},{4,20},{8,24},{12,28},{16,0},{20,4},{24,8},{28,12},{1,17},{... | collective-permute-start | bytes 786440 | tf_op jit(solution)/shard_map/ppermute | solution.py:67
  46.4 3.0 %collective-permute-done.8 = bf16[32,4096]{1,0:T(8,128)(2,1)S(1)} collective-permute-done((bf16[32,4096]{1,0:T(8,128)(2,1)}, bf16[32,4096]{1,0:T(8,128)(2,1)S(1)}, u32[]{:S(2)}, u32[]{:S(2)}) %collective-permute-start.8) | collective-permute-done | bytes 262176 | tf_op jit(solution)/shard_map/ppermute | solution.py:67
  49.4 1.1 %add_convert_fusion.1 = (bf16[32,4096]{1,0:T(8,128)(2,1)S(1)}, f32[32,4096]{1,0:T(8,128)S(1)}) fusion(f32[32,4096]{1,0:T(8,128)S(1)} %get-tuple-element.35, bf16[32,4096]{1,0:T(8,128)(2,1)S(1)} %collective-permute-done.8, pred[]{:T(512)} %eq.30, bf16[96,4096]{1,0:T(8,128)(2,1)} %collective-permute-done.6, f32[32,4096]{1,0:T(8,128)S(1)} %get-tuple-element.30), kind=kLoop, calls=%fused_computation.6 | loop fusion | flops 917504 | bytes 2359297 | tf_op jit(solution)/shard_map/convert_element_type | solution.py:292
  50.5 1.6 %collective-permute-start.10 = (bf16[32,4096]{1,0:T(8,128)(2,1)S(1)}, bf16[32,4096]{1,0:T(8,128)(2,1)S(1)}, u32[]{:S(2)}, u32[]{:S(2)}) collective-permute-start(bf16[32,4096]{1,0:T(8,128)(2,1)S(1)} %get-tuple-element.59), channel_id=1, source_target_pairs={{0,16},{4,20},{8,24},{12,28},{16,0},{20,4},{24,8},{28,12},{1,17},{... | collective-permute-start | bytes 786440 | tf_op jit(solution)/shard_map/ppermute | solution.py:67
  52.1 0.7 collective-permute-done.12
  52.9 1.6 %collective-permute-start.15 = (bf16[16,4096]{1,0:T(8,128)(2,1)S(1)}, bf16[16,4096]{1,0:T(8,128)(2,1)S(1)}, u32[]{:S(2)}, u32[]{:S(2)}) collective-permute-start(bf16[16,4096]{1,0:T(8,128)(2,1)S(1)} %select_convert_fusion.2), channel_id=1, source_target_pairs={{0,1},{1,0},{2,3},{3,2},{4,5},{5,4},{6,7},{7,6},{8,9},{9,8},{10,11... | collective-permute-start | bytes 393224 | tf_op jit(solution)/shard_map/ppermute | solution.py:71
  54.5 1.1 %convert_add_fusion.1 = (f32[32,4096]{1,0:T(8,128)S(1)}, bf16[32,4096]{1,0:T(8,128)(2,1)S(1)}) fusion(f32[32,4096]{1,0:T(8,128)S(1)} %get-tuple-element.37, bf16[32,4096]{1,0:T(8,128)(2,1)S(1)} %collective-permute-done.11, pred[]{:T(512)} %eq.30, bf16[96,4096]{1,0:T(8,128)(2,1)} %collective-permute-done.6, f32[32,4096]{1,0:T(8,128)S(1)} %get-tuple-element.36), kind=kLoop, calls=%fused_computation.1 | loop fusion | flops 917504 | bytes 2359297 | tf_op jit(solution)/shard_map/add | solution.py:294
  55.6 1.6 %collective-permute-start.14 = (bf16[32,4096]{1,0:T(8,128)(2,1)S(1)}, bf16[32,4096]{1,0:T(8,128)(2,1)S(1)}, u32[]{:S(2)}, u32[]{:S(2)}) collective-permute-start(bf16[32,4096]{1,0:T(8,128)(2,1)S(1)} %get-tuple-element.56), channel_id=1, source_target_pairs={{0,16},{4,20},{8,24},{12,28},{16,0},{20,4},{24,8},{28,12},{1,17},{... | collective-permute-start | bytes 786440 | tf_op jit(solution)/shard_map/ppermute | solution.py:67
  57.1 1.3 %collective-permute-done.10 = bf16[32,4096]{1,0:T(8,128)(2,1)S(1)} collective-permute-done((bf16[32,4096]{1,0:T(8,128)(2,1)S(1)}, bf16[32,4096]{1,0:T(8,128)(2,1)S(1)}, u32[]{:S(2)}, u32[]{:S(2)}) %collective-permute-start.10) | collective-permute-done | bytes 262176 | tf_op jit(solution)/shard_map/ppermute | solution.py:67
  58.4 0.1 convert_add_fusion.2
  58.5 1.6 %collective-permute-start.13 = (bf16[16,4096]{1,0:T(8,128)(2,1)S(1)}, bf16[16,4096]{1,0:T(8,128)(2,1)S(1)}, u32[]{:S(2)}, u32[]{:S(2)}) collective-permute-start(bf16[16,4096]{1,0:T(8,128)(2,1)S(1)} %select_convert_fusion.1), channel_id=1, source_target_pairs={{0,1},{1,0},{2,3},{3,2},{4,5},{5,4},{6,7},{7,6},{8,9},{9,8},{10,11... | collective-permute-start | bytes 393224 | tf_op jit(solution)/shard_map/ppermute | solution.py:71
  60.1 0.0 collective-permute-done.15
  60.2 2.5 %collective-permute-start.17 = (bf16[16,4096]{1,0:T(8,128)(2,1)S(1)}, bf16[16,4096]{1,0:T(8,128)(2,1)S(1)}, u32[]{:S(2)}, u32[]{:S(2)}) collective-permute-start(bf16[16,4096]{1,0:T(8,128)(2,1)S(1)} %fusion.4), channel_id=1, source_target_pairs={{0,3},{3,0},{1,2},{2,1},{4,7},{7,4},{5,6},{6,5},{8,11},{11,8},{9,1... | collective-permute-start | bytes 393224 | tf_op jit(solution)/shard_map/ppermute | solution.py:71
  62.7 0.0 collective-permute-done.14
  62.8 1.5 %collective-permute-start.18 = (bf16[16,4096]{1,0:T(8,128)(2,1)S(1)}, bf16[16,4096]{1,0:T(8,128)(2,1)S(1)}, u32[]{:S(2)}, u32[]{:S(2)}) collective-permute-start(bf16[16,4096]{1,0:T(8,128)(2,1)S(1)} %select_convert_fusion), channel_id=1, source_target_pairs={{0,1},{1,0},{2,3},{3,2},{4,5},{5,4},{6,7},{7,6},{8,9},{9,8},{10,11... | collective-permute-start | bytes 393224 | tf_op jit(solution)/shard_map/ppermute | solution.py:71
  64.2 0.1 collective-permute-done.13
  64.4 2.8 %collective-permute-start.16 = (bf16[16,4096]{1,0:T(8,128)(2,1)S(1)}, bf16[16,4096]{1,0:T(8,128)(2,1)S(1)}, u32[]{:S(2)}, u32[]{:S(2)}) collective-permute-start(bf16[16,4096]{1,0:T(8,128)(2,1)S(1)} %fusion.5), channel_id=1, source_target_pairs={{0,3},{3,0},{1,2},{2,1},{4,7},{7,4},{5,6},{6,5},{8,11},{11,8},{9,1... | collective-permute-start | bytes 393224 | tf_op jit(solution)/shard_map/ppermute | solution.py:71
  67.2 1.7 %collective-permute-done.18 = bf16[16,4096]{1,0:T(8,128)(2,1)S(1)} collective-permute-done((bf16[16,4096]{1,0:T(8,128)(2,1)S(1)}, bf16[16,4096]{1,0:T(8,128)(2,1)S(1)}, u32[]{:S(2)}, u32[]{:S(2)}) %collective-permute-start.18) | collective-permute-done | bytes 131104 | tf_op jit(solution)/shard_map/ppermute | solution.py:71
  69.0 5.6 %collective-permute-start.21 = (bf16[16,4096]{1,0:T(8,128)(2,1)S(1)}, bf16[16,4096]{1,0:T(8,128)(2,1)S(1)}, u32[]{:S(2)}, u32[]{:S(2)}) collective-permute-start(bf16[16,4096]{1,0:T(8,128)(2,1)S(1)} %fusion.6), channel_id=1, source_target_pairs={{0,3},{3,0},{1,2},{2,1},{4,7},{7,4},{5,6},{6,5},{8,11},{11,8},{9,1... | collective-permute-start | bytes 393224 | tf_op jit(solution)/shard_map/ppermute | solution.py:71
  74.6 0.0 collective-permute-done.17
  74.6 0.1 add_convert_fusion.5
  74.7 0.1 collective-permute-start.20
  74.8 0.1 add_convert_fusion.4
  74.8 2.1 %collective-permute-start.19 = (bf16[16,4096]{1,0:T(8,128)(2,1)S(1)}, bf16[16,4096]{1,0:T(8,128)(2,1)S(1)}, u32[]{:S(2)}, u32[]{:S(2)}) collective-permute-start(bf16[16,4096]{1,0:T(8,128)(2,1)S(1)} %add_convert_fusion.4), channel_id=1, source_target_pairs={{0,1},{1,0},{2,3},{3,2},{4,5},{5,4},{6,7},{7,6},{8,9},{9,8},{10,11... | collective-permute-start | bytes 393224 | tf_op jit(solution)/shard_map/ppermute | solution.py:71
  76.9 1.5 %collective-permute-done.21 = bf16[16,4096]{1,0:T(8,128)(2,1)S(1)} collective-permute-done((bf16[16,4096]{1,0:T(8,128)(2,1)S(1)}, bf16[16,4096]{1,0:T(8,128)(2,1)S(1)}, u32[]{:S(2)}, u32[]{:S(2)}) %collective-permute-start.21) | collective-permute-done | bytes 131104 | tf_op jit(solution)/shard_map/ppermute | solution.py:71
  78.5 0.1 add_convert_fusion.3
  78.5 0.6 collective-permute-start.22
  79.1 1.8 %collective-permute-done.20 = bf16[16,4096]{1,0:T(8,128)(2,1)S(1)} collective-permute-done((bf16[16,4096]{1,0:T(8,128)(2,1)S(1)}, bf16[16,4096]{1,0:T(8,128)(2,1)S(1)}, u32[]{:S(2)}, u32[]{:S(2)}) %collective-permute-start.20) | collective-permute-done | bytes 131104 | tf_op jit(solution)/shard_map/ppermute | solution.py:71
  80.9 0.7 pad_maximum_fusion
  81.6 1.0 %collective-permute-done.19 = bf16[16,4096]{1,0:T(8,128)(2,1)S(1)} collective-permute-done((bf16[16,4096]{1,0:T(8,128)(2,1)S(1)}, bf16[16,4096]{1,0:T(8,128)(2,1)S(1)}, u32[]{:S(2)}, u32[]{:S(2)}) %collective-permute-start.19) | collective-permute-done | bytes 131104 | tf_op jit(solution)/shard_map/ppermute | solution.py:71
  82.6 0.7 pad_maximum_fusion.1
  83.3 0.7 collective-permute-done.22
  84.0 0.7 pad_maximum_fusion.2
  (19 shorter events, 0.4 us)
Async XLA Ops:
  0.6 5.3 %collective-permute-start.2 = (bf16[192,4096]{1,0:T(8,128)(2,1)}, bf16[192,4096]{1,0:T(8,128)(2,1)}, u32[]{:S(2)}, u32[]{:S(2)}) collective-permute-start(bf16[192,4096]{1,0:T(8,128)(2,1)} %refs_0_.3), channel_id=1, source_target_pairs={{0,4},{4,0},{8,12},{12,8},{16,20},{20,16},{24,28},{28,24},{1,5},{5... | collective-permute-start | bytes 4718600 | tf_op jit(solution)/shard_map/ppermute | solution.py:67
  1.1 5.6 %collective-permute-start.3 = (bf16[192,4096]{1,0:T(8,128)(2,1)}, bf16[192,4096]{1,0:T(8,128)(2,1)}, u32[]{:S(2)}, u32[]{:S(2)}) collective-permute-start(bf16[192,4096]{1,0:T(8,128)(2,1)} %refs_2_.3), channel_id=1, source_target_pairs={{0,4},{4,0},{8,12},{12,8},{16,20},{20,16},{24,28},{28,24},{1,5},{5... | collective-permute-start | bytes 4718600 | tf_op jit(solution)/shard_map/ppermute | solution.py:67
  2.4 13.4 %collective-permute-start = (bf16[96,4096]{1,0:T(8,128)(2,1)S(1)}, bf16[96,4096]{1,0:T(8,128)(2,1)S(1)}, u32[]{:S(2)}, u32[]{:S(2)}) collective-permute-start(bf16[96,4096]{1,0:T(8,128)(2,1)S(1)} %shard_map.76), channel_id=1, source_target_pairs={{0,20},{4,8},{8,12},{12,0},{16,4},{20,24},{24,28},{28,16},{1,21},{... | collective-permute-start | bytes 2359304 | tf_op jit(solution)/shard_map/ppermute | solution.py:206
  5.1 7.8 %collective-permute-start.1 = (bf16[96,4096]{1,0:T(8,128)(2,1)S(1)}, bf16[96,4096]{1,0:T(8,128)(2,1)S(1)}, u32[]{:S(2)}, u32[]{:S(2)}) collective-permute-start(bf16[96,4096]{1,0:T(8,128)(2,1)S(1)} %shard_map.76), channel_id=1, source_target_pairs={{0,4},{4,0},{8,28},{12,8},{16,20},{20,16},{24,12},{28,24},{1,5},{5... | collective-permute-start | bytes 2359304 | tf_op jit(solution)/shard_map/ppermute | solution.py:206
  5.5 4.2 %collective-permute-start.5 = (bf16[96,4096]{1,0:T(8,128)(2,1)S(1)}, bf16[96,4096]{1,0:T(8,128)(2,1)S(1)}, u32[]{:S(2)}, u32[]{:S(2)}) collective-permute-start(bf16[96,4096]{1,0:T(8,128)(2,1)S(1)} %shard_map.76), channel_id=1, source_target_pairs={{0,4},{4,0},{8,12},{12,8},{16,20},{20,16},{24,28},{28,24},{1,5},{5... | collective-permute-start | bytes 2359304 | tf_op jit(solution)/shard_map/ppermute | solution.py:67
  9.7 16.6 %copy-start = (bf16[768,4096]{1,0:T(8,128)(2,1)}, bf16[768,4096]{1,0:T(8,128)(2,1)S(1)}, u32[]{:S(2)}) copy-start(bf16[768,4096]{1,0:T(8,128)(2,1)S(1)} %shard_map.77.refs_3_.refs_2_) | copy-start | bytes 18874372
  12.8 13.4 %collective-permute-start.7 = (bf16[96,4096]{1,0:T(8,128)(2,1)S(1)}, bf16[96,4096]{1,0:T(8,128)(2,1)S(1)}, u32[]{:S(2)}, u32[]{:S(2)}) collective-permute-start(bf16[96,4096]{1,0:T(8,128)(2,1)S(1)} %collective-permute-done.1.refs_1_), channel_id=1, source_target_pairs={{0,16},{4,12},{8,24},{12,4},{16,0},{20,28},{24,8},{28,20},{1,17},{... | collective-permute-start | bytes 2359304 | tf_op jit(solution)/shard_map/ppermute | solution.py:67
  18.2 18.1 %collective-permute-start.4 = (bf16[96,4096]{1,0:T(8,128)(2,1)S(1)}, bf16[96,4096]{1,0:T(8,128)(2,1)S(1)}, u32[]{:S(2)}, u32[]{:S(2)}) collective-permute-start(bf16[96,4096]{1,0:T(8,128)(2,1)S(1)} %collective-permute-done.refs_2_), channel_id=1, source_target_pairs={{0,16},{8,24},{16,0},{24,8},{1,17},{9,25},{17,1},{25,9},{2,18},{10... | collective-permute-start | bytes 2359304 | tf_op jit(solution)/shard_map/ppermute | solution.py:67
  21.1 22.6 %collective-permute-start.6 = (bf16[96,4096]{1,0:T(8,128)(2,1)}, bf16[96,4096]{1,0:T(8,128)(2,1)}, u32[]{:S(2)}, u32[]{:S(2)}) collective-permute-start(bf16[96,4096]{1,0:T(8,128)(2,1)} %shard_map.80), channel_id=1, source_target_pairs={{0,8},{8,0},{16,24},{24,16},{1,9},{9,1},{17,25},{25,17},{2,10},{10... | collective-permute-start | bytes 2359304 | tf_op jit(solution)/shard_map/ppermute | solution.py:67
  30.6 13.2 %collective-permute-start.9 = (bf16[32,4096]{1,0:T(8,128)(2,1)}, bf16[32,4096]{1,0:T(8,128)(2,1)S(1)}, u32[]{:S(2)}, u32[]{:S(2)}) collective-permute-start(bf16[32,4096]{1,0:T(8,128)(2,1)} %get-tuple-element.34), channel_id=1, source_target_pairs={{0,8},{4,12},{8,0},{12,4},{16,24},{20,28},{24,16},{28,20},{1,9},{5... | collective-permute-start | bytes 786440 | tf_op jit(solution)/shard_map/ppermute | solution.py:67
  34.3 15.1 %collective-permute-start.8 = (bf16[32,4096]{1,0:T(8,128)(2,1)}, bf16[32,4096]{1,0:T(8,128)(2,1)S(1)}, u32[]{:S(2)}, u32[]{:S(2)}) collective-permute-start(bf16[32,4096]{1,0:T(8,128)(2,1)} %get-tuple-element.32), channel_id=1, source_target_pairs={{0,8},{4,12},{8,0},{12,4},{16,24},{20,28},{24,16},{28,20},{1,9},{5... | collective-permute-start | bytes 786440 | tf_op jit(solution)/shard_map/ppermute | solution.py:67
  34.3 20.2 %collective-permute-start.11 = (bf16[32,4096]{1,0:T(8,128)(2,1)}, bf16[32,4096]{1,0:T(8,128)(2,1)S(1)}, u32[]{:S(2)}, u32[]{:S(2)}) collective-permute-start(bf16[32,4096]{1,0:T(8,128)(2,1)} %get-tuple-element.41), channel_id=1, source_target_pairs={{0,8},{4,12},{8,0},{12,4},{16,24},{20,28},{24,16},{28,20},{1,9},{5... | collective-permute-start | bytes 786440 | tf_op jit(solution)/shard_map/ppermute | solution.py:67
  36.3 2.8 %copy-start.1 = (bf16[768,4096]{1,0:T(8,128)(2,1)S(1)}, bf16[768,4096]{1,0:T(8,128)(2,1)}, u32[]{:S(2)}) copy-start(bf16[768,4096]{1,0:T(8,128)(2,1)} %copy-done) | copy-start | bytes 18874372
  44.9 7.9 %collective-permute-start.12 = (bf16[32,4096]{1,0:T(8,128)(2,1)S(1)}, bf16[32,4096]{1,0:T(8,128)(2,1)S(1)}, u32[]{:S(2)}, u32[]{:S(2)}) collective-permute-start(bf16[32,4096]{1,0:T(8,128)(2,1)S(1)} %get-tuple-element.58), channel_id=1, source_target_pairs={{0,16},{4,20},{8,24},{12,28},{16,0},{20,4},{24,8},{28,12},{1,17},{... | collective-permute-start | bytes 786440 | tf_op jit(solution)/shard_map/ppermute | solution.py:67
  50.5 7.9 %collective-permute-start.10 = (bf16[32,4096]{1,0:T(8,128)(2,1)S(1)}, bf16[32,4096]{1,0:T(8,128)(2,1)S(1)}, u32[]{:S(2)}, u32[]{:S(2)}) collective-permute-start(bf16[32,4096]{1,0:T(8,128)(2,1)S(1)} %get-tuple-element.59), channel_id=1, source_target_pairs={{0,16},{4,20},{8,24},{12,28},{16,0},{20,4},{24,8},{28,12},{1,17},{... | collective-permute-start | bytes 786440 | tf_op jit(solution)/shard_map/ppermute | solution.py:67
  52.9 7.3 %collective-permute-start.15 = (bf16[16,4096]{1,0:T(8,128)(2,1)S(1)}, bf16[16,4096]{1,0:T(8,128)(2,1)S(1)}, u32[]{:S(2)}, u32[]{:S(2)}) collective-permute-start(bf16[16,4096]{1,0:T(8,128)(2,1)S(1)} %select_convert_fusion.2), channel_id=1, source_target_pairs={{0,1},{1,0},{2,3},{3,2},{4,5},{5,4},{6,7},{7,6},{8,9},{9,8},{10,11... | collective-permute-start | bytes 393224 | tf_op jit(solution)/shard_map/ppermute | solution.py:71
  55.6 7.1 %collective-permute-start.14 = (bf16[32,4096]{1,0:T(8,128)(2,1)S(1)}, bf16[32,4096]{1,0:T(8,128)(2,1)S(1)}, u32[]{:S(2)}, u32[]{:S(2)}) collective-permute-start(bf16[32,4096]{1,0:T(8,128)(2,1)S(1)} %get-tuple-element.56), channel_id=1, source_target_pairs={{0,16},{4,20},{8,24},{12,28},{16,0},{20,4},{24,8},{28,12},{1,17},{... | collective-permute-start | bytes 786440 | tf_op jit(solution)/shard_map/ppermute | solution.py:67
  58.5 5.9 %collective-permute-start.13 = (bf16[16,4096]{1,0:T(8,128)(2,1)S(1)}, bf16[16,4096]{1,0:T(8,128)(2,1)S(1)}, u32[]{:S(2)}, u32[]{:S(2)}) collective-permute-start(bf16[16,4096]{1,0:T(8,128)(2,1)S(1)} %select_convert_fusion.1), channel_id=1, source_target_pairs={{0,1},{1,0},{2,3},{3,2},{4,5},{5,4},{6,7},{7,6},{8,9},{9,8},{10,11... | collective-permute-start | bytes 393224 | tf_op jit(solution)/shard_map/ppermute | solution.py:71
  60.2 14.5 %collective-permute-start.17 = (bf16[16,4096]{1,0:T(8,128)(2,1)S(1)}, bf16[16,4096]{1,0:T(8,128)(2,1)S(1)}, u32[]{:S(2)}, u32[]{:S(2)}) collective-permute-start(bf16[16,4096]{1,0:T(8,128)(2,1)S(1)} %fusion.4), channel_id=1, source_target_pairs={{0,3},{3,0},{1,2},{2,1},{4,7},{7,4},{5,6},{6,5},{8,11},{11,8},{9,1... | collective-permute-start | bytes 393224 | tf_op jit(solution)/shard_map/ppermute | solution.py:71
  62.8 6.2 %collective-permute-start.18 = (bf16[16,4096]{1,0:T(8,128)(2,1)S(1)}, bf16[16,4096]{1,0:T(8,128)(2,1)S(1)}, u32[]{:S(2)}, u32[]{:S(2)}) collective-permute-start(bf16[16,4096]{1,0:T(8,128)(2,1)S(1)} %select_convert_fusion), channel_id=1, source_target_pairs={{0,1},{1,0},{2,3},{3,2},{4,5},{5,4},{6,7},{7,6},{8,9},{9,8},{10,11... | collective-permute-start | bytes 393224 | tf_op jit(solution)/shard_map/ppermute | solution.py:71
  64.4 10.4 %collective-permute-start.16 = (bf16[16,4096]{1,0:T(8,128)(2,1)S(1)}, bf16[16,4096]{1,0:T(8,128)(2,1)S(1)}, u32[]{:S(2)}, u32[]{:S(2)}) collective-permute-start(bf16[16,4096]{1,0:T(8,128)(2,1)S(1)} %fusion.5), channel_id=1, source_target_pairs={{0,3},{3,0},{1,2},{2,1},{4,7},{7,4},{5,6},{6,5},{8,11},{11,8},{9,1... | collective-permute-start | bytes 393224 | tf_op jit(solution)/shard_map/ppermute | solution.py:71
  69.0 9.5 %collective-permute-start.21 = (bf16[16,4096]{1,0:T(8,128)(2,1)S(1)}, bf16[16,4096]{1,0:T(8,128)(2,1)S(1)}, u32[]{:S(2)}, u32[]{:S(2)}) collective-permute-start(bf16[16,4096]{1,0:T(8,128)(2,1)S(1)} %fusion.6), channel_id=1, source_target_pairs={{0,3},{3,0},{1,2},{2,1},{4,7},{7,4},{5,6},{6,5},{8,11},{11,8},{9,1... | collective-permute-start | bytes 393224 | tf_op jit(solution)/shard_map/ppermute | solution.py:71
  74.7 6.2 %collective-permute-start.20 = (bf16[16,4096]{1,0:T(8,128)(2,1)S(1)}, bf16[16,4096]{1,0:T(8,128)(2,1)S(1)}, u32[]{:S(2)}, u32[]{:S(2)}) collective-permute-start(bf16[16,4096]{1,0:T(8,128)(2,1)S(1)} %add_convert_fusion.5), channel_id=1, source_target_pairs={{0,1},{1,0},{2,3},{3,2},{4,5},{5,4},{6,7},{7,6},{8,9},{9,8},{10,11... | collective-permute-start | bytes 393224 | tf_op jit(solution)/shard_map/ppermute | solution.py:71
  74.8 7.7 %collective-permute-start.19 = (bf16[16,4096]{1,0:T(8,128)(2,1)S(1)}, bf16[16,4096]{1,0:T(8,128)(2,1)S(1)}, u32[]{:S(2)}, u32[]{:S(2)}) collective-permute-start(bf16[16,4096]{1,0:T(8,128)(2,1)S(1)} %add_convert_fusion.4), channel_id=1, source_target_pairs={{0,1},{1,0},{2,3},{3,2},{4,5},{5,4},{6,7},{7,6},{8,9},{9,8},{10,11... | collective-permute-start | bytes 393224 | tf_op jit(solution)/shard_map/ppermute | solution.py:71
  78.5 5.5 %collective-permute-start.22 = (bf16[16,4096]{1,0:T(8,128)(2,1)S(1)}, bf16[16,4096]{1,0:T(8,128)(2,1)S(1)}, u32[]{:S(2)}, u32[]{:S(2)}) collective-permute-start(bf16[16,4096]{1,0:T(8,128)(2,1)S(1)} %add_convert_fusion.3), channel_id=1, source_target_pairs={{0,1},{1,0},{2,3},{3,2},{4,5},{5,4},{6,7},{7,6},{8,9},{9,8},{10,11... | collective-permute-start | bytes 393224 | tf_op jit(solution)/shard_map/ppermute | solution.py:71
